TPU v7x, 256 devices: a whole 4x4x8 slice. The times are simulated.
256 devices in a mesh: ctx: 32 (over y_hi, z, core), head: 8 (over y_lo, x).
Axes of the slice: x: 4, y: 4 (y_hi: 2, y_lo: 2; y = y_hi * 2 + y_lo), z: 8, core: 2. Of those that a mesh axis runs over, the one named last changes fastest.
Arguments:
- queries: bfloat16 [16384, 4096], P(('ctx', 'head')), may hold values from -5.5 to 5.5
- keys: bfloat16 [16384, 1024], P(('ctx', 'head')), may hold values from -5.5 to 5.5
- values: bfloat16 [16384, 1024], P(('ctx', 'head')), may hold values from -6 to 6
- block_order: int32 [64], replicated, may hold values from 0 to 63, each once
Outputs:
- attended: bfloat16 [16384, 4096], P(('ctx', 'head'))
Inputs may be any that keep to these rules, and one draw needn't show every extreme that they name: `block_order`: each number appears once.
All inputs are finite; a program needn't handle non-finite values.
Results may differ from a plain program's by a relative error of at most 0.007.
Values may be sent and summed in bfloat16 or wider, within the bound.
No kernel may reach another device: no remote copies, remote signals or barrier semaphores. Data moves between devices by JAX's collectives and lax.ppermute only.
A program may use at most 64 MiB of HBM per device.

v0:
```python
import jax
import jax.numpy as jnp
from jax import lax
from jax.sharding import PartitionSpec as P

HEAD_DIM = 128


NEG_FILL = -1e30


def from_behind(array, axis, by):
    size = lax.axis_size(axis)
    return lax.ppermute(array, axis, [(i, (i + by) % size) for i in range(size)])


def positions_of(block_order, first_row, count, half_rows):
    row_ids = first_row + jnp.arange(count, dtype=jnp.int32)
    owners = row_ids // half_rows
    onehot = owners[:, None] == jnp.arange(block_order.shape[0], dtype=jnp.int32)[None, :]
    starts = jnp.sum(jnp.where(onehot, block_order[None, :], 0), axis=1)
    return starts * half_rows + row_ids % half_rows


def attend(carried, query_part, query_pos, key_part, value_part, key_pos):
    run_max, run_sum, run_out = carried
    score_scale = query_part.shape[-1] ** (-0.5)
    scores = (
        jnp.einsum("qhgd,khd->hgqk", query_part, key_part, preferred_element_type=jnp.float32)
        * score_scale
    )
    visible = (key_pos[None, :] <= query_pos[:, None])[None, None]
    row_max = jnp.max(jnp.where(visible, scores, NEG_FILL), axis=-1)
    new_max = jnp.maximum(run_max, row_max)
    weights = jnp.where(visible, jnp.exp(scores - new_max[..., None]), 0.0)
    keep_factor = jnp.exp(run_max - new_max)
    run_sum = run_sum * keep_factor + jnp.sum(weights, axis=-1)
    run_out = run_out * keep_factor[..., None] + jnp.einsum(
        "hgqk,khd->hgqd",
        weights.astype(jnp.bfloat16),
        value_part,
        preferred_element_type=jnp.float32,
    )
    return (new_max, run_sum, run_out)


def unchanged(carried, query_part, query_pos, key_part, value_part, key_pos):
    return carried


def body(queries, keys, values, block_order):
    query_rows, key_rows, value_rows = (
        lax.all_to_all(queries, "head", split_axis=1, concat_axis=0, tiled=True),
        lax.all_to_all(keys, "head", split_axis=1, concat_axis=0, tiled=True),
        lax.all_to_all(values, "head", split_axis=1, concat_axis=0, tiled=True),
    )
    local_rows = query_rows.shape[0]
    half_rows = local_rows // 2
    key_heads = key_rows.shape[1] // HEAD_DIM
    groups = query_rows.shape[1] // key_rows.shape[1]
    ctx_count = lax.axis_size("ctx")
    ctx_index = lax.axis_index("ctx")
    query_grid = query_rows.reshape(local_rows, key_heads, groups, HEAD_DIM)
    query_pos = positions_of(block_order, ctx_index * local_rows, local_rows, half_rows)
    key_value = jnp.stack([key_rows, value_rows])

    def absorb(carried, key_block, key_pos):
        piece_rows = key_block.shape[1]
        run_max, run_sum, run_out = carried
        for query_half in range(2):
            query_start = query_half * half_rows
            query_part = query_grid[query_start : query_start + half_rows]
            part_pos = query_pos[query_start : query_start + half_rows]
            piece_state = (run_max[query_half], run_sum[query_half], run_out[query_half])
            for key_index in range(piece_rows // half_rows):
                key_start = key_index * half_rows
                key_part = key_block[0, key_start : key_start + half_rows].reshape(
                    half_rows, key_heads, HEAD_DIM
                )
                value_part = key_block[1, key_start : key_start + half_rows].reshape(
                    half_rows, key_heads, HEAD_DIM
                )
                part_keys = key_pos[key_start : key_start + half_rows]
                piece_state = lax.cond(
                    jnp.min(part_keys) <= jnp.max(part_pos),
                    attend,
                    unchanged,
                    piece_state,
                    query_part,
                    part_pos,
                    key_part,
                    value_part,
                    part_keys,
                )
            run_max = run_max.at[query_half].set(piece_state[0])
            run_sum = run_sum.at[query_half].set(piece_state[1])
            run_out = run_out.at[query_half].set(piece_state[2])
        return (run_max, run_sum, run_out)

    def source_positions(source):
        return positions_of(
            block_order, jnp.mod(source, ctx_count) * local_rows, local_rows, half_rows
        )

    initial = (
        jnp.full((2, key_heads, groups, half_rows), NEG_FILL, jnp.float32),
        jnp.zeros((2, key_heads, groups, half_rows), jnp.float32),
        jnp.zeros((2, key_heads, groups, half_rows, HEAD_DIM), jnp.float32),
    )

    def one_turn(turn_index, carried):
        moving, progress = carried
        moving = from_behind(moving, "ctx", 1)
        return (moving, absorb(progress, moving, source_positions(ctx_index - turn_index)))

    progress = absorb(initial, key_value, query_pos)
    moving, progress = lax.fori_loop(1, ctx_count, one_turn, (key_value, progress))
    run_max, run_sum, run_out = progress
    result = run_out / run_sum[..., None]
    result = (
        result.transpose(0, 3, 1, 2, 4)
        .reshape(local_rows, key_heads * groups * HEAD_DIM)
        .astype(jnp.bfloat16)
    )
    return lax.all_to_all(result, "head", split_axis=0, concat_axis=1, tiled=True)


def solution(mesh):
    return jax.shard_map(
        body,
        mesh=mesh,
        in_specs=(
            P(("ctx", "head"), None),
            P(("ctx", "head"), None),
            P(("ctx", "head"), None),
            P(),
        ),
        out_specs=P(("ctx", "head"), None),
        check_vma=False,
    )
```

profile of v0, /device:TPU:16, one launch (start us, length us, event | category | flops | bytes accessed | tf_op | source)
XLA Modules:
  0.0 484.1 jit_solution(8712800428721761459)
XLA Ops:
  1.6 5.0 %all-to-all-start = ((bf16[64,8,128]{2,0,1:T(8,128)(2,1)}), bf16[64,8,128]{2,0,1:T(8,128)(2,1)S(1)}, u32[]{:S(2)}, u32[]{:S(2)}) async-start(bf16[64,8,128]{2,0,1:T(8,128)(2,1)} %copy_bitcast_fusion.2), calls=%async_computation | async-start | bytes 262144 | tf_op jit(solution)/shard_map/all_to_all | solution.py:54
  6.6 1.6 copy_bitcast_fusion.1
  8.3 4.9 %all-to-all-done = bf16[64,8,128]{2,0,1:T(8,128)(2,1)S(1)} async-done(((bf16[64,8,128]{2,0,1:T(8,128)(2,1)}), bf16[64,8,128]{2,0,1:T(8,128)(2,1)S(1)}, u32[]{:S(2)}, u32[]{:S(2)}) %all-to-all-start) | async-done | bytes 131104 | tf_op jit(solution)/shard_map/all_to_all | solution.py:54
  13.2 3.4 all-to-all-start.1
  23.1 5.5 %all-to-all-start.2 = ((bf16[64,8,512]{2,0,1:T(8,128)(2,1)}), bf16[64,8,512]{2,0,1:T(8,128)(2,1)S(1)}, u32[]{:S(2)}, u32[]{:S(2)}) async-start(bf16[64,8,512]{2,0,1:T(8,128)(2,1)} %bitcast.407), calls=%async_computation.2 | async-start | bytes 1048576 | tf_op jit(solution)/shard_map/all_to_all | solution.py:53
  29.3 7.9 %all-to-all-done.2 = bf16[64,8,512]{2,0,1:T(8,128)(2,1)S(1)} async-done(((bf16[64,8,512]{2,0,1:T(8,128)(2,1)}), bf16[64,8,512]{2,0,1:T(8,128)(2,1)S(1)}, u32[]{:S(2)}, u32[]{:S(2)}) %all-to-all-start.2) | async-done | bytes 524320 | tf_op jit(solution)/shard_map/all_to_all | solution.py:53
  41.5 429.4 %while.34 = (s32[]{:T(128)}, bf16[2,512,128]{2,1,0:T(8,128)(2,1)}, f32[2,1,4,256]{3,2,1,0:T(4,128)S(1)}, f32[2,1,4,256]{3,2,1,0:T(4,128)S(1)}, f32[2,1,4,256,128...) while((s32[]{:T(128)}, bf16[2,512,128]{2,1,0:T(8,128)(2,1)}, ...), condition=%wide.region_41.42_spmd, body=%wide.region_21.41_spmd.sunk | while | flops 547744768 | bytes 27085864 | solution.py:117
  47.6 3.6 collective-permute-done
  51.3 1.2 conditional.16
  63.0 3.6 collective-permute-done
  77.2 3.6 collective-permute-done
  90.3 3.6 collective-permute-done
  102.1 3.6 collective-permute-done
  116.3 3.6 collective-permute-done
  120.0 1.2 conditional.16
  122.5 1.2 conditional.18
  131.7 3.6 collective-permute-done
  145.9 3.6 collective-permute-done
  149.6 1.2 conditional.16
  152.2 1.2 conditional.18
  161.4 3.6 collective-permute-done
  173.2 3.6 collective-permute-done
  188.6 3.6 collective-permute-done
  201.6 3.6 collective-permute-done
  217.0 3.6 collective-permute-done
  231.3 3.6 collective-permute-done
  234.9 1.2 conditional.16
  244.3 3.6 collective-permute-done
  258.5 3.6 collective-permute-done
  262.2 1.2 conditional.16
  273.9 3.6 collective-permute-done
  285.8 3.6 collective-permute-done
  300.0 3.6 collective-permute-done
  313.0 3.6 collective-permute-done
  326.0 3.6 collective-permute-done
  339.0 3.6 collective-permute-done
  352.0 3.6 collective-permute-done
  366.3 3.6 collective-permute-done
  380.5 3.6 collective-permute-done
  394.7 3.6 collective-permute-done
  407.7 3.6 collective-permute-done
  420.7 4.1 collective-permute-done
  424.9 1.2 conditional.16
  427.5 1.2 conditional.18
  436.7 3.6 collective-permute-done
  450.9 3.6 collective-permute-done
  463.9 3.6 collective-permute-done
  471.9 11.3 %all_to_all.64 = bf16[8,64,512]{2,1,0:T(8,128)(2,1)S(1)} all-to-all(bf16[8,64,512]{2,1,0:T(8,128)(2,1)S(1)} %convert_element_type.96), channel_id=1, replica_groups=mesh['ctx'=32,'head'=8] {'head'}, dimensions={0} | all-to-all | bytes 1048576 | tf_op jit(solution)/shard_map/all_to_all | solution.py:125
  (1294 shorter events, 255.9 us)
Async XLA Ops:
  0.0 0.9 copy-start
  0.9 21.1 %copy-start.1 = (bf16[64,4096]{1,0:T(8,128)(2,1)S(1)}, bf16[64,4096]{1,0:T(8,128)(2,1)}, u32[]{:S(2)}) copy-start(bf16[64,4096]{1,0:T(8,128)(2,1)} %param.46) | copy-start | bytes 1572868
  1.6 11.6 %all-to-all-start = ((bf16[64,8,128]{2,0,1:T(8,128)(2,1)}), bf16[64,8,128]{2,0,1:T(8,128)(2,1)S(1)}, u32[]{:S(2)}, u32[]{:S(2)}) async-start(bf16[64,8,128]{2,0,1:T(8,128)(2,1)} %copy_bitcast_fusion.2), calls=%async_computation | async-start | bytes 262144 | tf_op jit(solution)/shard_map/all_to_all | solution.py:54
  6.6 1.6 copy-start.2
  13.2 9.9 %all-to-all-start.1 = ((bf16[64,8,128]{2,0,1:T(8,128)(2,1)}), bf16[64,8,128]{2,0,1:T(8,128)(2,1)S(1)}, u32[]{:S(2)}, u32[]{:S(2)}) async-start(bf16[64,8,128]{2,0,1:T(8,128)(2,1)} %copy_bitcast_fusion.1), calls=%async_computation.1 | async-start | bytes 262144 | tf_op jit(solution)/shard_map/all_to_all | solution.py:55
  23.1 14.2 %all-to-all-start.2 = ((bf16[64,8,512]{2,0,1:T(8,128)(2,1)}), bf16[64,8,512]{2,0,1:T(8,128)(2,1)S(1)}, u32[]{:S(2)}, u32[]{:S(2)}) async-start(bf16[64,8,512]{2,0,1:T(8,128)(2,1)} %bitcast.407), calls=%async_computation.2 | async-start | bytes 1048576 | tf_op jit(solution)/shard_map/all_to_all | solution.py:53
  41.5 9.7 %collective-permute-start = (bf16[2,512,128]{2,1,0:T(8,128)(2,1)}, bf16[2,512,128]{2,1,0:T(8,128)(2,1)S(1)}, u32[]{:S(2)}, u32[]{:S(2)}) collective-permute-start(bf16[2,512,128]{2,1,0:T(8,128)(2,1)} %get-tuple-element.1260), channel_id=1, source_target_pairs={{0,8},{8,16},{16,24},{24,32},{32,40},{40,48},{48,56},{56,64},{64,7... | collective-permute-start | bytes 786440 | tf_op jit(solution)/shard_map/while/body/eval_jaxpr/ppermute | solution.py:14
  57.1 9.6 %collective-permute-start = (bf16[2,512,128]{2,1,0:T(8,128)(2,1)}, bf16[2,512,128]{2,1,0:T(8,128)(2,1)S(1)}, u32[]{:S(2)}, u32[]{:S(2)}) collective-permute-start(bf16[2,512,128]{2,1,0:T(8,128)(2,1)} %get-tuple-element.1260), channel_id=1, source_target_pairs={{0,8},{8,16},{16,24},{24,32},{32,40},{40,48},{48,56},{56,64},{64,7... | collective-permute-start | bytes 786440 | tf_op jit(solution)/shard_map/while/body/eval_jaxpr/ppermute | solution.py:14
  71.3 9.6 %collective-permute-start = (bf16[2,512,128]{2,1,0:T(8,128)(2,1)}, bf16[2,512,128]{2,1,0:T(8,128)(2,1)S(1)}, u32[]{:S(2)}, u32[]{:S(2)}) collective-permute-start(bf16[2,512,128]{2,1,0:T(8,128)(2,1)} %get-tuple-element.1260), channel_id=1, source_target_pairs={{0,8},{8,16},{16,24},{24,32},{32,40},{40,48},{48,56},{56,64},{64,7... | collective-permute-start | bytes 786440 | tf_op jit(solution)/shard_map/while/body/eval_jaxpr/ppermute | solution.py:14
  84.3 9.6 %collective-permute-start = (bf16[2,512,128]{2,1,0:T(8,128)(2,1)}, bf16[2,512,128]{2,1,0:T(8,128)(2,1)S(1)}, u32[]{:S(2)}, u32[]{:S(2)}) collective-permute-start(bf16[2,512,128]{2,1,0:T(8,128)(2,1)} %get-tuple-element.1260), channel_id=1, source_target_pairs={{0,8},{8,16},{16,24},{24,32},{32,40},{40,48},{48,56},{56,64},{64,7... | collective-permute-start | bytes 786440 | tf_op jit(solution)/shard_map/while/body/eval_jaxpr/ppermute | solution.py:14
  96.1 9.6 %collective-permute-start = (bf16[2,512,128]{2,1,0:T(8,128)(2,1)}, bf16[2,512,128]{2,1,0:T(8,128)(2,1)S(1)}, u32[]{:S(2)}, u32[]{:S(2)}) collective-permute-start(bf16[2,512,128]{2,1,0:T(8,128)(2,1)} %get-tuple-element.1260), channel_id=1, source_target_pairs={{0,8},{8,16},{16,24},{24,32},{32,40},{40,48},{48,56},{56,64},{64,7... | collective-permute-start | bytes 786440 | tf_op jit(solution)/shard_map/while/body/eval_jaxpr/ppermute | solution.py:14
  110.3 9.6 %collective-permute-start = (bf16[2,512,128]{2,1,0:T(8,128)(2,1)}, bf16[2,512,128]{2,1,0:T(8,128)(2,1)S(1)}, u32[]{:S(2)}, u32[]{:S(2)}) collective-permute-start(bf16[2,512,128]{2,1,0:T(8,128)(2,1)} %get-tuple-element.1260), channel_id=1, source_target_pairs={{0,8},{8,16},{16,24},{24,32},{32,40},{40,48},{48,56},{56,64},{64,7... | collective-permute-start | bytes 786440 | tf_op jit(solution)/shard_map/while/body/eval_jaxpr/ppermute | solution.py:14
  125.7 9.6 %collective-permute-start = (bf16[2,512,128]{2,1,0:T(8,128)(2,1)}, bf16[2,512,128]{2,1,0:T(8,128)(2,1)S(1)}, u32[]{:S(2)}, u32[]{:S(2)}) collective-permute-start(bf16[2,512,128]{2,1,0:T(8,128)(2,1)} %get-tuple-element.1260), channel_id=1, source_target_pairs={{0,8},{8,16},{16,24},{24,32},{32,40},{40,48},{48,56},{56,64},{64,7... | collective-permute-start | bytes 786440 | tf_op jit(solution)/shard_map/while/body/eval_jaxpr/ppermute | solution.py:14
  140.0 9.6 %collective-permute-start = (bf16[2,512,128]{2,1,0:T(8,128)(2,1)}, bf16[2,512,128]{2,1,0:T(8,128)(2,1)S(1)}, u32[]{:S(2)}, u32[]{:S(2)}) collective-permute-start(bf16[2,512,128]{2,1,0:T(8,128)(2,1)} %get-tuple-element.1260), channel_id=1, source_target_pairs={{0,8},{8,16},{16,24},{24,32},{32,40},{40,48},{48,56},{56,64},{64,7... | collective-permute-start | bytes 786440 | tf_op jit(solution)/shard_map/while/body/eval_jaxpr/ppermute | solution.py:14
  155.4 9.6 %collective-permute-start = (bf16[2,512,128]{2,1,0:T(8,128)(2,1)}, bf16[2,512,128]{2,1,0:T(8,128)(2,1)S(1)}, u32[]{:S(2)}, u32[]{:S(2)}) collective-permute-start(bf16[2,512,128]{2,1,0:T(8,128)(2,1)} %get-tuple-element.1260), channel_id=1, source_target_pairs={{0,8},{8,16},{16,24},{24,32},{32,40},{40,48},{48,56},{56,64},{64,7... | collective-permute-start | bytes 786440 | tf_op jit(solution)/shard_map/while/body/eval_jaxpr/ppermute | solution.py:14
  167.2 9.6 %collective-permute-start = (bf16[2,512,128]{2,1,0:T(8,128)(2,1)}, bf16[2,512,128]{2,1,0:T(8,128)(2,1)S(1)}, u32[]{:S(2)}, u32[]{:S(2)}) collective-permute-start(bf16[2,512,128]{2,1,0:T(8,128)(2,1)} %get-tuple-element.1260), channel_id=1, source_target_pairs={{0,8},{8,16},{16,24},{24,32},{32,40},{40,48},{48,56},{56,64},{64,7... | collective-permute-start | bytes 786440 | tf_op jit(solution)/shard_map/while/body/eval_jaxpr/ppermute | solution.py:14
  182.6 9.6 %collective-permute-start = (bf16[2,512,128]{2,1,0:T(8,128)(2,1)}, bf16[2,512,128]{2,1,0:T(8,128)(2,1)S(1)}, u32[]{:S(2)}, u32[]{:S(2)}) collective-permute-start(bf16[2,512,128]{2,1,0:T(8,128)(2,1)} %get-tuple-element.1260), channel_id=1, source_target_pairs={{0,8},{8,16},{16,24},{24,32},{32,40},{40,48},{48,56},{56,64},{64,7... | collective-permute-start | bytes 786440 | tf_op jit(solution)/shard_map/while/body/eval_jaxpr/ppermute | solution.py:14
  195.6 9.6 %collective-permute-start = (bf16[2,512,128]{2,1,0:T(8,128)(2,1)}, bf16[2,512,128]{2,1,0:T(8,128)(2,1)S(1)}, u32[]{:S(2)}, u32[]{:S(2)}) collective-permute-start(bf16[2,512,128]{2,1,0:T(8,128)(2,1)} %get-tuple-element.1260), channel_id=1, source_target_pairs={{0,8},{8,16},{16,24},{24,32},{32,40},{40,48},{48,56},{56,64},{64,7... | collective-permute-start | bytes 786440 | tf_op jit(solution)/shard_map/while/body/eval_jaxpr/ppermute | solution.py:14
  211.1 9.6 %collective-permute-start = (bf16[2,512,128]{2,1,0:T(8,128)(2,1)}, bf16[2,512,128]{2,1,0:T(8,128)(2,1)S(1)}, u32[]{:S(2)}, u32[]{:S(2)}) collective-permute-start(bf16[2,512,128]{2,1,0:T(8,128)(2,1)} %get-tuple-element.1260), channel_id=1, source_target_pairs={{0,8},{8,16},{16,24},{24,32},{32,40},{40,48},{48,56},{56,64},{64,7... | collective-permute-start | bytes 786440 | tf_op jit(solution)/shard_map/while/body/eval_jaxpr/ppermute | solution.py:14
  225.3 9.6 %collective-permute-start = (bf16[2,512,128]{2,1,0:T(8,128)(2,1)}, bf16[2,512,128]{2,1,0:T(8,128)(2,1)S(1)}, u32[]{:S(2)}, u32[]{:S(2)}) collective-permute-start(bf16[2,512,128]{2,1,0:T(8,128)(2,1)} %get-tuple-element.1260), channel_id=1, source_target_pairs={{0,8},{8,16},{16,24},{24,32},{32,40},{40,48},{48,56},{56,64},{64,7... | collective-permute-start | bytes 786440 | tf_op jit(solution)/shard_map/while/body/eval_jaxpr/ppermute | solution.py:14
  238.3 9.6 %collective-permute-start = (bf16[2,512,128]{2,1,0:T(8,128)(2,1)}, bf16[2,512,128]{2,1,0:T(8,128)(2,1)S(1)}, u32[]{:S(2)}, u32[]{:S(2)}) collective-permute-start(bf16[2,512,128]{2,1,0:T(8,128)(2,1)} %get-tuple-element.1260), channel_id=1, source_target_pairs={{0,8},{8,16},{16,24},{24,32},{32,40},{40,48},{48,56},{56,64},{64,7... | collective-permute-start | bytes 786440 | tf_op jit(solution)/shard_map/while/body/eval_jaxpr/ppermute | solution.py:14
  252.5 9.6 %collective-permute-start = (bf16[2,512,128]{2,1,0:T(8,128)(2,1)}, bf16[2,512,128]{2,1,0:T(8,128)(2,1)S(1)}, u32[]{:S(2)}, u32[]{:S(2)}) collective-permute-start(bf16[2,512,128]{2,1,0:T(8,128)(2,1)} %get-tuple-element.1260), channel_id=1, source_target_pairs={{0,8},{8,16},{16,24},{24,32},{32,40},{40,48},{48,56},{56,64},{64,7... | collective-permute-start | bytes 786440 | tf_op jit(solution)/shard_map/while/body/eval_jaxpr/ppermute | solution.py:14
  267.9 9.6 %collective-permute-start = (bf16[2,512,128]{2,1,0:T(8,128)(2,1)}, bf16[2,512,128]{2,1,0:T(8,128)(2,1)S(1)}, u32[]{:S(2)}, u32[]{:S(2)}) collective-permute-start(bf16[2,512,128]{2,1,0:T(8,128)(2,1)} %get-tuple-element.1260), channel_id=1, source_target_pairs={{0,8},{8,16},{16,24},{24,32},{32,40},{40,48},{48,56},{56,64},{64,7... | collective-permute-start | bytes 786440 | tf_op jit(solution)/shard_map/while/body/eval_jaxpr/ppermute | solution.py:14
  279.8 9.6 %collective-permute-start = (bf16[2,512,128]{2,1,0:T(8,128)(2,1)}, bf16[2,512,128]{2,1,0:T(8,128)(2,1)S(1)}, u32[]{:S(2)}, u32[]{:S(2)}) collective-permute-start(bf16[2,512,128]{2,1,0:T(8,128)(2,1)} %get-tuple-element.1260), channel_id=1, source_target_pairs={{0,8},{8,16},{16,24},{24,32},{32,40},{40,48},{48,56},{56,64},{64,7... | collective-permute-start | bytes 786440 | tf_op jit(solution)/shard_map/while/body/eval_jaxpr/ppermute | solution.py:14
  294.0 9.6 %collective-permute-start = (bf16[2,512,128]{2,1,0:T(8,128)(2,1)}, bf16[2,512,128]{2,1,0:T(8,128)(2,1)S(1)}, u32[]{:S(2)}, u32[]{:S(2)}) collective-permute-start(bf16[2,512,128]{2,1,0:T(8,128)(2,1)} %get-tuple-element.1260), channel_id=1, source_target_pairs={{0,8},{8,16},{16,24},{24,32},{32,40},{40,48},{48,56},{56,64},{64,7... | collective-permute-start | bytes 786440 | tf_op jit(solution)/shard_map/while/body/eval_jaxpr/ppermute | solution.py:14
  307.0 9.6 %collective-permute-start = (bf16[2,512,128]{2,1,0:T(8,128)(2,1)}, bf16[2,512,128]{2,1,0:T(8,128)(2,1)S(1)}, u32[]{:S(2)}, u32[]{:S(2)}) collective-permute-start(bf16[2,512,128]{2,1,0:T(8,128)(2,1)} %get-tuple-element.1260), channel_id=1, source_target_pairs={{0,8},{8,16},{16,24},{24,32},{32,40},{40,48},{48,56},{56,64},{64,7... | collective-permute-start | bytes 786440 | tf_op jit(solution)/shard_map/while/body/eval_jaxpr/ppermute | solution.py:14
  320.0 9.6 %collective-permute-start = (bf16[2,512,128]{2,1,0:T(8,128)(2,1)}, bf16[2,512,128]{2,1,0:T(8,128)(2,1)S(1)}, u32[]{:S(2)}, u32[]{:S(2)}) collective-permute-start(bf16[2,512,128]{2,1,0:T(8,128)(2,1)} %get-tuple-element.1260), channel_id=1, source_target_pairs={{0,8},{8,16},{16,24},{24,32},{32,40},{40,48},{48,56},{56,64},{64,7... | collective-permute-start | bytes 786440 | tf_op jit(solution)/shard_map/while/body/eval_jaxpr/ppermute | solution.py:14
  333.0 9.6 %collective-permute-start = (bf16[2,512,128]{2,1,0:T(8,128)(2,1)}, bf16[2,512,128]{2,1,0:T(8,128)(2,1)S(1)}, u32[]{:S(2)}, u32[]{:S(2)}) collective-permute-start(bf16[2,512,128]{2,1,0:T(8,128)(2,1)} %get-tuple-element.1260), channel_id=1, source_target_pairs={{0,8},{8,16},{16,24},{24,32},{32,40},{40,48},{48,56},{56,64},{64,7... | collective-permute-start | bytes 786440 | tf_op jit(solution)/shard_map/while/body/eval_jaxpr/ppermute | solution.py:14
  346.1 9.6 %collective-permute-start = (bf16[2,512,128]{2,1,0:T(8,128)(2,1)}, bf16[2,512,128]{2,1,0:T(8,128)(2,1)S(1)}, u32[]{:S(2)}, u32[]{:S(2)}) collective-permute-start(bf16[2,512,128]{2,1,0:T(8,128)(2,1)} %get-tuple-element.1260), channel_id=1, source_target_pairs={{0,8},{8,16},{16,24},{24,32},{32,40},{40,48},{48,56},{56,64},{64,7... | collective-permute-start | bytes 786440 | tf_op jit(solution)/shard_map/while/body/eval_jaxpr/ppermute | solution.py:14
  360.3 9.6 %collective-permute-start = (bf16[2,512,128]{2,1,0:T(8,128)(2,1)}, bf16[2,512,128]{2,1,0:T(8,128)(2,1)S(1)}, u32[]{:S(2)}, u32[]{:S(2)}) collective-permute-start(bf16[2,512,128]{2,1,0:T(8,128)(2,1)} %get-tuple-element.1260), channel_id=1, source_target_pairs={{0,8},{8,16},{16,24},{24,32},{32,40},{40,48},{48,56},{56,64},{64,7... | collective-permute-start | bytes 786440 | tf_op jit(solution)/shard_map/while/body/eval_jaxpr/ppermute | solution.py:14
  374.5 9.6 %collective-permute-start = (bf16[2,512,128]{2,1,0:T(8,128)(2,1)}, bf16[2,512,128]{2,1,0:T(8,128)(2,1)S(1)}, u32[]{:S(2)}, u32[]{:S(2)}) collective-permute-start(bf16[2,512,128]{2,1,0:T(8,128)(2,1)} %get-tuple-element.1260), channel_id=1, source_target_pairs={{0,8},{8,16},{16,24},{24,32},{32,40},{40,48},{48,56},{56,64},{64,7... | collective-permute-start | bytes 786440 | tf_op jit(solution)/shard_map/while/body/eval_jaxpr/ppermute | solution.py:14
  388.7 9.6 %collective-permute-start = (bf16[2,512,128]{2,1,0:T(8,128)(2,1)}, bf16[2,512,128]{2,1,0:T(8,128)(2,1)S(1)}, u32[]{:S(2)}, u32[]{:S(2)}) collective-permute-start(bf16[2,512,128]{2,1,0:T(8,128)(2,1)} %get-tuple-element.1260), channel_id=1, source_target_pairs={{0,8},{8,16},{16,24},{24,32},{32,40},{40,48},{48,56},{56,64},{64,7... | collective-permute-start | bytes 786440 | tf_op jit(solution)/shard_map/while/body/eval_jaxpr/ppermute | solution.py:14
  401.7 9.6 %collective-permute-start = (bf16[2,512,128]{2,1,0:T(8,128)(2,1)}, bf16[2,512,128]{2,1,0:T(8,128)(2,1)S(1)}, u32[]{:S(2)}, u32[]{:S(2)}) collective-permute-start(bf16[2,512,128]{2,1,0:T(8,128)(2,1)} %get-tuple-element.1260), channel_id=1, source_target_pairs={{0,8},{8,16},{16,24},{24,32},{32,40},{40,48},{48,56},{56,64},{64,7... | collective-permute-start | bytes 786440 | tf_op jit(solution)/shard_map/while/body/eval_jaxpr/ppermute | solution.py:14
  414.7 10.1 %collective-permute-start = (bf16[2,512,128]{2,1,0:T(8,128)(2,1)}, bf16[2,512,128]{2,1,0:T(8,128)(2,1)S(1)}, u32[]{:S(2)}, u32[]{:S(2)}) collective-permute-start(bf16[2,512,128]{2,1,0:T(8,128)(2,1)} %get-tuple-element.1260), channel_id=1, source_target_pairs={{0,8},{8,16},{16,24},{24,32},{32,40},{40,48},{48,56},{56,64},{64,7... | collective-permute-start | bytes 786440 | tf_op jit(solution)/shard_map/while/body/eval_jaxpr/ppermute | solution.py:14
  430.7 9.6 %collective-permute-start = (bf16[2,512,128]{2,1,0:T(8,128)(2,1)}, bf16[2,512,128]{2,1,0:T(8,128)(2,1)S(1)}, u32[]{:S(2)}, u32[]{:S(2)}) collective-permute-start(bf16[2,512,128]{2,1,0:T(8,128)(2,1)} %get-tuple-element.1260), channel_id=1, source_target_pairs={{0,8},{8,16},{16,24},{24,32},{32,40},{40,48},{48,56},{56,64},{64,7... | collective-permute-start | bytes 786440 | tf_op jit(solution)/shard_map/while/body/eval_jaxpr/ppermute | solution.py:14
  444.9 9.6 %collective-permute-start = (bf16[2,512,128]{2,1,0:T(8,128)(2,1)}, bf16[2,512,128]{2,1,0:T(8,128)(2,1)S(1)}, u32[]{:S(2)}, u32[]{:S(2)}) collective-permute-start(bf16[2,512,128]{2,1,0:T(8,128)(2,1)} %get-tuple-element.1260), channel_id=1, source_target_pairs={{0,8},{8,16},{16,24},{24,32},{32,40},{40,48},{48,56},{56,64},{64,7... | collective-permute-start | bytes 786440 | tf_op jit(solution)/shard_map/while/body/eval_jaxpr/ppermute | solution.py:14
  457.9 9.6 %collective-permute-start = (bf16[2,512,128]{2,1,0:T(8,128)(2,1)}, bf16[2,512,128]{2,1,0:T(8,128)(2,1)S(1)}, u32[]{:S(2)}, u32[]{:S(2)}) collective-permute-start(bf16[2,512,128]{2,1,0:T(8,128)(2,1)} %get-tuple-element.1260), channel_id=1, source_target_pairs={{0,8},{8,16},{16,24},{24,32},{32,40},{40,48},{48,56},{56,64},{64,7... | collective-permute-start | bytes 786440 | tf_op jit(solution)/shard_map/while/body/eval_jaxpr/ppermute | solution.py:14
where the time goes:
time: 487 us; the launch traced here: 484 us
  loops' own time  164 us (34%)
  waiting for transfers between devices  126 us (26%)
  matrix products  71.3 us (15%)
  other arithmetic  56.9 us (12%)
  local copies, waits for them, and re-layouts  35 us (7%)
  starting transfers between devices  14 us (3%)
  blocking collectives  11.3 us (2%)
  between operations  4.94 us (1%)
    another operation x1, loops' own time, body(): lax.fori_loop(1, ctx_count, one_turn, (key_value, progress))  160 us
    ppermute x31, waiting for transfers between devices, from_behind(): lax.ppermute(array, axis, [(i, (i + by) % size) for i in range(size)])  113 us
    dot_general x86, matrix products, attend(): jnp.einsum('hgqk,khd->hgqd', weights.astype(jnp.bfloat16), value_part, pr...  43.2 us
    dot_general x86, matrix products, attend(): jnp.einsum('qhgd,khd->hgqk', query_part, key_part, preferred_element_type...  28.2 us
    reduce_min x31, other arithmetic, absorb(): jnp.min(part_keys) <= jnp.max(part_pos)  22.2 us
    while x31, local copies, waits for them, and re-layouts  21.5 us
    reduce_sum x86, other arithmetic, attend(): run_sum = run_sum * keep_factor + jnp.sum(weights, axis=-1)  17.9 us
    all_to_all x1, blocking collectives, body(): lax.all_to_all(result, 'head', split_axis=0, concat_axis=1, tiled=True)  11.3 us
  transfers between devices with their start and end apart: 34, of which 34 were waited for; matrix products, arithmetic and copies ran while one was open for 7% of the time, Pallas kernels for 0%

commit v1 on v0

v1 whole, which is shorter than its diff:
```python
import functools

import jax
import jax.numpy as jnp
import numpy as np
from jax import lax
from jax.experimental import pallas as pl
from jax.experimental.pallas import tpu as pltpu
from jax.sharding import Mesh
from jax.sharding import PartitionSpec as P

HEAD_DIM = 128
BLOCK = 256
ROWS = 2 * BLOCK
BLOCKS = 4
EXTENDED = HEAD_DIM + 16
NEG = -1e30
LOG2E_SCALE = float(np.log2(np.e) / np.sqrt(HEAD_DIM))
AXES = ("yh", "z", "c", "yl", "x")
F32 = jnp.float32
BF16 = jnp.bfloat16
SMEM = pl.BlockSpec(memory_space=pltpu.SMEM)
VMEM = pl.BlockSpec(memory_space=pltpu.VMEM)
ANY = pl.BlockSpec(memory_space=pl.ANY)
VMEM_BYTES = 48 * 2**20


def nt(a, b):
    return lax.dot_general(a, b, (((1,), (0,)), ((), ())), preferred_element_type=F32)


def prepare_kernel(got_ref, q_ref, kv_ref):
    for b in range(BLOCKS):
        for h in range(2):
            q_ref[b, :, h * BLOCK : (h + 1) * BLOCK] = got_ref[
                b, :, h * HEAD_DIM : (h + 1) * HEAD_DIM
            ].T
        kv_ref[b, :BLOCK] = got_ref[b, :, 2 * HEAD_DIM : 3 * HEAD_DIM]
        value = got_ref[b, :, 3 * HEAD_DIM :].T
        kv_ref[b, BLOCK : BLOCK + HEAD_DIM] = value[:, :HEAD_DIM]
        kv_ref[b, BLOCK + HEAD_DIM :] = value[:, HEAD_DIM:]


def prepare(got):
    return pl.pallas_call(
        prepare_kernel,
        out_shape=(
            jax.ShapeDtypeStruct((BLOCKS, HEAD_DIM, ROWS), BF16),
            jax.ShapeDtypeStruct((BLOCKS, 2 * BLOCK, HEAD_DIM), BF16),
        ),
        in_specs=[VMEM],
        out_specs=(VMEM, VMEM),
        name="prepare",
    )(got)


def value_of(kv_ref, t):
    return jnp.concatenate(
        [kv_ref[t, BLOCK : BLOCK + HEAD_DIM], kv_ref[t, BLOCK + HEAD_DIM :]], axis=1
    )


def own_kernel(meta_ref, order_ref, q_ref, kv_ref, m_ref, acc_ref):
    first = (meta_ref[0] * 8 + meta_ref[1]) * BLOCKS
    values = jnp.concatenate([value_of(kv_ref, t) for t in range(BLOCKS)], axis=1)
    lhs = jnp.concatenate([values, jnp.ones((16, BLOCKS * BLOCK), BF16)], axis=0)
    keys = jnp.concatenate([kv_ref[t, :BLOCK] for t in range(BLOCKS)], axis=0)
    row = lax.broadcasted_iota(jnp.int32, (BLOCK, ROWS), 0)
    col = lax.broadcasted_iota(jnp.int32, (BLOCK, ROWS), 1) & (BLOCK - 1)
    ahead = row - col
    for i in range(BLOCKS):
        scores = nt(keys, q_ref[i]) * LOG2E_SCALE
        q_pos = order_ref[first + i] * BLOCK
        parts = []
        for t in range(BLOCKS):
            part = scores[t * BLOCK : (t + 1) * BLOCK]
            room = q_pos - order_ref[first + t] * BLOCK
            parts.append(jnp.where(ahead <= room, part, NEG))
        scores = jnp.concatenate(parts, axis=0)
        row_max = jnp.max(scores, axis=0, keepdims=True)
        m_ref[i] = row_max
        acc_ref[i] = nt(lhs, jnp.exp2(scores - row_max).astype(BF16))


def own_start(meta, order, q, kv):
    return pl.pallas_call(
        own_kernel,
        out_shape=(
            jax.ShapeDtypeStruct((BLOCKS, 1, ROWS), F32),
            jax.ShapeDtypeStruct((BLOCKS, EXTENDED, ROWS), F32),
        ),
        in_specs=[SMEM, SMEM, VMEM, VMEM],
        out_specs=(VMEM, VMEM),
        compiler_params=pltpu.CompilerParams(vmem_limit_bytes=VMEM_BYTES),
        cost_estimate=pl.CostEstimate(
            flops=16 * 4 * BLOCK * ROWS * 256, bytes_accessed=4 << 20, transcendentals=2 << 20
        ),
        name="own_start",
    )(meta, order, q, kv)


def attend_kernel(steps, starts, final, *refs):
    count = len(steps)
    meta_ref, order_ref, q_ref = refs[:3]
    kv_refs = refs[3 : 3 + count]
    rest = refs[3 + count :]
    if not starts:
        m_in, acc_in = rest[:2]
        rest = rest[2:]
    if final:
        out_ref, m_ref, acc_ref = rest[:3]
        rest = rest[3:]
    else:
        m_ref, acc_ref = rest[:2]
        rest = rest[2:]
    kv_s, scores_a, scores_b, max_a, max_b, item_q, item_k, item_v, item_f, sems = rest

    copies = []
    at = 0
    for n, (size, _, _) in enumerate(steps):
        copies.append(pltpu.make_async_copy(kv_refs[n], kv_s.at[pl.ds(at, size)], sems.at[n]))
        copies[-1].start()
        at += size
    total = at
    kv_s[total] = jnp.zeros((2 * BLOCK, HEAD_DIM), BF16)
    if starts:
        m_ref[...] = jnp.full(m_ref.shape, NEG, F32)
        acc_ref[...] = jnp.zeros(acc_ref.shape, F32)
    else:
        m_ref[...] = m_in[...]
        acc_ref[...] = acc_in[...]

    yh, z, c = meta_ref[0], meta_ref[1], meta_ref[2]
    up = 2 * c - 1
    q_side = 1 - yh if starts or final else yh
    q_first = (q_side * 8 + z) * BLOCKS

    begin = 0
    for i in range(BLOCKS):
        q_pos = order_ref[q_first + i]
        fill = begin
        t = 0
        for size, distance, half in steps:
            plane = (z + up * distance + 16) & 7
            base = (yh * 8 + plane) * BLOCKS
            if size < BLOCKS:
                base = base + (c if half == 0 else 1 - c) * size
            for b in range(size):
                item_q[fill >> 1] = i
                item_k[fill] = t
                item_v[fill] = t
                item_f[fill] = 1.0
                fill = fill + jnp.where(order_ref[base + b] < q_pos, 1, 0)
                t += 1
        last = item_k[jnp.maximum(fill - 1, 0)]
        item_k[fill] = last
        item_v[fill] = total
        item_f[fill] = 0.0
        begin = begin + (((fill - begin) + 1) >> 1) * 2
    items = begin >> 1
    back = jnp.maximum(items - 1, 0)
    again_q, again_k, again_l = item_q[back], item_k[2 * back], item_k[2 * back + 1]
    again_q = jnp.where(items > 0, again_q, 0)
    again_k = jnp.where(items > 0, again_k, 0)
    again_l = jnp.where(items > 0, again_l, 0)
    for n in range(2):
        item_q[items + n] = again_q
        item_k[2 * (items + n)] = again_k
        item_k[2 * (items + n) + 1] = again_l
        item_v[2 * (items + n)] = total
        item_v[2 * (items + n) + 1] = total
        item_f[2 * (items + n)] = 0.0
        item_f[2 * (items + n) + 1] = 0.0

    for copy in copies:
        copy.wait()

    halves = [slice(0, BLOCK), slice(BLOCK, ROWS)]

    def score(j, scores, maxima, cols):
        keys = jnp.concatenate([kv_s[item_k[2 * j], :BLOCK], kv_s[item_k[2 * j + 1], :BLOCK]], 0)
        s = nt(keys, q_ref[item_q[j], :, cols]) * LOG2E_SCALE
        scores[:, cols] = s
        maxima[:, cols] = jnp.max(s, axis=0, keepdims=True)

    def absorb(j, scores, maxima, cols):
        i = item_q[j]
        values = jnp.concatenate([value_of(kv_s, item_v[2 * j + n]) for n in range(2)], axis=1)
        ones = jnp.concatenate(
            [jnp.full((16, BLOCK), item_f[2 * j + n], F32).astype(BF16) for n in range(2)], axis=1
        )
        lhs = jnp.concatenate([values, ones], axis=0)
        old = m_ref[i, :, cols]
        new = jnp.maximum(old, maxima[:, cols])
        keep = jnp.exp2(old - new)
        m_ref[i, :, cols] = new
        p = jnp.exp2(scores[:, cols] - new).astype(BF16)
        acc_ref[i, :, cols] = acc_ref[i, :, cols] * keep + nt(lhs, p)

    def both(j, scores, maxima, next_scores, next_maxima):
        for cols in halves:
            score(j + 1, next_scores, next_maxima, cols)
            absorb(j, scores, maxima, cols)

    for cols in halves:
        score(0, scores_a, max_a, cols)

    def two_items(h, carry):
        both(2 * h, scores_a, max_a, scores_b, max_b)
        both(2 * h + 1, scores_b, max_b, scores_a, max_a)
        return carry

    lax.fori_loop(0, (items + 1) >> 1, two_items, 0)

    if final:
        sub = lax.broadcasted_iota(jnp.int32, (16, ROWS), 0)
        for i in range(BLOCKS):
            sums = acc_ref[i, HEAD_DIM : HEAD_DIM + 1]
            some = sums > 0.0
            safe = jnp.where(some, sums, 1.0)
            logs = jnp.where(some, m_ref[i] + jnp.log2(safe), NEG)
            high = logs.astype(BF16).astype(F32)
            middle = (logs - high).astype(BF16).astype(F32)
            low = logs - high - middle
            out_ref[i, :HEAD_DIM] = (acc_ref[i, :HEAD_DIM] * (1.0 / safe)).astype(BF16)
            out_ref[i, HEAD_DIM:] = jnp.where(
                sub == 0, high, jnp.where(sub == 1, middle, jnp.where(sub == 2, low, 0.0))
            ).astype(BF16)


def attend(meta, order, q, shards, state, final):
    steps = tuple((a.shape[0], distance, half) for a, distance, half in shards)
    total = sum(s[0] for s in steps)
    starts = state is None
    args = [meta, order, q] + [a for a, _, _ in shards] + ([] if starts else list(state))
    m_shape, acc_shape = (BLOCKS, 1, ROWS), (BLOCKS, EXTENDED, ROWS)
    work = [pltpu.VMEM(m_shape, F32), pltpu.VMEM(acc_shape, F32)]
    if final:
        out_shape = (jax.ShapeDtypeStruct(acc_shape, BF16),)
    else:
        out_shape = (jax.ShapeDtypeStruct(m_shape, F32), jax.ShapeDtypeStruct(acc_shape, F32))
        work = []
    pairs = BLOCKS * total // 2
    slots = 2 * (BLOCKS * ((total + 1) // 2) + 4)
    got = pl.pallas_call(
        functools.partial(attend_kernel, steps, starts, final),
        out_shape=out_shape,
        in_specs=[SMEM, SMEM, VMEM] + [ANY] * len(shards) + ([] if starts else [VMEM, VMEM]),
        out_specs=tuple(VMEM for _ in out_shape),
        scratch_shapes=work
        + [
            pltpu.VMEM((total + 1, 2 * BLOCK, HEAD_DIM), BF16),
            pltpu.VMEM((2 * BLOCK, ROWS), F32),
            pltpu.VMEM((2 * BLOCK, ROWS), F32),
            pltpu.VMEM((1, ROWS), F32),
            pltpu.VMEM((1, ROWS), F32),
            pltpu.SMEM((slots // 2,), jnp.int32),
            pltpu.SMEM((slots,), jnp.int32),
            pltpu.SMEM((slots,), jnp.int32),
            pltpu.SMEM((slots,), F32),
            pltpu.SemaphoreType.DMA((len(shards),)),
        ],
        compiler_params=pltpu.CompilerParams(vmem_limit_bytes=VMEM_BYTES),
        cost_estimate=pl.CostEstimate(
            flops=pairs * 4 * BLOCK * ROWS * 256,
            bytes_accessed=6 << 20,
            transcendentals=pairs * BLOCK * ROWS,
        ),
        name="attend",
    )(*args)
    return got[0] if final else got


def combine_kernel(m_ref, acc_ref, other_ref, out_ref):
    for i in range(BLOCKS):
        sums = acc_ref[i, HEAD_DIM : HEAD_DIM + 1]
        mine = m_ref[i] + jnp.log2(sums)
        tail = other_ref[i, HEAD_DIM:].astype(F32)
        theirs = tail[0:1] + tail[1:2] + tail[2:3]
        top = jnp.maximum(mine, theirs)
        weight_mine, weight_theirs = jnp.exp2(mine - top), jnp.exp2(theirs - top)
        whole = weight_mine + weight_theirs
        result = acc_ref[i, :HEAD_DIM] * (weight_mine / (sums * whole)) + other_ref[
            i, :HEAD_DIM
        ].astype(F32) * (weight_theirs / whole)
        result = result.astype(BF16)
        for h in range(2):
            out_ref[i, :, h * HEAD_DIM : (h + 1) * HEAD_DIM] = result[
                :, h * BLOCK : (h + 1) * BLOCK
            ].T


def combine(state, other):
    return pl.pallas_call(
        combine_kernel,
        out_shape=jax.ShapeDtypeStruct((BLOCKS, BLOCK, 2 * HEAD_DIM), BF16),
        in_specs=[VMEM] * 3,
        out_specs=VMEM,
        name="combine",
    )(*state, other)


def body(queries, keys, values, block_order):
    rows = queries.shape[0]
    group = ("c", "yl", "x")
    z_size = lax.axis_size("z")
    meta = jnp.stack([lax.axis_index("yh"), lax.axis_index("z"), lax.axis_index("c")]).astype(jnp.int32)
    to_send = jnp.concatenate(
        [
            queries.reshape(rows, 8, 2, 256).transpose(2, 1, 0, 3),
            jnp.broadcast_to(keys.reshape(rows, 8, 128).transpose(1, 0, 2)[None], (2, 8, rows, 128)),
            jnp.broadcast_to(values.reshape(rows, 8, 128).transpose(1, 0, 2)[None], (2, 8, rows, 128)),
        ],
        axis=3,
    ).reshape(16, rows, 512)
    got = lax.all_to_all(to_send, group, 0, 0, tiled=True).reshape(BLOCKS, BLOCK, 512)
    q, kv = prepare(got)

    ring = [(2 * i + k, 2 * ((i + 1 - 2 * k) % z_size) + k) for i in range(z_size) for k in (0, 1)]
    swap = [(0, 1), (1, 0)]

    def onward(a):
        return lax.ppermute(a, ("z", "c"), ring)

    def swapped(a):
        return lax.ppermute(a, "c", swap)

    r1 = onward(kv)
    other_q = lax.ppermute(q, "yh", swap)
    s1, r2 = swapped(r1), onward(r1)
    s2, r3 = swapped(r2), onward(r2)
    r4 = onward(lax.dynamic_slice_in_dim(r3, 2 * lax.axis_index("c"), 2, 0))
    s3, s4 = swapped(r3), swapped(r4)

    mine = own_start(meta, block_order, q, kv)
    mine = attend(meta, block_order, q, [(r1, 1, 0), (s1, -1, 0)], mine, False)
    theirs = attend(meta, block_order, other_q, [(kv, 0, 0), (r1, 1, 0), (s1, -1, 0), (r2, 2, 0), (s2, -2, 0)], None, False)
    mine = attend(meta, block_order, q, [(r2, 2, 0), (s2, -2, 0)], mine, False)
    late = [(r3, 3, 0), (s3, -3, 0), (r4, 4, 0), (s4, -4, 1)]
    sent = attend(meta, block_order, other_q, late, theirs, True)
    other = lax.ppermute(sent, "yh", swap)
    mine = attend(meta, block_order, q, late, mine, False)
    result = combine(mine, other).reshape(16, rows, 256)
    back = lax.all_to_all(result, group, 0, 0, tiled=True)
    return back.reshape(2, 8, rows, 256).transpose(2, 1, 0, 3).reshape(rows, 4096)


def solution(mesh):
    fine = Mesh(mesh.devices.reshape(2, 8, 2, 2, 4), AXES)
    spec = P(AXES, None)
    return jax.shard_map(
        body, mesh=fine, in_specs=(spec, spec, spec, P()), out_specs=spec, check_vma=False
    )
```

time: 487 us -> 141 us (0.29)
  the two profiles are of different devices: /device:TPU:16 before, /device:TPU:81 now
where the time goes in v1:
time: 141 us; the launch traced here: 143 us
  Pallas kernels  46.5 us (33%)
  blocking collectives  36.8 us (26%)
  starting transfers between devices  24.9 us (18%)
  waiting for transfers between devices  22.3 us (16%)
  local copies, waits for them, and re-layouts  10.4 us (7%)
  other arithmetic  1.5 us (1%)
    pallas_call x5, Pallas kernels, attend(): pl.pallas_call(functools.partial(attend_kernel, steps, starts, final), ou...  37.2 us
    ppermute x4, waiting for transfers between devices, onward(): return lax.ppermute(a, ('z', 'c'), ring)  22.3 us
    all_to_all x1, blocking collectives, body(): lax.all_to_all(to_send, group, 0, 0, tiled=True).reshape(BLOCKS, BLOCK, 512)  21.9 us
    all_to_all x1, blocking collectives, body(): back = lax.all_to_all(result, group, 0, 0, tiled=True)  14.9 us
    ppermute x1, starting transfers between devices, body(): other = lax.ppermute(sent, 'yh', swap)  13.9 us
    ppermute x4, starting transfers between devices, swapped(): return lax.ppermute(a, 'c', swap)  10.6 us
    unnamed x18, local copies, waits for them, and re-layouts  6.38 us
    pallas_call x1, Pallas kernels, own_start(): pl.pallas_call(own_kernel, out_shape=(jax.ShapeDtypeStruct((BLOCKS, 1, RO...  4.28 us
  transfers between devices with their start and end apart: 10, of which 3 were waited for; matrix products, arithmetic and copies ran while one was open for 0% of the time, Pallas kernels for 25%

profile of v1, /device:TPU:81, one launch (start us, length us, event | category | flops | bytes accessed | tf_op | source)
XLA Modules:
  0.0 142.6 jit_solution(14451550822477432005)
XLA Ops:
  0.0 0.9 copy.8
  0.9 0.9 copy.7
  1.9 1.4 reshape.26
  3.3 0.2 broadcast_in_dim.5
  3.5 0.2 broadcast_in_dim.4
  3.6 1.4 pad_maximum_fusion
  5.0 0.6 copy.5
  5.6 21.9 %all_to_all.10 = bf16[16,64,512]{2,1,0:T(8,128)(2,1)} all-to-all(bf16[16,64,512]{2,1,0:T(8,128)(2,1)S(1)} %bitcast.20), channel_id=1, replica_groups=mesh['yh'=2,'z'=8,'c'=2,'yl'=2,'x'=4] {'c','yl','x'}, dimensions={0} | all-to-all | bytes 2097152 | tf_op jit(solution)/shard_map/all_to_all | solution.py:316
  27.5 2.5 %prepare.1 = (bf16[4,128,512]{2,1,0:T(8,128)(2,1)}, bf16[4,512,128]{2,1,0:T(8,128)(2,1)}) custom-call(bf16[4,256,512]{2,1,0:T(8,128)(2,1)} %bitcast.19), custom_call_target="tpu_custom_call" | custom-call | tf_op jit(solution)/shard_map/prepare/pallas_call | solution.py:45
  30.0 0.0 collective-permute-start
  30.0 8.7 %collective-permute-done.refs_3_.refs_4_ = bf16[4,512,128]{2,1,0:T(8,128)(2,1)S(1)} collective-permute-done((bf16[4,512,128]{2,1,0:T(8,128)(2,1)}, bf16[4,512,128]{2,1,0:T(8,128)(2,1)S(1)}, u32[]{:S(2)}, u32[]{:S(2)}) %collective-permute-start) | collective-permute-done | bytes 524320 | tf_op jit(solution)/shard_map/ppermute | solution.py:323
  38.7 0.0 collective-permute-start.1
  38.7 9.4 %collective-permute-done.1.refs_3_.refs_6_ = bf16[4,512,128]{2,1,0:T(8,128)(2,1)S(1)} collective-permute-done((bf16[4,512,128]{2,1,0:T(8,128)(2,1)S(1)}, bf16[4,512,128]{2,1,0:T(8,128)(2,1)S(1)}, u32[]{:S(2)}, u32[]{:S(2)}) %collective-permute-start.1) | collective-permute-done | bytes 524320 | tf_op jit(solution)/shard_map/ppermute | solution.py:323
  48.1 0.0 collective-permute-start.2
  48.1 0.3 collective-permute-start.8
  48.4 4.7 %collective-permute-start.7 = (bf16[4,512,128]{2,1,0:T(8,128)(2,1)S(1)}, bf16[4,512,128]{2,1,0:T(8,128)(2,1)S(1)}, u32[]{:S(2)}, u32[]{:S(2)}) collective-permute-start(bf16[4,512,128]{2,1,0:T(8,128)(2,1)S(1)} %collective-permute-done.refs_3_.refs_4_), channel_id=1, source_target_pairs={{0,8},{8,0},{1,9},{9,1},{2,10},{10,2},{3,11},{11,3},{4,12},{12,4},... | collective-permute-start | bytes 1572872 | tf_op jit(solution)/shard_map/ppermute | solution.py:326
  53.1 0.0 collective-permute-start.6
  53.2 4.2 %collective-permute-done.2.refs_3_ = bf16[4,512,128]{2,1,0:T(8,128)(2,1)S(1)} collective-permute-done((bf16[4,512,128]{2,1,0:T(8,128)(2,1)S(1)}, bf16[4,512,128]{2,1,0:T(8,128)(2,1)S(1)}, u32[]{:S(2)}, u32[]{:S(2)}) %collective-permute-start.2) | collective-permute-done | bytes 524320 | tf_op jit(solution)/shard_map/ppermute | solution.py:323
  57.3 0.1 collective-permute-start.4
  57.4 0.1 pad_add_fusion.meta_ref.refs_0_
  57.5 5.6 %collective-permute-start.3 = (bf16[4,512,128]{2,1,0:T(8,128)(2,1)S(1)}, bf16[4,512,128]{2,1,0:T(8,128)(2,1)S(1)}, u32[]{:S(2)}, u32[]{:S(2)}) collective-permute-start(bf16[4,512,128]{2,1,0:T(8,128)(2,1)S(1)} %collective-permute-done.2.refs_3_), channel_id=1, source_target_pairs={{0,8},{8,0},{1,9},{9,1},{2,10},{10,2},{3,11},{11,3},{4,12},{12,4},... | collective-permute-start | bytes 1572872 | tf_op jit(solution)/shard_map/ppermute | solution.py:326
  63.1 0.0 copy-done.6
  63.1 1.0 copy-done.2
  64.2 1.0 copy-done.4
  65.2 4.3 %own_start.1 = (f32[4,1,512]{2,1,0:T(1,128)S(1)}, f32[4,144,512]{2,1,0:T(8,128)S(1)}) custom-call(s32[3]{0:T(128)S(1)} %pad_add_fusion.meta_ref.refs_0_, s32[64]{0:T(128)S(1)} %copy-done.6, bf16[4,128,512]{2,1,0:T(8,128)(2,1)S(1)} %copy-done.2, bf16[4,512,128]{2,1,0:T(8,128)(2,1)S(1)} %copy-done.4), custom_call_target="tpu_custom_call" | custom-call | flops 2147483648 | bytes 4194304 | tf_op jit(solution)/shard_map/own_start/pallas_call | solution.py:86
  69.5 0.0 collective-permute-done.4.refs_5_
  69.5 0.3 collective-permute-start.5
  69.8 0.0 collective-permute-done.8.refs_2_
  69.8 0.0 collective-permute-done.7.refs_4_.refs_5_
  69.8 0.0 collective-permute-done.6.refs_4_.refs_7_
  69.8 0.0 copy-done.5
  69.8 7.5 %attend.8 = (f32[4,1,512]{2,1,0:T(1,128)S(1)}, f32[4,144,512]{2,1,0:T(8,128)S(1)}) custom-call(s32[3]{0:T(128)S(1)} %pad_add_fusion.meta_ref.refs_0_, s32[64]{0:T(128)S(1)} %copy-done.6, bf16[4,128,512]{2,1,0:T(8,128)(2,1)S(1)} %collective-permute-done.8.refs_2_, bf16[4,512,128]{2,1,0:T(8,128)(2,1)S(1)} %copy-done.5, ...), custom_call_target="tpu_custom_call" | custom-call | flops 5368709120 | bytes 6291456 | tf_op jit(solution)/shard_map/attend/pallas_call | solution.py:245
  77.3 0.0 collective-permute-done.5.refs_6_
  77.3 0.0 collective-permute-done.3.refs_4_
  77.3 0.0 copy-start.3
  77.3 5.9 %attend.9 = bf16[4,144,512]{2,1,0:T(8,128)(2,1)S(1)} custom-call(s32[3]{0:T(128)S(1)} %pad_add_fusion.meta_ref.refs_0_, s32[64]{0:T(128)S(1)} %copy-done.6, bf16[4,128,512]{2,1,0:T(8,128)(2,1)S(1)} %collective-permute-done.8.refs_2_, bf16[4,512,128]{2,1,0:T(8,128)(2,1)S(1)} %collective-permute-done.2.refs_3_, ...), custom_call_target="tpu_custom_call" | custom-call | flops 3221225472 | bytes 6291456 | tf_op jit(solution)/shard_map/attend/pallas_call | solution.py:245
  83.2 13.9 %collective-permute-start.9 = (bf16[4,144,512]{2,1,0:T(8,128)(2,1)S(1)}, bf16[4,144,512]{2,1,0:T(8,128)(2,1)S(1)}, u32[]{:S(2)}, u32[]{:S(2)}) collective-permute-start(bf16[4,144,512]{2,1,0:T(8,128)(2,1)S(1)} %attend.9), channel_id=1, source_target_pairs={{0,128},{128,0},{1,129},{129,1},{2,130},{130,2},{3,131},{131,3},{4... | collective-permute-start | bytes 1769480 | tf_op jit(solution)/shard_map/ppermute | solution.py:341
  97.1 6.4 %attend.5 = (f32[4,1,512]{2,1,0:T(1,128)S(1)}, f32[4,144,512]{2,1,0:T(8,128)S(1)}) custom-call(s32[3]{0:T(128)S(1)} %pad_add_fusion.meta_ref.refs_0_, s32[64]{0:T(128)S(1)} %copy-done.6, bf16[4,128,512]{2,1,0:T(8,128)(2,1)S(1)} %copy-done.3, bf16[4,512,128]{2,1,0:T(8,128)(2,1)S(1)} %collective-permute-done.refs_3_.refs_4_, ...), custom_call_target="tpu_custom_call" | custom-call | flops 2147483648 | bytes 6291456 | tf_op jit(solution)/shard_map/attend/pallas_call | solution.py:245
  103.5 7.2 %attend.6 = (f32[4,1,512]{2,1,0:T(1,128)S(1)}, f32[4,144,512]{2,1,0:T(8,128)S(1)}) custom-call(s32[3]{0:T(128)S(1)} %pad_add_fusion.meta_ref.refs_0_, s32[64]{0:T(128)S(1)} %copy-done.6, bf16[4,128,512]{2,1,0:T(8,128)(2,1)S(1)} %copy-done.3, bf16[4,512,128]{2,1,0:T(8,128)(2,1)S(1)} %collective-permute-done.1.refs_3_.refs_6_, ...), custom_call_target="tpu_custom_call" | custom-call | flops 2147483648 | bytes 6291456 | tf_op jit(solution)/shard_map/attend/pallas_call | solution.py:245
  110.7 10.3 %attend.7 = (f32[4,1,512]{2,1,0:T(1,128)S(1)}, f32[4,144,512]{2,1,0:T(8,128)S(1)}) custom-call(s32[3]{0:T(128)S(1)} %pad_add_fusion.meta_ref.refs_0_, s32[64]{0:T(128)S(1)} %copy-done.6, bf16[4,128,512]{2,1,0:T(8,128)(2,1)S(1)} %copy-done.3, bf16[4,512,128]{2,1,0:T(8,128)(2,1)S(1)} %collective-permute-done.2.refs_3_, ...), custom_call_target="tpu_custom_call" | custom-call | flops 3221225472 | bytes 6291456 | tf_op jit(solution)/shard_map/attend/pallas_call | solution.py:245
  121.0 1.0 copy-done
  122.1 0.6 copy-done.1
  122.7 0.0 collective-permute-done.9.other_ref
  122.7 0.8 copy-done.7
  123.5 2.5 %combine.1 = bf16[4,256,256]{2,1,0:T(8,128)(2,1)} custom-call(f32[4,1,512]{2,1,0:T(1,128)} %copy-done.1, f32[4,144,512]{2,1,0:T(8,128)} %copy-done, bf16[4,144,512]{2,1,0:T(8,128)(2,1)} %copy-done.7), custom_call_target="tpu_custom_call" | custom-call | tf_op jit(solution)/shard_map/combine/pallas_call | solution.py:294
  126.0 14.9 %all_to_all.11 = bf16[16,64,256]{2,1,0:T(8,128)(2,1)S(1)} all-to-all(bf16[16,64,256]{2,1,0:T(8,128)(2,1)} %bitcast.24), channel_id=1, replica_groups=mesh['yh'=2,'z'=8,'c'=2,'yl'=2,'x'=4] {'c','yl','x'}, dimensions={0} | all-to-all | bytes 1048576 | tf_op jit(solution)/shard_map/all_to_all | solution.py:344
  140.9 0.5 copy.10
  141.4 1.2 reshape.33
  (9 shorter events, 0.0 us)
Async XLA Ops:
  27.5 35.6 %copy-start.6 = (s32[64]{0:T(128)S(1)}, s32[64]{0:T(128)}, u32[]{:S(2)}) copy-start(s32[64]{0:T(128)} %refs_1_.9) | copy-start | bytes 772
  30.0 8.7 %collective-permute-start = (bf16[4,512,128]{2,1,0:T(8,128)(2,1)}, bf16[4,512,128]{2,1,0:T(8,128)(2,1)S(1)}, u32[]{:S(2)}, u32[]{:S(2)}) collective-permute-start(bf16[4,512,128]{2,1,0:T(8,128)(2,1)} %get-tuple-element.18.kv_ref.refs_3_), channel_id=1, source_target_pairs={{0,16},{8,120},{16,32},{24,8},{32,48},{40,24},{48,64},{56,40},{64,... | collective-permute-start | bytes 1572872 | tf_op jit(solution)/shard_map/ppermute | solution.py:323
  38.7 9.4 %collective-permute-start.1 = (bf16[4,512,128]{2,1,0:T(8,128)(2,1)S(1)}, bf16[4,512,128]{2,1,0:T(8,128)(2,1)S(1)}, u32[]{:S(2)}, u32[]{:S(2)}) collective-permute-start(bf16[4,512,128]{2,1,0:T(8,128)(2,1)S(1)} %collective-permute-done.refs_3_.refs_4_), channel_id=1, source_target_pairs={{0,16},{8,120},{16,32},{24,8},{32,48},{40,24},{48,64},{56,40},{64,... | collective-permute-start | bytes 1572872 | tf_op jit(solution)/shard_map/ppermute | solution.py:323
  48.1 9.2 %collective-permute-start.2 = (bf16[4,512,128]{2,1,0:T(8,128)(2,1)S(1)}, bf16[4,512,128]{2,1,0:T(8,128)(2,1)S(1)}, u32[]{:S(2)}, u32[]{:S(2)}) collective-permute-start(bf16[4,512,128]{2,1,0:T(8,128)(2,1)S(1)} %collective-permute-done.1.refs_3_.refs_6_), channel_id=1, source_target_pairs={{0,16},{8,120},{16,32},{24,8},{32,48},{40,24},{48,64},{56,40},{64,... | collective-permute-start | bytes 1572872 | tf_op jit(solution)/shard_map/ppermute | solution.py:323
  48.1 21.7 %collective-permute-start.8 = (bf16[4,128,512]{2,1,0:T(8,128)(2,1)}, bf16[4,128,512]{2,1,0:T(8,128)(2,1)S(1)}, u32[]{:S(2)}, u32[]{:S(2)}) collective-permute-start(bf16[4,128,512]{2,1,0:T(8,128)(2,1)} %get-tuple-element.17.q_ref.refs_2_), channel_id=1, source_target_pairs={{0,128},{128,0},{1,129},{129,1},{2,130},{130,2},{3,131},{131,3},{4... | collective-permute-start | bytes 1572872 | tf_op jit(solution)/shard_map/ppermute | solution.py:329
  48.4 21.4 %collective-permute-start.7 = (bf16[4,512,128]{2,1,0:T(8,128)(2,1)S(1)}, bf16[4,512,128]{2,1,0:T(8,128)(2,1)S(1)}, u32[]{:S(2)}, u32[]{:S(2)}) collective-permute-start(bf16[4,512,128]{2,1,0:T(8,128)(2,1)S(1)} %collective-permute-done.refs_3_.refs_4_), channel_id=1, source_target_pairs={{0,8},{8,0},{1,9},{9,1},{2,10},{10,2},{3,11},{11,3},{4,12},{12,4},... | collective-permute-start | bytes 1572872 | tf_op jit(solution)/shard_map/ppermute | solution.py:326
  53.1 16.7 %collective-permute-start.6 = (bf16[4,512,128]{2,1,0:T(8,128)(2,1)S(1)}, bf16[4,512,128]{2,1,0:T(8,128)(2,1)S(1)}, u32[]{:S(2)}, u32[]{:S(2)}) collective-permute-start(bf16[4,512,128]{2,1,0:T(8,128)(2,1)S(1)} %collective-permute-done.1.refs_3_.refs_6_), channel_id=1, source_target_pairs={{0,8},{8,0},{1,9},{9,1},{2,10},{10,2},{3,11},{11,3},{4,12},{12,4},... | collective-permute-start | bytes 1572872 | tf_op jit(solution)/shard_map/ppermute | solution.py:326
  57.3 12.1 %collective-permute-start.4 = (bf16[2,512,128]{2,1,0:T(8,128)(2,1)S(1)}, bf16[2,512,128]{2,1,0:T(8,128)(2,1)S(1)}, u32[]{:S(2)}, u32[]{:S(2)}) collective-permute-start(bf16[2,512,128]{2,1,0:T(8,128)(2,1)S(1)} %constant_dynamic-slice_fusion), channel_id=1, source_target_pairs={{0,16},{8,120},{16,32},{24,8},{32,48},{40,24},{48,64},{56,40},{64,... | collective-permute-start | bytes 786440 | tf_op jit(solution)/shard_map/ppermute | solution.py:323
  57.5 19.8 %collective-permute-start.3 = (bf16[4,512,128]{2,1,0:T(8,128)(2,1)S(1)}, bf16[4,512,128]{2,1,0:T(8,128)(2,1)S(1)}, u32[]{:S(2)}, u32[]{:S(2)}) collective-permute-start(bf16[4,512,128]{2,1,0:T(8,128)(2,1)S(1)} %collective-permute-done.2.refs_3_), channel_id=1, source_target_pairs={{0,8},{8,0},{1,9},{9,1},{2,10},{10,2},{3,11},{11,3},{4,12},{12,4},... | collective-permute-start | bytes 1572872 | tf_op jit(solution)/shard_map/ppermute | solution.py:326
  63.1 1.0 copy-start.2
  64.2 1.0 copy-start.4
  65.2 4.6 %copy-start.5 = (bf16[4,512,128]{2,1,0:T(8,128)(2,1)S(1)}, bf16[4,512,128]{2,1,0:T(8,128)(2,1)}, u32[]{:S(2)}) copy-start(bf16[4,512,128]{2,1,0:T(8,128)(2,1)} %get-tuple-element.18.kv_ref.refs_3_) | copy-start | bytes 1572868
  69.5 7.8 %collective-permute-start.5 = (bf16[2,512,128]{2,1,0:T(8,128)(2,1)S(1)}, bf16[2,512,128]{2,1,0:T(8,128)(2,1)S(1)}, u32[]{:S(2)}, u32[]{:S(2)}) collective-permute-start(bf16[2,512,128]{2,1,0:T(8,128)(2,1)S(1)} %collective-permute-done.4.refs_5_), channel_id=1, source_target_pairs={{0,8},{8,0},{1,9},{9,1},{2,10},{10,2},{3,11},{11,3},{4,12},{12,4},... | collective-permute-start | bytes 786440 | tf_op jit(solution)/shard_map/ppermute | solution.py:326
  77.3 19.8 %copy-start.3 = (bf16[4,128,512]{2,1,0:T(8,128)(2,1)S(1)}, bf16[4,128,512]{2,1,0:T(8,128)(2,1)}, u32[]{:S(2)}) copy-start(bf16[4,128,512]{2,1,0:T(8,128)(2,1)} %get-tuple-element.17.q_ref.refs_2_) | copy-start | bytes 1572868
  83.2 39.5 %collective-permute-start.9 = (bf16[4,144,512]{2,1,0:T(8,128)(2,1)S(1)}, bf16[4,144,512]{2,1,0:T(8,128)(2,1)S(1)}, u32[]{:S(2)}, u32[]{:S(2)}) collective-permute-start(bf16[4,144,512]{2,1,0:T(8,128)(2,1)S(1)} %attend.9), channel_id=1, source_target_pairs={{0,128},{128,0},{1,129},{129,1},{2,130},{130,2},{3,131},{131,3},{4... | collective-permute-start | bytes 1769480 | tf_op jit(solution)/shard_map/ppermute | solution.py:341
  121.0 1.0 copy-start
  122.1 0.6 copy-start.1
  122.7 0.8 copy-start.7

commit v2 on v1

--- a/solution.py
+++ b/solution.py
@@ -13,7 +13,8 @@
 BLOCK = 256
 ROWS = 2 * BLOCK
 BLOCKS = 4
-EXTENDED = HEAD_DIM + 16
+EXTENDED = HEAD_DIM + 8
+PARTIAL = HEAD_DIM + 16
 NEG = -1e30
 LOG2E_SCALE = float(np.log2(np.e) / np.sqrt(HEAD_DIM))
 AXES = ("yh", "z", "c", "yl", "x")
@@ -21,8 +22,8 @@
 BF16 = jnp.bfloat16
 SMEM = pl.BlockSpec(memory_space=pltpu.SMEM)
 VMEM = pl.BlockSpec(memory_space=pltpu.VMEM)
-ANY = pl.BlockSpec(memory_space=pl.ANY)
-VMEM_BYTES = 48 * 2**20
+VMEM_BYTES = 16 * 2**20
+SMALL = pltpu.CompilerParams(vmem_limit_bytes=8 * 2**20)
 
 
 def nt(a, b):
@@ -50,6 +51,7 @@
         ),
         in_specs=[VMEM],
         out_specs=(VMEM, VMEM),
+        compiler_params=SMALL,
         name="prepare",
     )(got)
 
@@ -79,7 +81,7 @@
         scores = jnp.concatenate(parts, axis=0)
         row_max = jnp.max(scores, axis=0, keepdims=True)
         m_ref[i] = row_max
-        acc_ref[i] = nt(lhs, jnp.exp2(scores - row_max).astype(BF16))
+        acc_ref[i] = nt(lhs, jnp.exp2(scores - row_max).astype(BF16))[:EXTENDED]
 
 
 def own_start(meta, order, q, kv):
@@ -93,65 +95,66 @@
         out_specs=(VMEM, VMEM),
         compiler_params=pltpu.CompilerParams(vmem_limit_bytes=VMEM_BYTES),
         cost_estimate=pl.CostEstimate(
-            flops=16 * 4 * BLOCK * ROWS * 256, bytes_accessed=4 << 20, transcendentals=2 << 20
+            flops=16 * 4 * BLOCK * ROWS * 8, bytes_accessed=1 << 18, transcendentals=1 << 16
         ),
         name="own_start",
     )(meta, order, q, kv)
 
 
-def attend_kernel(steps, starts, final, *refs):
+def attend_kernel(steps, partner, starts, final, *refs):
     count = len(steps)
-    meta_ref, order_ref, q_ref = refs[:3]
-    kv_refs = refs[3 : 3 + count]
-    rest = refs[3 + count :]
+    meta_ref, order_ref = refs[:2]
+    q_refs, refs = (refs[2:4], refs[4:]) if partner else (refs[2:3], refs[3:])
+    kv_refs = refs[:count]
+    rest = refs[count:]
     if not starts:
         m_in, acc_in = rest[:2]
         rest = rest[2:]
     if final:
-        out_ref, m_ref, acc_ref = rest[:3]
-        rest = rest[3:]
+        out_ref, rest = rest[0], rest[1:]
+    m_ref, acc_ref, kv_s, scores_a, scores_b, max_a, max_b = rest[:7]
+    item_q, item_k, item_v, item_f = rest[7:11]
+    if partner:
+        q_ref = rest[11]
+        for n in range(2):
+            q_ref[2 * n : 2 * n + 2] = q_refs[n][...]
     else:
-        m_ref, acc_ref = rest[:2]
-        rest = rest[2:]
-    kv_s, scores_a, scores_b, max_a, max_b, item_q, item_k, item_v, item_f, sems = rest
-
-    copies = []
-    at = 0
-    for n, (size, _, _) in enumerate(steps):
-        copies.append(pltpu.make_async_copy(kv_refs[n], kv_s.at[pl.ds(at, size)], sems.at[n]))
-        copies[-1].start()
-        at += size
-    total = at
-    kv_s[total] = jnp.zeros((2 * BLOCK, HEAD_DIM), BF16)
+        q_ref = q_refs[0]
+
+    total = sum(size for size, _, _ in steps)
     if starts:
         m_ref[...] = jnp.full(m_ref.shape, NEG, F32)
         acc_ref[...] = jnp.zeros(acc_ref.shape, F32)
     else:
         m_ref[...] = m_in[...]
         acc_ref[...] = acc_in[...]
+    at = 0
+    for n, (size, _, _) in enumerate(steps):
+        kv_s[at : at + size] = kv_refs[n][...]
+        at += size
+    kv_s[total] = jnp.zeros((2 * BLOCK, HEAD_DIM), BF16)
 
     yh, z, c = meta_ref[0], meta_ref[1], meta_ref[2]
     up = 2 * c - 1
-    q_side = 1 - yh if starts or final else yh
-    q_first = (q_side * 8 + z) * BLOCKS
+    q_first = ((1 - yh if partner else yh) * 8 + z) * BLOCKS
+    k_pos = []
+    for size, distance, half in steps:
+        plane = (z + up * distance + 16) & 7
+        base = (yh * 8 + plane) * BLOCKS
+        if size < BLOCKS:
+            base = base + (c if half == 0 else 1 - c) * size
+        k_pos.extend(order_ref[base + b] for b in range(size))
 
     begin = 0
     for i in range(BLOCKS):
         q_pos = order_ref[q_first + i]
         fill = begin
-        t = 0
-        for size, distance, half in steps:
-            plane = (z + up * distance + 16) & 7
-            base = (yh * 8 + plane) * BLOCKS
-            if size < BLOCKS:
-                base = base + (c if half == 0 else 1 - c) * size
-            for b in range(size):
-                item_q[fill >> 1] = i
-                item_k[fill] = t
-                item_v[fill] = t
-                item_f[fill] = 1.0
-                fill = fill + jnp.where(order_ref[base + b] < q_pos, 1, 0)
-                t += 1
+        for t in range(total):
+            item_q[fill >> 1] = i
+            item_k[fill] = t
+            item_v[fill] = t
+            item_f[fill] = 1.0
+            fill = fill + jnp.where(k_pos[t] < q_pos, 1, 0)
         last = item_k[jnp.maximum(fill - 1, 0)]
         item_k[fill] = last
         item_v[fill] = total
@@ -159,10 +162,9 @@
         begin = begin + (((fill - begin) + 1) >> 1) * 2
     items = begin >> 1
     back = jnp.maximum(items - 1, 0)
-    again_q, again_k, again_l = item_q[back], item_k[2 * back], item_k[2 * back + 1]
-    again_q = jnp.where(items > 0, again_q, 0)
-    again_k = jnp.where(items > 0, again_k, 0)
-    again_l = jnp.where(items > 0, again_l, 0)
+    again_q = jnp.where(items > 0, item_q[back], 0)
+    again_k = jnp.where(items > 0, item_k[2 * back], 0)
+    again_l = jnp.where(items > 0, item_k[2 * back + 1], 0)
     for n in range(2):
         item_q[items + n] = again_q
         item_k[2 * (items + n)] = again_k
@@ -171,9 +173,6 @@
         item_v[2 * (items + n) + 1] = total
         item_f[2 * (items + n)] = 0.0
         item_f[2 * (items + n) + 1] = 0.0
-
-    for copy in copies:
-        copy.wait()
 
     halves = [slice(0, BLOCK), slice(BLOCK, ROWS)]
 
@@ -195,22 +194,28 @@
         keep = jnp.exp2(old - new)
         m_ref[i, :, cols] = new
         p = jnp.exp2(scores[:, cols] - new).astype(BF16)
-        acc_ref[i, :, cols] = acc_ref[i, :, cols] * keep + nt(lhs, p)
+        acc_ref[i, :, cols] = acc_ref[i, :, cols] * keep + nt(lhs, p)[:EXTENDED]
 
     def both(j, scores, maxima, next_scores, next_maxima):
         for cols in halves:
             score(j + 1, next_scores, next_maxima, cols)
             absorb(j, scores, maxima, cols)
 
+    def several(at_once, first):
+        def turn(h, carry):
+            j = first + at_once * h
+            for n in range(0, at_once, 2):
+                both(j + n, scores_a, max_a, scores_b, max_b)
+                both(j + n + 1, scores_b, max_b, scores_a, max_a)
+            return carry
+
+        return turn
+
     for cols in halves:
         score(0, scores_a, max_a, cols)
-
-    def two_items(h, carry):
-        both(2 * h, scores_a, max_a, scores_b, max_b)
-        both(2 * h + 1, scores_b, max_b, scores_a, max_a)
-        return carry
-
-    lax.fori_loop(0, (items + 1) >> 1, two_items, 0)
+    fours = items >> 2
+    lax.fori_loop(0, fours, several(4, 0), 0)
+    lax.fori_loop(0, (items - 4 * fours + 1) >> 1, several(2, 4 * fours), 0)
 
     if final:
         sub = lax.broadcasted_iota(jnp.int32, (16, ROWS), 0)
@@ -228,24 +233,24 @@
             ).astype(BF16)
 
 
-def attend(meta, order, q, shards, state, final):
+def attend(meta, order, q, shards, state, partner, final):
     steps = tuple((a.shape[0], distance, half) for a, distance, half in shards)
     total = sum(s[0] for s in steps)
     starts = state is None
-    args = [meta, order, q] + [a for a, _, _ in shards] + ([] if starts else list(state))
+    args = [meta, order] + list(q) + [a for a, _, _ in shards] + ([] if starts else list(state))
     m_shape, acc_shape = (BLOCKS, 1, ROWS), (BLOCKS, EXTENDED, ROWS)
-    work = [pltpu.VMEM(m_shape, F32), pltpu.VMEM(acc_shape, F32)]
     if final:
-        out_shape = (jax.ShapeDtypeStruct(acc_shape, BF16),)
+        out_shape = (jax.ShapeDtypeStruct((BLOCKS, PARTIAL, ROWS), BF16),)
+        work = [pltpu.VMEM(m_shape, F32), pltpu.VMEM(acc_shape, F32)]
     else:
         out_shape = (jax.ShapeDtypeStruct(m_shape, F32), jax.ShapeDtypeStruct(acc_shape, F32))
         work = []
     pairs = BLOCKS * total // 2
     slots = 2 * (BLOCKS * ((total + 1) // 2) + 4)
     got = pl.pallas_call(
-        functools.partial(attend_kernel, steps, starts, final),
+        functools.partial(attend_kernel, steps, partner, starts, final),
         out_shape=out_shape,
-        in_specs=[SMEM, SMEM, VMEM] + [ANY] * len(shards) + ([] if starts else [VMEM, VMEM]),
+        in_specs=[SMEM, SMEM] + [VMEM] * (len(args) - 2),
         out_specs=tuple(VMEM for _ in out_shape),
         scratch_shapes=work
         + [
@@ -258,13 +263,13 @@
             pltpu.SMEM((slots,), jnp.int32),
             pltpu.SMEM((slots,), jnp.int32),
             pltpu.SMEM((slots,), F32),
-            pltpu.SemaphoreType.DMA((len(shards),)),
-        ],
+        ]
+        + ([pltpu.VMEM((BLOCKS, HEAD_DIM, ROWS), BF16)] if partner else []),
         compiler_params=pltpu.CompilerParams(vmem_limit_bytes=VMEM_BYTES),
         cost_estimate=pl.CostEstimate(
-            flops=pairs * 4 * BLOCK * ROWS * 256,
-            bytes_accessed=6 << 20,
-            transcendentals=pairs * BLOCK * ROWS,
+            flops=pairs * 4 * BLOCK * ROWS * 8,
+            bytes_accessed=1 << 18,
+            transcendentals=pairs * BLOCK * ROWS // 32,
         ),
         name="attend",
     )(*args)
@@ -296,8 +301,51 @@
         out_shape=jax.ShapeDtypeStruct((BLOCKS, BLOCK, 2 * HEAD_DIM), BF16),
         in_specs=[VMEM] * 3,
         out_specs=VMEM,
+        compiler_params=SMALL,
         name="combine",
     )(*state, other)
+
+
+def pack_kernel(queries_ref, keys_ref, values_ref, out_ref):
+    for g in range(8):
+        keys = keys_ref[:, g * HEAD_DIM : (g + 1) * HEAD_DIM]
+        values = values_ref[:, g * HEAD_DIM : (g + 1) * HEAD_DIM]
+        for c in range(2):
+            first = (2 * g + c) * 2 * HEAD_DIM
+            out_ref[8 * c + g, :, : 2 * HEAD_DIM] = queries_ref[:, first : first + 2 * HEAD_DIM]
+            out_ref[8 * c + g, :, 2 * HEAD_DIM : 3 * HEAD_DIM] = keys
+            out_ref[8 * c + g, :, 3 * HEAD_DIM :] = values
+
+
+def pack(queries, keys, values):
+    rows = queries.shape[0]
+    return pl.pallas_call(
+        pack_kernel,
+        out_shape=jax.ShapeDtypeStruct((16, rows, 4 * HEAD_DIM), BF16),
+        in_specs=[VMEM] * 3,
+        out_specs=VMEM,
+        compiler_params=SMALL,
+        name="pack",
+    )(queries, keys, values)
+
+
+def unpack_kernel(back_ref, out_ref):
+    for g in range(8):
+        for c in range(2):
+            first = (2 * g + c) * 2 * HEAD_DIM
+            out_ref[:, first : first + 2 * HEAD_DIM] = back_ref[8 * c + g]
+
+
+def unpack(back):
+    rows = back.shape[1]
+    return pl.pallas_call(
+        unpack_kernel,
+        out_shape=jax.ShapeDtypeStruct((rows, 32 * HEAD_DIM), BF16),
+        in_specs=[VMEM],
+        out_specs=VMEM,
+        compiler_params=SMALL,
+        name="unpack",
+    )(back)
 
 
 def body(queries, keys, values, block_order):
@@ -305,16 +353,8 @@
     group = ("c", "yl", "x")
     z_size = lax.axis_size("z")
     meta = jnp.stack([lax.axis_index("yh"), lax.axis_index("z"), lax.axis_index("c")]).astype(jnp.int32)
-    to_send = jnp.concatenate(
-        [
-            queries.reshape(rows, 8, 2, 256).transpose(2, 1, 0, 3),
-            jnp.broadcast_to(keys.reshape(rows, 8, 128).transpose(1, 0, 2)[None], (2, 8, rows, 128)),
-            jnp.broadcast_to(values.reshape(rows, 8, 128).transpose(1, 0, 2)[None], (2, 8, rows, 128)),
-        ],
-        axis=3,
-    ).reshape(16, rows, 512)
-    got = lax.all_to_all(to_send, group, 0, 0, tiled=True).reshape(BLOCKS, BLOCK, 512)
-    q, kv = prepare(got)
+    got = lax.all_to_all(pack(queries, keys, values), group, 0, 0, tiled=True)
+    q, kv = prepare(got.reshape(BLOCKS, BLOCK, 512))
 
     ring = [(2 * i + k, 2 * ((i + 1 - 2 * k) % z_size) + k) for i in range(z_size) for k in (0, 1)]
     swap = [(0, 1), (1, 0)]
@@ -326,23 +366,33 @@
         return lax.ppermute(a, "c", swap)
 
     r1 = onward(kv)
-    other_q = lax.ppermute(q, "yh", swap)
-    s1, r2 = swapped(r1), onward(r1)
-    s2, r3 = swapped(r2), onward(r2)
+    other_a = lax.ppermute(q[:2], "yh", swap)
+    mine = own_start(meta, block_order, q, kv)
+    r1, mine, other_a, q = lax.optimization_barrier((r1, mine, other_a, q))
+
+    r2, s1 = onward(r1), swapped(r1)
+    other_q = (other_a, lax.ppermute(q[2:], "yh", swap))
+    near = [(r1, 1, 0), (s1, -1, 0)]
+    mine = attend(meta, block_order, (q,), near, mine, False, False)
+    r2, mine, other_q = lax.optimization_barrier((r2, mine, other_q))
+
+    r3, s2 = onward(r2), swapped(r2)
+    theirs = attend(meta, block_order, other_q, [(kv, 0, 0)] + near, None, True, False)
+    r3, theirs = lax.optimization_barrier((r3, theirs))
+
     r4 = onward(lax.dynamic_slice_in_dim(r3, 2 * lax.axis_index("c"), 2, 0))
-    s3, s4 = swapped(r3), swapped(r4)
-
-    mine = own_start(meta, block_order, q, kv)
-    mine = attend(meta, block_order, q, [(r1, 1, 0), (s1, -1, 0)], mine, False)
-    theirs = attend(meta, block_order, other_q, [(kv, 0, 0), (r1, 1, 0), (s1, -1, 0), (r2, 2, 0), (s2, -2, 0)], None, False)
-    mine = attend(meta, block_order, q, [(r2, 2, 0), (s2, -2, 0)], mine, False)
-    late = [(r3, 3, 0), (s3, -3, 0), (r4, 4, 0), (s4, -4, 1)]
-    sent = attend(meta, block_order, other_q, late, theirs, True)
+    s3 = swapped(r3)
+    middle = [(r2, 2, 0), (s2, -2, 0)]
+    theirs = attend(meta, block_order, other_q, middle, theirs, True, False)
+    r4, theirs = lax.optimization_barrier((r4, theirs))
+
+    s4 = swapped(r4)
+    far = [(r3, 3, 0), (s3, -3, 0), (r4, 4, 0), (s4, -4, 1)]
+    sent = attend(meta, block_order, other_q, far, theirs, True, True)
     other = lax.ppermute(sent, "yh", swap)
-    mine = attend(meta, block_order, q, late, mine, False)
+    mine = attend(meta, block_order, (q,), middle + far, mine, False, False)
     result = combine(mine, other).reshape(16, rows, 256)
-    back = lax.all_to_all(result, group, 0, 0, tiled=True)
-    return back.reshape(2, 8, rows, 256).transpose(2, 1, 0, 3).reshape(rows, 4096)
+    return unpack(lax.all_to_all(result, group, 0, 0, tiled=True))
 
 
 def solution(mesh):

time: 141 us -> 108 us (0.77)
  the two profiles are of different devices: /device:TPU:81 before, /device:TPU:1 now
where the time goes in v2:
time: 108 us; the launch traced here: 109 us
  Pallas kernels  37.8 us (35%)
  blocking collectives  36.9 us (34%)
  starting transfers between devices  24.1 us (22%)
  local copies, waits for them, and re-layouts  6.02 us (6%)
  waiting for transfers between devices  4.05 us (4%)
    pallas_call x5, Pallas kernels, attend(): pl.pallas_call(functools.partial(attend_kernel, steps, partner, starts, f...  32 us
    all_to_all x1, blocking collectives, body(): got = lax.all_to_all(pack(queries, keys, values), group, 0, 0, tiled=True)  22.9 us
    all_to_all x1, blocking collectives, body(): return unpack(lax.all_to_all(result, group, 0, 0, tiled=True))  14 us
    ppermute x4, starting transfers between devices, onward(): return lax.ppermute(a, ('z', 'c'), ring)  13.5 us
    unnamed x20, local copies, waits for them, and re-layouts  5.96 us
    pallas_call x1, Pallas kernels, own_start(): pl.pallas_call(own_kernel, out_shape=(jax.ShapeDtypeStruct((BLOCKS, 1, RO...  4.29 us
    ppermute x1, starting transfers between devices, body(): other = lax.ppermute(sent, 'yh', swap)  3.44 us
    ppermute x1, waiting for transfers between devices, body(): other = lax.ppermute(sent, 'yh', swap)  2.86 us
  transfers between devices with their start and end apart: 11, of which 2 were waited for; matrix products, arithmetic and copies ran while one was open for 0% of the time, Pallas kernels for 27%

profile of v2, /device:TPU:1, one launch (start us, length us, event | category | flops | bytes accessed | tf_op | source)
XLA Modules:
  0.0 109.1 jit_solution(7907347495803587020)
XLA Ops:
  0.0 1.0 copy-done.6
  1.0 0.9 copy-done.7
  1.9 0.9 copy-done.8
  2.9 0.1 pack.1
  3.0 22.9 %all_to_all.10 = bf16[16,64,512]{2,1,0:T(8,128)(2,1)S(1)} all-to-all(bf16[16,64,512]{2,1,0:T(8,128)(2,1)S(1)} %pack.1), channel_id=1, replica_groups=mesh['yh'=2,'z'=8,'c'=2,'yl'=2,'x'=4] {'c','yl','x'}, dimensions={0} | all-to-all | bytes 2097152 | tf_op jit(solution)/shard_map/all_to_all | solution.py:356
  25.8 0.3 prepare.1
  26.1 5.7 %collective-permute-start = (bf16[4,512,128]{2,1,0:T(8,128)(2,1)S(1)}, bf16[4,512,128]{2,1,0:T(8,128)(2,1)S(1)}, u32[]{:S(2)}, u32[]{:S(2)}) collective-permute-start(bf16[4,512,128]{2,1,0:T(8,128)(2,1)S(1)} %get-tuple-element.33.kv_ref.refs_4_), channel_id=1, source_target_pairs={{0,16},{8,120},{16,32},{24,8},{32,48},{40,24},{48,64},{56,40},{64,... | collective-permute-start | bytes 1572872 | tf_op jit(solution)/shard_map/ppermute | solution.py:363
  31.8 2.7 %collective-permute-start.1 = (bf16[2,128,512]{2,1,0:T(8,128)(2,1)S(1)}, bf16[2,128,512]{2,1,0:T(8,128)(2,1)S(1)}, u32[]{:S(2)}, u32[]{:S(2)}) collective-permute-start(bf16[2,128,512]{2,1,0:T(8,128)(2,1)S(1)} %slice.6), channel_id=1, source_target_pairs={{0,128},{128,0},{1,129},{129,1},{2,130},{130,2},{3,131},{131,3},{4... | collective-permute-start | bytes 786440 | tf_op jit(solution)/shard_map/ppermute | solution.py:369
  34.5 0.1 pad_add_fusion.meta_ref.refs_0_
  34.6 0.0 copy-done.9
  34.6 4.3 %own_start.1 = (f32[4,1,512]{2,1,0:T(1,128)S(1)}, f32[4,136,512]{2,1,0:T(8,128)S(1)}) custom-call(s32[3]{0:T(128)S(1)} %pad_add_fusion.meta_ref.refs_0_, s32[64]{0:T(128)S(1)} %copy-done.9, bf16[4,128,512]{2,1,0:T(8,128)(2,1)S(1)} %get-tuple-element.37.q_ref.refs_2_, bf16[4,512,128]{2,1,0:T(8,128)(2,1)S(1)} %get-tuple-element.33.kv_ref.refs_4_), custom_call_target="tpu_custom_call" | custom-call | flops 67108864 | bytes 262144 | tf_op jit(solution)/shard_map/own_start/pallas_call | solution.py:88
  38.9 0.0 collective-permute-done.1.refs_2_
  38.9 0.0 collective-permute-done.refs_3_.refs_5_
  38.9 0.0 copy-start
  38.9 0.5 collective-permute-start.3
  39.4 3.3 %collective-permute-start.2 = (bf16[4,512,128]{2,1,0:T(8,128)(2,1)S(1)}, bf16[4,512,128]{2,1,0:T(8,128)(2,1)S(1)}, u32[]{:S(2)}, u32[]{:S(2)}) collective-permute-start(bf16[4,512,128]{2,1,0:T(8,128)(2,1)S(1)} %collective-permute-done.refs_3_.refs_5_), channel_id=1, source_target_pairs={{0,16},{8,120},{16,32},{24,8},{32,48},{40,24},{48,64},{56,40},{64,... | collective-permute-start | bytes 1572872 | tf_op jit(solution)/shard_map/ppermute | solution.py:363
  42.8 2.7 %collective-permute-start.4 = (bf16[2,128,512]{2,1,0:T(8,128)(2,1)S(1)}, bf16[2,128,512]{2,1,0:T(8,128)(2,1)S(1)}, u32[]{:S(2)}, u32[]{:S(2)}) collective-permute-start(bf16[2,128,512]{2,1,0:T(8,128)(2,1)S(1)} %slice.7), channel_id=1, source_target_pairs={{0,128},{128,0},{1,129},{129,1},{2,130},{130,2},{3,131},{131,3},{4... | collective-permute-start | bytes 786440 | tf_op jit(solution)/shard_map/ppermute | solution.py:374
  45.5 0.0 collective-permute-done.3.refs_4_.refs_6_
  45.5 3.5 %attend.5 = (f32[4,1,512]{2,1,0:T(1,128)S(1)}, f32[4,136,512]{2,1,0:T(8,128)S(1)}) custom-call(s32[3]{0:T(128)S(1)} %pad_add_fusion.meta_ref.refs_0_, s32[64]{0:T(128)S(1)} %copy-done.9, bf16[4,128,512]{2,1,0:T(8,128)(2,1)S(1)} %get-tuple-element.37.q_ref.refs_2_, bf16[4,512,128]{2,1,0:T(8,128)(2,1)S(1)} %collective-permute-done.refs_3_.refs_5_, ...), custom_call_target="tpu_custom_call" | custom-call | flops 67108864 | bytes 262144 | tf_op jit(solution)/shard_map/attend/pallas_call | solution.py:250
  49.0 0.0 copy-done
  49.0 0.0 copy-done.2
  49.0 0.0 copy-start.4
  49.0 1.0 copy-done.4
  50.0 0.0 collective-permute-done.4.refs_3_
  50.0 0.0 collective-permute-done.2.refs_4_.refs_3_
  50.0 3.0 %collective-permute-start.6 = (bf16[4,512,128]{2,1,0:T(8,128)(2,1)S(1)}, bf16[4,512,128]{2,1,0:T(8,128)(2,1)S(1)}, u32[]{:S(2)}, u32[]{:S(2)}) collective-permute-start(bf16[4,512,128]{2,1,0:T(8,128)(2,1)S(1)} %collective-permute-done.2.refs_4_.refs_3_), channel_id=1, source_target_pairs={{0,16},{8,120},{16,32},{24,8},{32,48},{40,24},{48,64},{56,40},{64,... | collective-permute-start | bytes 1572872 | tf_op jit(solution)/shard_map/ppermute | solution.py:363
  53.0 0.0 collective-permute-start.5
  53.1 1.0 copy-done.1
  54.1 1.0 copy-done.3
  55.1 5.7 %attend.6 = (f32[4,1,512]{2,1,0:T(1,128)S(1)}, f32[4,136,512]{2,1,0:T(8,128)S(1)}) custom-call(s32[3]{0:T(128)S(1)} %pad_add_fusion.meta_ref.refs_0_, s32[64]{0:T(128)S(1)} %copy-done.9, bf16[2,128,512]{2,1,0:T(8,128)(2,1)S(1)} %collective-permute-done.1.refs_2_, bf16[2,128,512]{2,1,0:T(8,128)(2,1)S(1)} %collective-permute-done.4.refs_3_, ...), custom_call_target="tpu_custom_call" | custom-call | flops 100663296 | bytes 262144 | tf_op jit(solution)/shard_map/attend/pallas_call | solution.py:250
  60.9 0.0 collective-permute-done.6.refs_5_.refs_4_
  60.9 1.5 %collective-permute-start.8 = (bf16[2,512,128]{2,1,0:T(8,128)(2,1)S(1)}, bf16[2,512,128]{2,1,0:T(8,128)(2,1)S(1)}, u32[]{:S(2)}, u32[]{:S(2)}) collective-permute-start(bf16[2,512,128]{2,1,0:T(8,128)(2,1)S(1)} %constant_dynamic-slice_fusion), channel_id=1, source_target_pairs={{0,16},{8,120},{16,32},{24,8},{32,48},{40,24},{48,64},{56,40},{64,... | collective-permute-start | bytes 786440 | tf_op jit(solution)/shard_map/ppermute | solution.py:363
  62.4 0.0 collective-permute-start.7
  62.4 0.0 collective-permute-done.5.refs_5_.refs_4_
  62.4 5.4 %attend.7 = (f32[4,1,512]{2,1,0:T(1,128)S(1)}, f32[4,136,512]{2,1,0:T(8,128)S(1)}) custom-call(s32[3]{0:T(128)S(1)} %pad_add_fusion.meta_ref.refs_0_, s32[64]{0:T(128)S(1)} %copy-done.9, bf16[2,128,512]{2,1,0:T(8,128)(2,1)S(1)} %collective-permute-done.1.refs_2_, bf16[2,128,512]{2,1,0:T(8,128)(2,1)S(1)} %collective-permute-done.4.refs_3_, ...), custom_call_target="tpu_custom_call" | custom-call | flops 67108864 | bytes 262144 | tf_op jit(solution)/shard_map/attend/pallas_call | solution.py:250
  67.8 0.0 collective-permute-done.8.refs_7_.refs_6_
  67.8 0.0 copy-start.5
  67.8 1.2 %collective-permute-start.9 = (bf16[2,512,128]{2,1,0:T(8,128)(2,1)S(1)}, bf16[2,512,128]{2,1,0:T(8,128)(2,1)S(1)}, u32[]{:S(2)}, u32[]{:S(2)}) collective-permute-start(bf16[2,512,128]{2,1,0:T(8,128)(2,1)S(1)} %collective-permute-done.8.refs_7_.refs_6_), channel_id=1, source_target_pairs={{0,8},{8,0},{1,9},{9,1},{2,10},{10,2},{3,11},{11,3},{4,12},{12,4},... | collective-permute-start | bytes 786440 | tf_op jit(solution)/shard_map/ppermute | solution.py:366
  69.1 1.2 %collective-permute-done.9.refs_8_.refs_7_ = bf16[2,512,128]{2,1,0:T(8,128)(2,1)S(1)} collective-permute-done((bf16[2,512,128]{2,1,0:T(8,128)(2,1)S(1)}, bf16[2,512,128]{2,1,0:T(8,128)(2,1)S(1)}, u32[]{:S(2)}, u32[]{:S(2)}) %collective-permute-start.9) | collective-permute-done | bytes 262176 | tf_op jit(solution)/shard_map/ppermute | solution.py:366
  70.2 0.0 collective-permute-done.7.refs_6_.refs_5_
  70.2 6.9 %attend.9 = bf16[4,144,512]{2,1,0:T(8,128)(2,1)S(1)} custom-call(s32[3]{0:T(128)S(1)} %pad_add_fusion.meta_ref.refs_0_, s32[64]{0:T(128)S(1)} %copy-done.9, bf16[2,128,512]{2,1,0:T(8,128)(2,1)S(1)} %collective-permute-done.1.refs_2_, bf16[2,128,512]{2,1,0:T(8,128)(2,1)S(1)} %collective-permute-done.4.refs_3_, ...), custom_call_target="tpu_custom_call" | custom-call | flops 100663296 | bytes 262144 | tf_op jit(solution)/shard_map/attend/pallas_call | solution.py:250
  77.2 3.4 %collective-permute-start.10 = (bf16[4,144,512]{2,1,0:T(8,128)(2,1)S(1)}, bf16[4,144,512]{2,1,0:T(8,128)(2,1)S(1)}, u32[]{:S(2)}, u32[]{:S(2)}) collective-permute-start(bf16[4,144,512]{2,1,0:T(8,128)(2,1)S(1)} %attend.9), channel_id=1, source_target_pairs={{0,128},{128,0},{1,129},{129,1},{2,130},{130,2},{3,131},{131,3},{4... | collective-permute-start | bytes 1769480 | tf_op jit(solution)/shard_map/ppermute | solution.py:392
  80.6 0.0 copy-done.5
  80.6 10.5 %attend.8 = (f32[4,1,512]{2,1,0:T(1,128)S(1)}, f32[4,136,512]{2,1,0:T(8,128)S(1)}) custom-call(s32[3]{0:T(128)S(1)} %pad_add_fusion.meta_ref.refs_0_, s32[64]{0:T(128)S(1)} %copy-done.9, bf16[4,128,512]{2,1,0:T(8,128)(2,1)S(1)} %get-tuple-element.37.q_ref.refs_2_, bf16[4,512,128]{2,1,0:T(8,128)(2,1)S(1)} %collective-permute-done.2.refs_4_.refs_3_, ...), custom_call_target="tpu_custom_call" | custom-call | flops 167772160 | bytes 262144 | tf_op jit(solution)/shard_map/attend/pallas_call | solution.py:250
  91.1 2.9 %collective-permute-done.10.other_ref = bf16[4,144,512]{2,1,0:T(8,128)(2,1)S(1)} collective-permute-done((bf16[4,144,512]{2,1,0:T(8,128)(2,1)S(1)}, bf16[4,144,512]{2,1,0:T(8,128)(2,1)S(1)}, u32[]{:S(2)}, u32[]{:S(2)}) %collective-permute-start.10) | collective-permute-done | bytes 589856 | tf_op jit(solution)/shard_map/ppermute | solution.py:392
  94.0 0.3 combine.1
  94.3 14.0 %all_to_all.11.back_ref = bf16[16,64,256]{2,1,0:T(8,128)(2,1)S(1)} all-to-all(bf16[16,64,256]{2,1,0:T(8,128)(2,1)S(1)} %bitcast.6), channel_id=1, replica_groups=mesh['yh'=2,'z'=8,'c'=2,'yl'=2,'x'=4] {'c','yl','x'}, dimensions={0} | all-to-all | bytes 1048576 | tf_op jit(solution)/shard_map/all_to_all | solution.py:395
  108.3 0.8 unpack.1
  (10 shorter events, 0.1 us)
Async XLA Ops:
  0.0 1.0 copy-start.6
  1.0 0.9 copy-start.7
  1.9 0.9 copy-start.8
  25.8 8.7 %copy-start.9 = (s32[64]{0:T(128)S(1)}, s32[64]{0:T(128)}, u32[]{:S(2)}) copy-start(s32[64]{0:T(128)} %refs_1_.9) | copy-start | bytes 772
  26.1 12.8 %collective-permute-start = (bf16[4,512,128]{2,1,0:T(8,128)(2,1)S(1)}, bf16[4,512,128]{2,1,0:T(8,128)(2,1)S(1)}, u32[]{:S(2)}, u32[]{:S(2)}) collective-permute-start(bf16[4,512,128]{2,1,0:T(8,128)(2,1)S(1)} %get-tuple-element.33.kv_ref.refs_4_), channel_id=1, source_target_pairs={{0,16},{8,120},{16,32},{24,8},{32,48},{40,24},{48,64},{56,40},{64,... | collective-permute-start | bytes 1572872 | tf_op jit(solution)/shard_map/ppermute | solution.py:363
  31.8 7.1 %collective-permute-start.1 = (bf16[2,128,512]{2,1,0:T(8,128)(2,1)S(1)}, bf16[2,128,512]{2,1,0:T(8,128)(2,1)S(1)}, u32[]{:S(2)}, u32[]{:S(2)}) collective-permute-start(bf16[2,128,512]{2,1,0:T(8,128)(2,1)S(1)} %slice.6), channel_id=1, source_target_pairs={{0,128},{128,0},{1,129},{129,1},{2,130},{130,2},{3,131},{131,3},{4... | collective-permute-start | bytes 786440 | tf_op jit(solution)/shard_map/ppermute | solution.py:369
  38.9 10.1 %copy-start = (bf16[4,512,128]{2,1,0:T(8,128)(2,1)}, bf16[4,512,128]{2,1,0:T(8,128)(2,1)S(1)}, u32[]{:S(2)}) copy-start(bf16[4,512,128]{2,1,0:T(8,128)(2,1)S(1)} %collective-permute-done.refs_3_.refs_5_) | copy-start | bytes 1572868
  38.9 6.6 %collective-permute-start.3 = (bf16[4,512,128]{2,1,0:T(8,128)(2,1)S(1)}, bf16[4,512,128]{2,1,0:T(8,128)(2,1)S(1)}, u32[]{:S(2)}, u32[]{:S(2)}) collective-permute-start(bf16[4,512,128]{2,1,0:T(8,128)(2,1)S(1)} %collective-permute-done.refs_3_.refs_5_), channel_id=1, source_target_pairs={{0,8},{8,0},{1,9},{9,1},{2,10},{10,2},{3,11},{11,3},{4,12},{12,4},... | collective-permute-start | bytes 1572872 | tf_op jit(solution)/shard_map/ppermute | solution.py:366
  39.4 10.6 %collective-permute-start.2 = (bf16[4,512,128]{2,1,0:T(8,128)(2,1)S(1)}, bf16[4,512,128]{2,1,0:T(8,128)(2,1)S(1)}, u32[]{:S(2)}, u32[]{:S(2)}) collective-permute-start(bf16[4,512,128]{2,1,0:T(8,128)(2,1)S(1)} %collective-permute-done.refs_3_.refs_5_), channel_id=1, source_target_pairs={{0,16},{8,120},{16,32},{24,8},{32,48},{40,24},{48,64},{56,40},{64,... | collective-permute-start | bytes 1572872 | tf_op jit(solution)/shard_map/ppermute | solution.py:363
  42.8 7.2 %collective-permute-start.4 = (bf16[2,128,512]{2,1,0:T(8,128)(2,1)S(1)}, bf16[2,128,512]{2,1,0:T(8,128)(2,1)S(1)}, u32[]{:S(2)}, u32[]{:S(2)}) collective-permute-start(bf16[2,128,512]{2,1,0:T(8,128)(2,1)S(1)} %slice.7), channel_id=1, source_target_pairs={{0,128},{128,0},{1,129},{129,1},{2,130},{130,2},{3,131},{131,3},{4... | collective-permute-start | bytes 786440 | tf_op jit(solution)/shard_map/ppermute | solution.py:374
  45.5 3.5 %copy-start.2 = (bf16[4,512,128]{2,1,0:T(8,128)(2,1)}, bf16[4,512,128]{2,1,0:T(8,128)(2,1)S(1)}, u32[]{:S(2)}) copy-start(bf16[4,512,128]{2,1,0:T(8,128)(2,1)S(1)} %collective-permute-done.3.refs_4_.refs_6_) | copy-start | bytes 1572868
  49.0 1.0 copy-start.4
  50.0 10.9 %collective-permute-start.6 = (bf16[4,512,128]{2,1,0:T(8,128)(2,1)S(1)}, bf16[4,512,128]{2,1,0:T(8,128)(2,1)S(1)}, u32[]{:S(2)}, u32[]{:S(2)}) collective-permute-start(bf16[4,512,128]{2,1,0:T(8,128)(2,1)S(1)} %collective-permute-done.2.refs_4_.refs_3_), channel_id=1, source_target_pairs={{0,16},{8,120},{16,32},{24,8},{32,48},{40,24},{48,64},{56,40},{64,... | collective-permute-start | bytes 1572872 | tf_op jit(solution)/shard_map/ppermute | solution.py:363
  53.0 9.3 %collective-permute-start.5 = (bf16[4,512,128]{2,1,0:T(8,128)(2,1)S(1)}, bf16[4,512,128]{2,1,0:T(8,128)(2,1)S(1)}, u32[]{:S(2)}, u32[]{:S(2)}) collective-permute-start(bf16[4,512,128]{2,1,0:T(8,128)(2,1)S(1)} %collective-permute-done.2.refs_4_.refs_3_), channel_id=1, source_target_pairs={{0,8},{8,0},{1,9},{9,1},{2,10},{10,2},{3,11},{11,3},{4,12},{12,4},... | collective-permute-start | bytes 1572872 | tf_op jit(solution)/shard_map/ppermute | solution.py:366
  53.0 1.0 copy-start.1
  54.1 1.0 copy-start.3
  60.9 6.9 %collective-permute-start.8 = (bf16[2,512,128]{2,1,0:T(8,128)(2,1)S(1)}, bf16[2,512,128]{2,1,0:T(8,128)(2,1)S(1)}, u32[]{:S(2)}, u32[]{:S(2)}) collective-permute-start(bf16[2,512,128]{2,1,0:T(8,128)(2,1)S(1)} %constant_dynamic-slice_fusion), channel_id=1, source_target_pairs={{0,16},{8,120},{16,32},{24,8},{32,48},{40,24},{48,64},{56,40},{64,... | collective-permute-start | bytes 786440 | tf_op jit(solution)/shard_map/ppermute | solution.py:363
  62.4 7.8 %collective-permute-start.7 = (bf16[4,512,128]{2,1,0:T(8,128)(2,1)S(1)}, bf16[4,512,128]{2,1,0:T(8,128)(2,1)S(1)}, u32[]{:S(2)}, u32[]{:S(2)}) collective-permute-start(bf16[4,512,128]{2,1,0:T(8,128)(2,1)S(1)} %collective-permute-done.6.refs_5_.refs_4_), channel_id=1, source_target_pairs={{0,8},{8,0},{1,9},{9,1},{2,10},{10,2},{3,11},{11,3},{4,12},{12,4},... | collective-permute-start | bytes 1572872 | tf_op jit(solution)/shard_map/ppermute | solution.py:366
  67.8 12.8 %copy-start.5 = (f32[4,136,512]{2,1,0:T(8,128)S(1)}, f32[4,136,512]{2,1,0:T(8,128)}, u32[]{:S(2)}) copy-start(f32[4,136,512]{2,1,0:T(8,128)} %copy-done.4) | copy-start | bytes 3342340
  67.8 2.4 %collective-permute-start.9 = (bf16[2,512,128]{2,1,0:T(8,128)(2,1)S(1)}, bf16[2,512,128]{2,1,0:T(8,128)(2,1)S(1)}, u32[]{:S(2)}, u32[]{:S(2)}) collective-permute-start(bf16[2,512,128]{2,1,0:T(8,128)(2,1)S(1)} %collective-permute-done.8.refs_7_.refs_6_), channel_id=1, source_target_pairs={{0,8},{8,0},{1,9},{9,1},{2,10},{10,2},{3,11},{11,3},{4,12},{12,4},... | collective-permute-start | bytes 786440 | tf_op jit(solution)/shard_map/ppermute | solution.py:366
  77.2 16.8 %collective-permute-start.10 = (bf16[4,144,512]{2,1,0:T(8,128)(2,1)S(1)}, bf16[4,144,512]{2,1,0:T(8,128)(2,1)S(1)}, u32[]{:S(2)}, u32[]{:S(2)}) collective-permute-start(bf16[4,144,512]{2,1,0:T(8,128)(2,1)S(1)} %attend.9), channel_id=1, source_target_pairs={{0,128},{128,0},{1,129},{129,1},{2,130},{130,2},{3,131},{131,3},{4... | collective-permute-start | bytes 1769480 | tf_op jit(solution)/shard_map/ppermute | solution.py:392

commit v3 on v2

v3 whole, which is shorter than its diff:
```python
import functools

import jax
import jax.numpy as jnp
import numpy as np
from jax import lax
from jax.experimental import pallas as pl
from jax.experimental.pallas import tpu as pltpu
from jax.sharding import Mesh
from jax.sharding import PartitionSpec as P

HEAD_DIM = 128
HALF = 128
ROWS = 2 * HALF
BLOCKS = 8
GROUP = 4
EXTENDED = HEAD_DIM + 8
PARTIAL = BLOCKS * HEAD_DIM
NEG = -1e30
LOG2E_SCALE = float(np.log2(np.e) / np.sqrt(HEAD_DIM))
AXES = ("yh", "z", "c", "yl", "x")
F32 = jnp.float32
BF16 = jnp.bfloat16
SMEM = pl.BlockSpec(memory_space=pltpu.SMEM)
VMEM = pl.BlockSpec(memory_space=pltpu.VMEM)
VMEM_BYTES = 16 * 2**20
SMALL = pltpu.CompilerParams(vmem_limit_bytes=8 * 2**20)


def nt(a, b):
    return lax.dot_general(a, b, (((1,), (0,)), ((), ())), preferred_element_type=F32)


def prepare_kernel(got_ref, q_ref, kv_ref):
    for b in range(BLOCKS):
        for h in range(2):
            q_ref[b, :, h * HALF : (h + 1) * HALF] = got_ref[
                b, :, h * HEAD_DIM : (h + 1) * HEAD_DIM
            ].T
        kv_ref[b, :HALF] = got_ref[b, :, 2 * HEAD_DIM : 3 * HEAD_DIM]
        kv_ref[b, HALF:] = got_ref[b, :, 3 * HEAD_DIM :].T


def prepare(got):
    return pl.pallas_call(
        prepare_kernel,
        out_shape=(
            jax.ShapeDtypeStruct((BLOCKS, HEAD_DIM, ROWS), BF16),
            jax.ShapeDtypeStruct((BLOCKS, 2 * HALF, HEAD_DIM), BF16),
        ),
        in_specs=[VMEM],
        out_specs=(VMEM, VMEM),
        compiler_params=SMALL,
        name="prepare",
    )(got)


def attend_kernel(steps, partner, starts, final, *refs):
    shards = len(steps)
    meta_ref, order_ref = refs[:2]
    q_refs, refs = (refs[2:4], refs[4:]) if partner else (refs[2:3], refs[3:])
    kv_refs = refs[:shards]
    rest = refs[shards:]
    if not starts:
        m_in, acc_in = rest[:2]
        rest = rest[2:]
    if final:
        out_ref, rest = rest[0], rest[1:]
    m_ref, acc_ref, kv_s = rest[:3]
    scores, maxima = rest[3:7], rest[7:11]
    item, slots, before, sorted_k = rest[11:15]
    if partner:
        q_ref = rest[15]
        split = q_refs[0].shape[0]
        q_ref[:split] = q_refs[0][...]
        q_ref[split:] = q_refs[1][...]
    else:
        q_ref = q_refs[0]

    total = BLOCKS * shards
    for n in range(shards):
        kv_s[n * BLOCKS : (n + 1) * BLOCKS] = kv_refs[n][...]
    kv_s[total] = jnp.zeros((2 * HALF, HEAD_DIM), BF16)

    yh, z, c = meta_ref[0], meta_ref[1], meta_ref[2]
    up = 2 * c - 1
    q_pos = [order_ref[((i // 4) * 8 + z) * 4 + i % 4] for i in range(BLOCKS)]
    k_pos = []
    for distance in steps:
        plane = (z + up * distance + 16) & 7
        k_pos += [order_ref[((b // 4) * 8 + plane) * 4 + b % 4] for b in range(BLOCKS)]

    for p in range(64):
        slots[p] = -1
    for t in range(total):
        slots[k_pos[t]] = t
    count = 0
    for p in range(64):
        found = slots[p]
        sorted_k[count] = found
        before[p] = count
        count = count + jnp.where(found >= 0, 1, 0)

    items = 0
    code = 0
    for i in range(BLOCKS):
        n_seen = before[q_pos[i]]
        mine = (i << 16) | (n_seen << 8)
        for n in range((total + GROUP - 1) // GROUP):
            item[items + n] = mine | (GROUP * n)
        code = jnp.where(n_seen > 0, mine | n_seen, code)
        items = items + ((n_seen + GROUP - 1) >> 2)
    for n in range(5):
        item[items + n] = code

    if starts:
        key_at = lax.broadcasted_iota(jnp.int32, (HALF, ROWS), 0)
        row_at = lax.broadcasted_iota(jnp.int32, (HALF, ROWS), 1) & (HALF - 1)
        key_side, row_side = yh, 1 - yh if partner else yh
        key_at = (key_at >> 5) * 64 + key_side * 32 + (key_at & 31)
        row_at = (row_at >> 5) * 64 + row_side * 32 + (row_at & 31)
        seen = key_at <= row_at
        ones = jnp.ones((16, HALF), BF16)
        for i in range(BLOCKS):
            s = jnp.where(seen, nt(kv_s[i, :HALF], q_ref[i]) * LOG2E_SCALE, NEG)
            top = jnp.max(s, axis=0, keepdims=True)
            p = jnp.where(seen, jnp.exp2(s - top), 0.0).astype(BF16)
            m_ref[i] = top
            acc_ref[i] = nt(jnp.concatenate([kv_s[i, HALF:], ones], axis=0), p)[:EXTENDED]
    else:
        m_ref[...] = m_in[...]
        acc_ref[...] = acc_in[...]

    def places(j):
        code = item[j]
        seen_count, base = (code >> 8) & 255, code & 255
        at = [base + g for g in range(GROUP)]
        blocks = [sorted_k[jnp.maximum(jnp.minimum(n, seen_count - 1), 0)] for n in at]
        return code >> 16, blocks, [n < seen_count for n in at]

    def score(j, scores, maxima):
        i, blocks, _ = places(j)
        keys = jnp.concatenate([kv_s[t, :HALF] for t in blocks], axis=0)
        s = nt(keys, q_ref[i]) * LOG2E_SCALE
        scores[...] = s
        maxima[...] = jnp.max(s, axis=0, keepdims=True)

    def absorb(j, scores, maxima):
        i, blocks, counts = places(j)
        values = [kv_s[jnp.where(ok, t, total), HALF:] for t, ok in zip(blocks, counts)]
        ones = [jnp.full((16, HALF), jnp.where(ok, 1.0, 0.0), F32).astype(BF16) for ok in counts]
        lhs = jnp.concatenate([jnp.concatenate(values, axis=1), jnp.concatenate(ones, axis=1)], axis=0)
        old = m_ref[i]
        new = jnp.maximum(old, maxima[...])
        keep = jnp.exp2(old - new)
        m_ref[i] = new
        p = jnp.exp2(scores[...] - new).astype(BF16)
        acc_ref[i] = acc_ref[i] * keep + nt(lhs, p)[:EXTENDED]

    def several(at_once, first):
        def turn(h, carry):
            j = first + at_once * h
            for n in range(at_once):
                score(j + n + 2, scores[(n + 2) % 4], maxima[(n + 2) % 4])
                absorb(j + n, scores[n % 4], maxima[n % 4])
            return carry

        return turn

    for n in range(2):
        score(n, scores[n], maxima[n])
    many = items >> 3
    lax.fori_loop(0, many, several(8, 0), 0)
    lax.fori_loop(0, (items - 8 * many + 3) >> 2, several(4, 8 * many), 0)

    if final:
        sub = lax.broadcasted_iota(jnp.int32, (32, ROWS), 0)
        tail = jnp.zeros((32, ROWS), F32)
        for i in range(BLOCKS):
            sums = acc_ref[i, HEAD_DIM : HEAD_DIM + 1]
            some = sums > 0.0
            safe = jnp.where(some, sums, 1.0)
            logs = jnp.where(some, m_ref[i] + jnp.log2(safe), NEG)
            high = logs.astype(BF16).astype(F32)
            middle = (logs - high).astype(BF16).astype(F32)
            low = logs - high - middle
            out_ref[i * HEAD_DIM : (i + 1) * HEAD_DIM] = (
                acc_ref[i, :HEAD_DIM] * (1.0 / safe)
            ).astype(BF16)
            for n, part in enumerate((high, middle, low)):
                tail = jnp.where(sub == BLOCKS * n + i, part, tail)
        out_ref[PARTIAL:] = tail.astype(BF16)


def attend(meta, order, q, shards, state, partner, final=False):
    steps = tuple(distance for _, distance in shards)
    total = BLOCKS * len(steps)
    starts = state is None
    args = [meta, order] + list(q) + [a for a, _ in shards] + ([] if starts else list(state))
    m_shape, acc_shape = (BLOCKS, 1, ROWS), (BLOCKS, EXTENDED, ROWS)
    if final:
        out_shape = (jax.ShapeDtypeStruct((PARTIAL + 32, ROWS), BF16),)
        work = [pltpu.VMEM(m_shape, F32), pltpu.VMEM(acc_shape, F32)]
    else:
        out_shape = (jax.ShapeDtypeStruct(m_shape, F32), jax.ShapeDtypeStruct(acc_shape, F32))
        work = []
    pairs = BLOCKS * total // 2
    items = BLOCKS * ((total + GROUP - 1) // GROUP) + 8
    got = pl.pallas_call(
        functools.partial(attend_kernel, steps, partner, starts, final),
        out_shape=out_shape,
        in_specs=[SMEM, SMEM] + [VMEM] * (len(args) - 2),
        out_specs=tuple(VMEM for _ in out_shape),
        scratch_shapes=work
        + [
            pltpu.VMEM((total + 1, 2 * HALF, HEAD_DIM), BF16),
        ]
        + [pltpu.VMEM((GROUP * HALF, ROWS), F32)] * 4
        + [pltpu.VMEM((1, ROWS), F32)] * 4
        + [
            pltpu.SMEM((items,), jnp.int32),
            pltpu.SMEM((64,), jnp.int32),
            pltpu.SMEM((64,), jnp.int32),
            pltpu.SMEM((total + 1,), jnp.int32),
        ]
        + ([pltpu.VMEM((BLOCKS, HEAD_DIM, ROWS), BF16)] if partner else []),
        compiler_params=pltpu.CompilerParams(vmem_limit_bytes=VMEM_BYTES),
        cost_estimate=pl.CostEstimate(
            flops=pairs * 4 * HALF * ROWS * 8, bytes_accessed=1 << 18, transcendentals=pairs * 1024
        ),
        name="attend",
    )(*args)
    return got[0] if final else got


def combine_kernel(m_ref, acc_ref, other_ref, out_ref):
    tail = other_ref[PARTIAL:].astype(F32)
    logs = tail[:BLOCKS] + tail[BLOCKS : 2 * BLOCKS] + tail[2 * BLOCKS : 3 * BLOCKS]
    for i in range(BLOCKS):
        sums = acc_ref[i, HEAD_DIM : HEAD_DIM + 1]
        mine = m_ref[i] + jnp.log2(sums)
        theirs = logs[i : i + 1]
        top = jnp.maximum(mine, theirs)
        weight_mine, weight_theirs = jnp.exp2(mine - top), jnp.exp2(theirs - top)
        whole = weight_mine + weight_theirs
        result = acc_ref[i, :HEAD_DIM] * (weight_mine / (sums * whole)) + other_ref[
            i * HEAD_DIM : (i + 1) * HEAD_DIM
        ].astype(F32) * (weight_theirs / whole)
        result = result.astype(BF16)
        for h in range(2):
            out_ref[i, :, h * HEAD_DIM : (h + 1) * HEAD_DIM] = result[
                :, h * HALF : (h + 1) * HALF
            ].T


def combine(state, other):
    return pl.pallas_call(
        combine_kernel,
        out_shape=jax.ShapeDtypeStruct((BLOCKS, HALF, 2 * HEAD_DIM), BF16),
        in_specs=[VMEM] * 3,
        out_specs=VMEM,
        compiler_params=SMALL,
        name="combine",
    )(*state, other)


def pack_kernel(queries_in, keys_in, values_in, out_ref, queries_ref, keys_ref, values_ref, sems):
    pairs = ((queries_in, queries_ref), (keys_in, keys_ref), (values_in, values_ref))
    copies = [pltpu.make_async_copy(a, b, sems.at[n]) for n, (a, b) in enumerate(pairs)]
    for copy in copies:
        copy.start()
    for copy in copies:
        copy.wait()
    rows = out_ref.shape[1]
    for side in range(2):
        part = slice(side * rows, (side + 1) * rows)
        for g in range(8):
            keys = keys_ref[part, g * HEAD_DIM : (g + 1) * HEAD_DIM]
            values = values_ref[part, g * HEAD_DIM : (g + 1) * HEAD_DIM]
            for c in range(2):
                first = (2 * g + c) * 2 * HEAD_DIM
                at = 16 * side + 8 * c + g
                out_ref[at, :, : 2 * HEAD_DIM] = queries_ref[part, first : first + 2 * HEAD_DIM]
                out_ref[at, :, 2 * HEAD_DIM : 3 * HEAD_DIM] = keys
                out_ref[at, :, 3 * HEAD_DIM :] = values


def pack(queries, keys, values):
    rows = queries.shape[0]
    return pl.pallas_call(
        pack_kernel,
        out_shape=jax.ShapeDtypeStruct((32, rows // 2, 4 * HEAD_DIM), BF16),
        in_specs=[pl.BlockSpec(memory_space=pl.ANY)] * 3,
        out_specs=VMEM,
        scratch_shapes=[pltpu.VMEM(a.shape, BF16) for a in (queries, keys, values)]
        + [pltpu.SemaphoreType.DMA((3,))],
        compiler_params=pltpu.CompilerParams(vmem_limit_bytes=56 * 2**20),
        name="pack",
    )(queries, keys, values)


def unpack_kernel(back_ref, out_ref):
    rows = back_ref.shape[1]
    for side in range(2):
        for g in range(8):
            for c in range(2):
                first = (2 * g + c) * 2 * HEAD_DIM
                out_ref[side * rows : (side + 1) * rows, first : first + 2 * HEAD_DIM] = back_ref[
                    16 * side + 8 * c + g
                ]


def unpack(back):
    rows = 2 * back.shape[1]
    return pl.pallas_call(
        unpack_kernel,
        out_shape=jax.ShapeDtypeStruct((rows, 32 * HEAD_DIM), BF16),
        in_specs=[VMEM],
        out_specs=VMEM,
        compiler_params=SMALL,
        name="unpack",
    )(back)


def body(queries, keys, values, block_order):
    rows = queries.shape[0]
    group = ("yh", "c", "yl", "x")
    z_size = lax.axis_size("z")
    meta = jnp.stack([lax.axis_index("yh"), lax.axis_index("z"), lax.axis_index("c")]).astype(jnp.int32)
    got = lax.all_to_all(pack(queries, keys, values), group, 0, 0, tiled=True)
    q, kv = prepare(got.reshape(BLOCKS, HALF, 512))

    ring = [(2 * i + k, 2 * ((i + 1 - 2 * k) % z_size) + k) for i in range(z_size) for k in (0, 1)]
    swap = [(0, 1), (1, 0)]

    def onward(a):
        return lax.ppermute(a, ("z", "c"), ring)

    def swapped(a):
        return lax.ppermute(a, "c", swap)

    r1 = onward(kv)
    other_a = lax.ppermute(q[:5], "yh", swap)
    mine = attend(meta, block_order, (q,), [(kv, 0)], None, False)
    r1, mine, other_a, q = lax.optimization_barrier((r1, mine, other_a, q))

    r2, s1 = onward(r1), swapped(r1)
    other_q = (other_a, lax.ppermute(q[5:], "yh", swap))
    near = [(r1, 1), (s1, -1)]
    r2, other_q = lax.optimization_barrier((r2, other_q))

    r3, s2 = onward(r2), swapped(r2)
    theirs = attend(meta, block_order, other_q, [(kv, 0)] + near, None, True)
    r3, theirs = lax.optimization_barrier((r3, theirs))

    r4, s3 = onward(r3), swapped(r3)
    later = [(r2, 2), (s2, -2), (r3, 3), (s3, -3)]
    theirs = attend(meta, block_order, other_q, later, theirs, True)
    r4, theirs = lax.optimization_barrier((r4, theirs))

    last = [(r4, 4)]
    sent = attend(meta, block_order, other_q, last, theirs, True, True)
    other = lax.ppermute(sent, "yh", swap)
    mine = attend(meta, block_order, (q,), near + later + last, mine, False)
    result = combine(mine, other).reshape(32, rows // 2, 256)
    return unpack(lax.all_to_all(result, group, 0, 0, tiled=True))


def solution(mesh):
    fine = Mesh(mesh.devices.reshape(2, 8, 2, 2, 4), AXES)
    spec = P(AXES, None)
    return jax.shard_map(
        body, mesh=fine, in_specs=(spec, spec, spec, P()), out_specs=spec, check_vma=False
    )
```

time: 108 us -> 109 us (level); the launches traced: 109 us -> 107 us
  waiting for transfers between devices: 4.05 us -> 15.1 us
  Pallas kernels: 37.8 us -> 30.9 us
  blocking collectives: 36.9 us -> 43.4 us
  starting transfers between devices: 24.1 us -> 17.8 us
  local copies, waits for them, and re-layouts: 6.02 us -> 0.04 us
    ppermute x2, waiting for transfers between devices: 0.01 us -> 9.65 us  [the longest x1 5.91 us: body(): other_q = (other_a, lax.ppermute(q[5:], 'yh', swap))]
    unnamed x20 -> x2, local copies, waits for them, and re-layouts: 5.96 us -> 0.01 us
    pallas_call x5, Pallas kernels: 32 us -> 27.3 us  [attend(): pl.pallas_call(functools.partial(attend_kernel, steps, partner, starts, f...]
    ppermute x2, starting transfers between devices: 5.41 us -> 0.81 us  [the longest x1 0.63 us: body(): other_a = lax.ppermute(q[:5], 'yh', swap)]
    all_to_all x1, blocking collectives: 14 us -> 17.5 us  [body(): return unpack(lax.all_to_all(result, group, 0, 0, tiled=True))]
    all_to_all x1, blocking collectives: 22.9 us -> 25.9 us  [body(): got = lax.all_to_all(pack(queries, keys, values), group, 0, 0, tiled=True)]
    ppermute x1, starting transfers between devices: 3.44 us -> 0.98 us  [body(): other = lax.ppermute(sent, 'yh', swap)]
    pallas_call x3 -> x2, Pallas kernels: 4.71 us -> 2.52 us  [the longest x1 2.21 us: pack(): pl.pallas_call(pack_kernel, out_shape=jax.ShapeDtypeStruct((32, rows // 2...]
  transfers between devices with their start and end apart: 11 -> 10, of which waited for: 2 -> 6; matrix products, arithmetic and copies ran while one was open for 0% -> 0% of each run, Pallas kernels for 27% -> 23%
where the time goes in v3:
time: 109 us; the launch traced here: 107 us
  blocking collectives  43.4 us (40%)
  Pallas kernels  30.9 us (28%)
  starting transfers between devices  17.8 us (16%)
  waiting for transfers between devices  15.1 us (14%)
    pallas_call x5, Pallas kernels, attend(): pl.pallas_call(functools.partial(attend_kernel, steps, partner, starts, f...  27.3 us
    all_to_all x1, blocking collectives, body(): got = lax.all_to_all(pack(queries, keys, values), group, 0, 0, tiled=True)  25.9 us
    all_to_all x1, blocking collectives, body(): return unpack(lax.all_to_all(result, group, 0, 0, tiled=True))  17.5 us
    ppermute x4, starting transfers between devices, onward(): return lax.ppermute(a, ('z', 'c'), ring)  13.1 us
    ppermute x1, waiting for transfers between devices, body(): other_q = (other_a, lax.ppermute(q[5:], 'yh', swap))  5.91 us
    ppermute x1, waiting for transfers between devices, body(): other_a = lax.ppermute(q[:5], 'yh', swap)  3.74 us
    ppermute x1, waiting for transfers between devices, body(): other = lax.ppermute(sent, 'yh', swap)  3.29 us
    ppermute x3, starting transfers between devices, swapped(): return lax.ppermute(a, 'c', swap)  2.88 us
  transfers between devices with their start and end apart: 10, of which 6 were waited for; matrix products, arithmetic and copies ran while one was open for 0% of the time, Pallas kernels for 23%

profile of v3, /device:TPU:1, one launch (start us, length us, event | category | flops | bytes accessed | tf_op | source)
XLA Modules:
  0.0 107.3 jit_solution(6521730418809628507)
XLA Ops:
  0.0 2.2 %pack.1 = bf16[32,32,512]{2,1,0:T(8,128)(2,1)} custom-call(bf16[64,4096]{1,0:T(8,128)(2,1)} %queries_in.1, bf16[64,1024]{1,0:T(8,128)(2,1)} %keys_in.1, bf16[64,1024]{1,0:T(8,128)(2,1)} %values_in.1), custom_call_target="tpu_custom_call" | custom-call | tf_op jit(solution)/shard_map/pack/pallas_call | solution.py:290
  2.2 25.9 %all_to_all.10 = bf16[32,32,512]{2,1,0:T(8,128)(2,1)S(1)} all-to-all(bf16[32,32,512]{2,1,0:T(8,128)(2,1)} %pack.1), channel_id=1, replica_groups=mesh['yh'=2,'z'=8,'c'=2,'yl'=2,'x'=4] {'yh','c','yl','x'}, dimensions={0} | all-to-all | bytes 2097152 | tf_op jit(solution)/shard_map/all_to_all | solution.py:330
  28.1 0.0 copy-start
  28.1 0.3 prepare.1
  28.4 5.7 %collective-permute-start = (bf16[8,256,128]{2,1,0:T(8,128)(2,1)S(1)}, bf16[8,256,128]{2,1,0:T(8,128)(2,1)S(1)}, u32[]{:S(2)}, u32[]{:S(2)}) collective-permute-start(bf16[8,256,128]{2,1,0:T(8,128)(2,1)S(1)} %get-tuple-element.29.refs_3_.refs_4_), channel_id=1, source_target_pairs={{0,16},{8,120},{16,32},{24,8},{32,48},{40,24},{48,64},{56,40},{64,... | collective-permute-start | bytes 1572872 | tf_op jit(solution)/shard_map/ppermute | solution.py:337
  34.1 0.6 collective-permute-start.1
  34.7 0.1 pad_add_fusion.refs_0_
  34.8 0.0 copy-done
  34.8 3.4 %attend.5 = (f32[8,1,256]{2,1,0:T(1,128)S(1)}, f32[8,136,256]{2,1,0:T(8,128)S(1)}) custom-call(s32[3]{0:T(128)S(1)} %pad_add_fusion.refs_0_, s32[64]{0:T(128)S(1)} %copy-done, bf16[8,128,256]{2,1,0:T(8,128)(2,1)S(1)} %get-tuple-element.33.refs_2_, bf16[8,256,128]{2,1,0:T(8,128)(2,1)S(1)} %get-tuple-element.29.refs_3_.refs_4_), custom_call_target="tpu_custom_call" | custom-call | flops 33554432 | bytes 262144 | tf_op jit(solution)/shard_map/attend/pallas_call | solution.py:209
  38.2 3.7 %collective-permute-done.1.refs_2_ = bf16[5,128,256]{2,1,0:T(8,128)(2,1)S(1)} collective-permute-done((bf16[5,128,256]{2,1,0:T(8,128)(2,1)S(1)}, bf16[5,128,256]{2,1,0:T(8,128)(2,1)S(1)}, u32[]{:S(2)}, u32[]{:S(2)}) %collective-permute-start.1) | collective-permute-done | bytes 327712 | tf_op jit(solution)/shard_map/ppermute | solution.py:343
  42.0 0.0 collective-permute-done.refs_5_.refs_3_
  42.0 3.8 %collective-permute-start.3 = (bf16[8,256,128]{2,1,0:T(8,128)(2,1)S(1)}, bf16[8,256,128]{2,1,0:T(8,128)(2,1)S(1)}, u32[]{:S(2)}, u32[]{:S(2)}) collective-permute-start(bf16[8,256,128]{2,1,0:T(8,128)(2,1)S(1)} %collective-permute-done.refs_5_.refs_3_), channel_id=1, source_target_pairs={{0,16},{8,120},{16,32},{24,8},{32,48},{40,24},{48,64},{56,40},{64,... | collective-permute-start | bytes 1572872 | tf_op jit(solution)/shard_map/ppermute | solution.py:337
  45.8 0.2 collective-permute-start.4
  46.0 0.0 collective-permute-start.2
  46.0 5.9 %collective-permute-done.4.refs_3_ = bf16[3,128,256]{2,1,0:T(8,128)(2,1)S(1)} collective-permute-done((bf16[3,128,256]{2,1,0:T(8,128)(2,1)S(1)}, bf16[3,128,256]{2,1,0:T(8,128)(2,1)S(1)}, u32[]{:S(2)}, u32[]{:S(2)}) %collective-permute-start.4) | collective-permute-done | bytes 196640 | tf_op jit(solution)/shard_map/ppermute | solution.py:348
  51.9 0.0 collective-permute-done.3.refs_4_.refs_5_
  51.9 3.1 %collective-permute-start.6 = (bf16[8,256,128]{2,1,0:T(8,128)(2,1)S(1)}, bf16[8,256,128]{2,1,0:T(8,128)(2,1)S(1)}, u32[]{:S(2)}, u32[]{:S(2)}) collective-permute-start(bf16[8,256,128]{2,1,0:T(8,128)(2,1)S(1)} %collective-permute-done.3.refs_4_.refs_5_), channel_id=1, source_target_pairs={{0,16},{8,120},{16,32},{24,8},{32,48},{40,24},{48,64},{56,40},{64,... | collective-permute-start | bytes 1572872 | tf_op jit(solution)/shard_map/ppermute | solution.py:337
  55.0 0.0 collective-permute-start.5
  55.0 0.0 collective-permute-done.2.refs_6_.refs_4_
  55.0 6.1 %attend.6 = (f32[8,1,256]{2,1,0:T(1,128)S(1)}, f32[8,136,256]{2,1,0:T(8,128)S(1)}) custom-call(s32[3]{0:T(128)S(1)} %pad_add_fusion.refs_0_, s32[64]{0:T(128)S(1)} %copy-done, bf16[5,128,256]{2,1,0:T(8,128)(2,1)S(1)} %collective-permute-done.1.refs_2_, bf16[3,128,256]{2,1,0:T(8,128)(2,1)S(1)} %collective-permute-done.4.refs_3_, ...), custom_call_target="tpu_custom_call" | custom-call | flops 100663296 | bytes 262144 | tf_op jit(solution)/shard_map/attend/pallas_call | solution.py:209
  61.1 0.1 collective-permute-done.6.refs_6_.refs_7_
  61.1 2.9 %collective-permute-start.7 = (bf16[8,256,128]{2,1,0:T(8,128)(2,1)S(1)}, bf16[8,256,128]{2,1,0:T(8,128)(2,1)S(1)}, u32[]{:S(2)}, u32[]{:S(2)}) collective-permute-start(bf16[8,256,128]{2,1,0:T(8,128)(2,1)S(1)} %collective-permute-done.6.refs_6_.refs_7_), channel_id=1, source_target_pairs={{0,8},{8,0},{1,9},{9,1},{2,10},{10,2},{3,11},{11,3},{4,12},{12,4},... | collective-permute-start | bytes 1572872 | tf_op jit(solution)/shard_map/ppermute | solution.py:340
  64.0 0.5 collective-permute-start.8
  64.5 0.0 collective-permute-done.5.refs_5_.refs_6_
  64.5 1.0 collective-permute-done.7.refs_7_.refs_8_
  65.5 5.7 %attend.7 = (f32[8,1,256]{2,1,0:T(1,128)S(1)}, f32[8,136,256]{2,1,0:T(8,128)S(1)}) custom-call(s32[3]{0:T(128)S(1)} %pad_add_fusion.refs_0_, s32[64]{0:T(128)S(1)} %copy-done, bf16[5,128,256]{2,1,0:T(8,128)(2,1)S(1)} %collective-permute-done.1.refs_2_, bf16[3,128,256]{2,1,0:T(8,128)(2,1)S(1)} %collective-permute-done.4.refs_3_, ...), custom_call_target="tpu_custom_call" | custom-call | flops 134217728 | bytes 262144 | tf_op jit(solution)/shard_map/attend/pallas_call | solution.py:209
  71.2 1.1 %collective-permute-done.8.refs_9_.refs_4_ = bf16[8,256,128]{2,1,0:T(8,128)(2,1)S(1)} collective-permute-done((bf16[8,256,128]{2,1,0:T(8,128)(2,1)S(1)}, bf16[8,256,128]{2,1,0:T(8,128)(2,1)S(1)}, u32[]{:S(2)}, u32[]{:S(2)}) %collective-permute-start.8) | collective-permute-done | bytes 524320 | tf_op jit(solution)/shard_map/ppermute | solution.py:337
  72.3 3.1 %attend.9 = bf16[1056,256]{1,0:T(8,128)(2,1)S(1)} custom-call(s32[3]{0:T(128)S(1)} %pad_add_fusion.refs_0_, s32[64]{0:T(128)S(1)} %copy-done, bf16[5,128,256]{2,1,0:T(8,128)(2,1)S(1)} %collective-permute-done.1.refs_2_, bf16[3,128,256]{2,1,0:T(8,128)(2,1)S(1)} %collective-permute-done.4.refs_3_, ...), custom_call_target="tpu_custom_call" | custom-call | flops 33554432 | bytes 262144 | tf_op jit(solution)/shard_map/attend/pallas_call | solution.py:209
  75.5 1.0 collective-permute-start.9
  76.4 9.0 %attend.8 = (f32[8,1,256]{2,1,0:T(1,128)S(1)}, f32[8,136,256]{2,1,0:T(8,128)S(1)}) custom-call(s32[3]{0:T(128)S(1)} %pad_add_fusion.refs_0_, s32[64]{0:T(128)S(1)} %copy-done, bf16[8,128,256]{2,1,0:T(8,128)(2,1)S(1)} %get-tuple-element.33.refs_2_, bf16[8,256,128]{2,1,0:T(8,128)(2,1)S(1)} %collective-permute-done.refs_5_.refs_3_, ...), custom_call_target="tpu_custom_call" | custom-call | flops 234881024 | bytes 262144 | tf_op jit(solution)/shard_map/attend/pallas_call | solution.py:209
  85.5 3.3 %collective-permute-done.9.other_ref = bf16[1056,256]{1,0:T(8,128)(2,1)S(1)} collective-permute-done((bf16[1056,256]{1,0:T(8,128)(2,1)S(1)}, bf16[1056,256]{1,0:T(8,128)(2,1)S(1)}, u32[]{:S(2)}, u32[]{:S(2)}) %collective-permute-start.9) | collective-permute-done | bytes 540704 | tf_op jit(solution)/shard_map/ppermute | solution.py:363
  88.7 0.3 combine.1
  89.1 17.5 %all_to_all.11.back_ref = bf16[32,32,256]{2,1,0:T(8,128)(2,1)S(1)} all-to-all(bf16[32,32,256]{2,1,0:T(8,128)(2,1)S(1)} %bitcast.6), channel_id=1, replica_groups=mesh['yh'=2,'z'=8,'c'=2,'yl'=2,'x'=4] {'yh','c','yl','x'}, dimensions={0} | all-to-all | bytes 1048576 | tf_op jit(solution)/shard_map/all_to_all | solution.py:366
  106.5 0.8 unpack.1
  (2 shorter events, 0.0 us)
Async XLA Ops:
  28.1 6.7 %copy-start = (s32[64]{0:T(128)S(1)}, s32[64]{0:T(128)}, u32[]{:S(2)}) copy-start(s32[64]{0:T(128)} %refs_1_.9) | copy-start | bytes 772
  28.4 13.6 %collective-permute-start = (bf16[8,256,128]{2,1,0:T(8,128)(2,1)S(1)}, bf16[8,256,128]{2,1,0:T(8,128)(2,1)S(1)}, u32[]{:S(2)}, u32[]{:S(2)}) collective-permute-start(bf16[8,256,128]{2,1,0:T(8,128)(2,1)S(1)} %get-tuple-element.29.refs_3_.refs_4_), channel_id=1, source_target_pairs={{0,16},{8,120},{16,32},{24,8},{32,48},{40,24},{48,64},{56,40},{64,... | collective-permute-start | bytes 1572872 | tf_op jit(solution)/shard_map/ppermute | solution.py:337
  34.1 7.9 %collective-permute-start.1 = (bf16[5,128,256]{2,1,0:T(8,128)(2,1)S(1)}, bf16[5,128,256]{2,1,0:T(8,128)(2,1)S(1)}, u32[]{:S(2)}, u32[]{:S(2)}) collective-permute-start(bf16[5,128,256]{2,1,0:T(8,128)(2,1)S(1)} %slice.6), channel_id=1, source_target_pairs={{0,128},{128,0},{1,129},{129,1},{2,130},{130,2},{3,131},{131,3},{4... | collective-permute-start | bytes 983048 | tf_op jit(solution)/shard_map/ppermute | solution.py:343
  42.0 9.9 %collective-permute-start.3 = (bf16[8,256,128]{2,1,0:T(8,128)(2,1)S(1)}, bf16[8,256,128]{2,1,0:T(8,128)(2,1)S(1)}, u32[]{:S(2)}, u32[]{:S(2)}) collective-permute-start(bf16[8,256,128]{2,1,0:T(8,128)(2,1)S(1)} %collective-permute-done.refs_5_.refs_3_), channel_id=1, source_target_pairs={{0,16},{8,120},{16,32},{24,8},{32,48},{40,24},{48,64},{56,40},{64,... | collective-permute-start | bytes 1572872 | tf_op jit(solution)/shard_map/ppermute | solution.py:337
  45.8 6.1 %collective-permute-start.4 = (bf16[3,128,256]{2,1,0:T(8,128)(2,1)S(1)}, bf16[3,128,256]{2,1,0:T(8,128)(2,1)S(1)}, u32[]{:S(2)}, u32[]{:S(2)}) collective-permute-start(bf16[3,128,256]{2,1,0:T(8,128)(2,1)S(1)} %slice.7), channel_id=1, source_target_pairs={{0,128},{128,0},{1,129},{129,1},{2,130},{130,2},{3,131},{131,3},{4... | collective-permute-start | bytes 589832 | tf_op jit(solution)/shard_map/ppermute | solution.py:348
  46.0 9.1 %collective-permute-start.2 = (bf16[8,256,128]{2,1,0:T(8,128)(2,1)S(1)}, bf16[8,256,128]{2,1,0:T(8,128)(2,1)S(1)}, u32[]{:S(2)}, u32[]{:S(2)}) collective-permute-start(bf16[8,256,128]{2,1,0:T(8,128)(2,1)S(1)} %collective-permute-done.refs_5_.refs_3_), channel_id=1, source_target_pairs={{0,8},{8,0},{1,9},{9,1},{2,10},{10,2},{3,11},{11,3},{4,12},{12,4},... | collective-permute-start | bytes 1572872 | tf_op jit(solution)/shard_map/ppermute | solution.py:340
  51.9 9.2 %collective-permute-start.6 = (bf16[8,256,128]{2,1,0:T(8,128)(2,1)S(1)}, bf16[8,256,128]{2,1,0:T(8,128)(2,1)S(1)}, u32[]{:S(2)}, u32[]{:S(2)}) collective-permute-start(bf16[8,256,128]{2,1,0:T(8,128)(2,1)S(1)} %collective-permute-done.3.refs_4_.refs_5_), channel_id=1, source_target_pairs={{0,16},{8,120},{16,32},{24,8},{32,48},{40,24},{48,64},{56,40},{64,... | collective-permute-start | bytes 1572872 | tf_op jit(solution)/shard_map/ppermute | solution.py:337
  55.0 9.5 %collective-permute-start.5 = (bf16[8,256,128]{2,1,0:T(8,128)(2,1)S(1)}, bf16[8,256,128]{2,1,0:T(8,128)(2,1)S(1)}, u32[]{:S(2)}, u32[]{:S(2)}) collective-permute-start(bf16[8,256,128]{2,1,0:T(8,128)(2,1)S(1)} %collective-permute-done.3.refs_4_.refs_5_), channel_id=1, source_target_pairs={{0,8},{8,0},{1,9},{9,1},{2,10},{10,2},{3,11},{11,3},{4,12},{12,4},... | collective-permute-start | bytes 1572872 | tf_op jit(solution)/shard_map/ppermute | solution.py:340
  61.1 4.4 %collective-permute-start.7 = (bf16[8,256,128]{2,1,0:T(8,128)(2,1)S(1)}, bf16[8,256,128]{2,1,0:T(8,128)(2,1)S(1)}, u32[]{:S(2)}, u32[]{:S(2)}) collective-permute-start(bf16[8,256,128]{2,1,0:T(8,128)(2,1)S(1)} %collective-permute-done.6.refs_6_.refs_7_), channel_id=1, source_target_pairs={{0,8},{8,0},{1,9},{9,1},{2,10},{10,2},{3,11},{11,3},{4,12},{12,4},... | collective-permute-start | bytes 1572872 | tf_op jit(solution)/shard_map/ppermute | solution.py:340
  64.0 8.3 %collective-permute-start.8 = (bf16[8,256,128]{2,1,0:T(8,128)(2,1)S(1)}, bf16[8,256,128]{2,1,0:T(8,128)(2,1)S(1)}, u32[]{:S(2)}, u32[]{:S(2)}) collective-permute-start(bf16[8,256,128]{2,1,0:T(8,128)(2,1)S(1)} %collective-permute-done.6.refs_6_.refs_7_), channel_id=1, source_target_pairs={{0,16},{8,120},{16,32},{24,8},{32,48},{40,24},{48,64},{56,40},{64,... | collective-permute-start | bytes 1572872 | tf_op jit(solution)/shard_map/ppermute | solution.py:337
  75.5 13.3 %collective-permute-start.9 = (bf16[1056,256]{1,0:T(8,128)(2,1)S(1)}, bf16[1056,256]{1,0:T(8,128)(2,1)S(1)}, u32[]{:S(2)}, u32[]{:S(2)}) collective-permute-start(bf16[1056,256]{1,0:T(8,128)(2,1)S(1)} %attend.9), channel_id=1, source_target_pairs={{0,128},{128,0},{1,129},{129,1},{2,130},{130,2},{3,131},{131,3},{4... | collective-permute-start | bytes 1622024 | tf_op jit(solution)/shard_map/ppermute | solution.py:363

commit v4 on v2

--- a/solution.py
+++ b/solution.py
@@ -14,7 +14,8 @@
 ROWS = 2 * BLOCK
 BLOCKS = 4
 EXTENDED = HEAD_DIM + 8
-PARTIAL = HEAD_DIM + 16
+GROUP = 2
+PARTIAL = BLOCKS * HEAD_DIM
 NEG = -1e30
 LOG2E_SCALE = float(np.log2(np.e) / np.sqrt(HEAD_DIM))
 AXES = ("yh", "z", "c", "yl", "x")
@@ -102,93 +103,90 @@
 
 
 def attend_kernel(steps, partner, starts, final, *refs):
-    count = len(steps)
+    shards = len(steps)
     meta_ref, order_ref = refs[:2]
     q_refs, refs = (refs[2:4], refs[4:]) if partner else (refs[2:3], refs[3:])
-    kv_refs = refs[:count]
-    rest = refs[count:]
+    kv_refs = refs[:shards]
+    rest = refs[shards:]
     if not starts:
         m_in, acc_in = rest[:2]
         rest = rest[2:]
     if final:
         out_ref, rest = rest[0], rest[1:]
     m_ref, acc_ref, kv_s, scores_a, scores_b, max_a, max_b = rest[:7]
-    item_q, item_k, item_v, item_f = rest[7:11]
+    item, slots, before, sorted_k = rest[7:11]
     if partner:
         q_ref = rest[11]
-        for n in range(2):
-            q_ref[2 * n : 2 * n + 2] = q_refs[n][...]
+        split = q_refs[0].shape[0]
+        q_ref[:split] = q_refs[0][...]
+        q_ref[split:] = q_refs[1][...]
     else:
         q_ref = q_refs[0]
 
-    total = sum(size for size, _, _ in steps)
+    total = BLOCKS * shards
+    for n in range(shards):
+        kv_s[n * BLOCKS : (n + 1) * BLOCKS] = kv_refs[n][...]
+    kv_s[total] = jnp.zeros((2 * BLOCK, HEAD_DIM), BF16)
     if starts:
         m_ref[...] = jnp.full(m_ref.shape, NEG, F32)
         acc_ref[...] = jnp.zeros(acc_ref.shape, F32)
     else:
         m_ref[...] = m_in[...]
         acc_ref[...] = acc_in[...]
-    at = 0
-    for n, (size, _, _) in enumerate(steps):
-        kv_s[at : at + size] = kv_refs[n][...]
-        at += size
-    kv_s[total] = jnp.zeros((2 * BLOCK, HEAD_DIM), BF16)
 
     yh, z, c = meta_ref[0], meta_ref[1], meta_ref[2]
     up = 2 * c - 1
-    q_first = ((1 - yh if partner else yh) * 8 + z) * BLOCKS
+    q_side = 1 - yh if partner else yh
+    q_pos = [order_ref[(q_side * 8 + z) * BLOCKS + i] for i in range(BLOCKS)]
     k_pos = []
-    for size, distance, half in steps:
+    for distance in steps:
         plane = (z + up * distance + 16) & 7
-        base = (yh * 8 + plane) * BLOCKS
-        if size < BLOCKS:
-            base = base + (c if half == 0 else 1 - c) * size
-        k_pos.extend(order_ref[base + b] for b in range(size))
-
-    begin = 0
+        k_pos += [order_ref[(yh * 8 + plane) * BLOCKS + b] for b in range(BLOCKS)]
+
+    for p in range(64):
+        slots[p] = -1
+    for t in range(total):
+        slots[k_pos[t]] = t
+    count = 0
+    for p in range(64):
+        found = slots[p]
+        sorted_k[count] = found
+        before[p] = count
+        count = count + jnp.where(found >= 0, 1, 0)
+
+    items = 0
+    code = 0
     for i in range(BLOCKS):
-        q_pos = order_ref[q_first + i]
-        fill = begin
-        for t in range(total):
-            item_q[fill >> 1] = i
-            item_k[fill] = t
-            item_v[fill] = t
-            item_f[fill] = 1.0
-            fill = fill + jnp.where(k_pos[t] < q_pos, 1, 0)
-        last = item_k[jnp.maximum(fill - 1, 0)]
-        item_k[fill] = last
-        item_v[fill] = total
-        item_f[fill] = 0.0
-        begin = begin + (((fill - begin) + 1) >> 1) * 2
-    items = begin >> 1
-    back = jnp.maximum(items - 1, 0)
-    again_q = jnp.where(items > 0, item_q[back], 0)
-    again_k = jnp.where(items > 0, item_k[2 * back], 0)
-    again_l = jnp.where(items > 0, item_k[2 * back + 1], 0)
-    for n in range(2):
-        item_q[items + n] = again_q
-        item_k[2 * (items + n)] = again_k
-        item_k[2 * (items + n) + 1] = again_l
-        item_v[2 * (items + n)] = total
-        item_v[2 * (items + n) + 1] = total
-        item_f[2 * (items + n)] = 0.0
-        item_f[2 * (items + n) + 1] = 0.0
+        n_seen = before[q_pos[i]]
+        mine = (i << 16) | (n_seen << 8)
+        for n in range((total + GROUP - 1) // GROUP):
+            item[items + n] = mine | (GROUP * n)
+        code = jnp.where(n_seen > 0, mine | n_seen, code)
+        items = items + ((n_seen + GROUP - 1) >> 1)
+    for n in range(3):
+        item[items + n] = code
+
+    def places(j):
+        code = item[j]
+        seen_count, base = (code >> 8) & 255, code & 255
+        at = [base + g for g in range(GROUP)]
+        blocks = [sorted_k[jnp.maximum(jnp.minimum(n, seen_count - 1), 0)] for n in at]
+        return code >> 16, blocks, [n < seen_count for n in at]
 
     halves = [slice(0, BLOCK), slice(BLOCK, ROWS)]
 
     def score(j, scores, maxima, cols):
-        keys = jnp.concatenate([kv_s[item_k[2 * j], :BLOCK], kv_s[item_k[2 * j + 1], :BLOCK]], 0)
-        s = nt(keys, q_ref[item_q[j], :, cols]) * LOG2E_SCALE
+        i, blocks, _ = places(j)
+        keys = jnp.concatenate([kv_s[t, :BLOCK] for t in blocks], axis=0)
+        s = nt(keys, q_ref[i, :, cols]) * LOG2E_SCALE
         scores[:, cols] = s
         maxima[:, cols] = jnp.max(s, axis=0, keepdims=True)
 
     def absorb(j, scores, maxima, cols):
-        i = item_q[j]
-        values = jnp.concatenate([value_of(kv_s, item_v[2 * j + n]) for n in range(2)], axis=1)
-        ones = jnp.concatenate(
-            [jnp.full((16, BLOCK), item_f[2 * j + n], F32).astype(BF16) for n in range(2)], axis=1
-        )
-        lhs = jnp.concatenate([values, ones], axis=0)
+        i, blocks, counts = places(j)
+        values = [value_of(kv_s, jnp.where(ok, t, total)) for t, ok in zip(blocks, counts)]
+        ones = [jnp.full((16, BLOCK), jnp.where(ok, 1.0, 0.0), F32).astype(BF16) for ok in counts]
+        lhs = jnp.concatenate([jnp.concatenate(values, axis=1), jnp.concatenate(ones, axis=1)], axis=0)
         old = m_ref[i, :, cols]
         new = jnp.maximum(old, maxima[:, cols])
         keep = jnp.exp2(old - new)
@@ -219,6 +217,7 @@
 
     if final:
         sub = lax.broadcasted_iota(jnp.int32, (16, ROWS), 0)
+        tail = jnp.zeros((16, ROWS), F32)
         for i in range(BLOCKS):
             sums = acc_ref[i, HEAD_DIM : HEAD_DIM + 1]
             some = sums > 0.0
@@ -227,26 +226,28 @@
             high = logs.astype(BF16).astype(F32)
             middle = (logs - high).astype(BF16).astype(F32)
             low = logs - high - middle
-            out_ref[i, :HEAD_DIM] = (acc_ref[i, :HEAD_DIM] * (1.0 / safe)).astype(BF16)
-            out_ref[i, HEAD_DIM:] = jnp.where(
-                sub == 0, high, jnp.where(sub == 1, middle, jnp.where(sub == 2, low, 0.0))
+            out_ref[i * HEAD_DIM : (i + 1) * HEAD_DIM] = (
+                acc_ref[i, :HEAD_DIM] * (1.0 / safe)
             ).astype(BF16)
-
-
-def attend(meta, order, q, shards, state, partner, final):
-    steps = tuple((a.shape[0], distance, half) for a, distance, half in shards)
-    total = sum(s[0] for s in steps)
+            for n, part in enumerate((high, middle, low)):
+                tail = jnp.where(sub == BLOCKS * n + i, part, tail)
+        out_ref[PARTIAL:] = tail.astype(BF16)
+
+
+def attend(meta, order, q, shards, state, partner, final=False):
+    steps = tuple(distance for _, distance in shards)
+    total = BLOCKS * len(steps)
     starts = state is None
-    args = [meta, order] + list(q) + [a for a, _, _ in shards] + ([] if starts else list(state))
+    args = [meta, order] + list(q) + [a for a, _ in shards] + ([] if starts else list(state))
     m_shape, acc_shape = (BLOCKS, 1, ROWS), (BLOCKS, EXTENDED, ROWS)
     if final:
-        out_shape = (jax.ShapeDtypeStruct((BLOCKS, PARTIAL, ROWS), BF16),)
+        out_shape = (jax.ShapeDtypeStruct((PARTIAL + 16, ROWS), BF16),)
         work = [pltpu.VMEM(m_shape, F32), pltpu.VMEM(acc_shape, F32)]
     else:
         out_shape = (jax.ShapeDtypeStruct(m_shape, F32), jax.ShapeDtypeStruct(acc_shape, F32))
         work = []
     pairs = BLOCKS * total // 2
-    slots = 2 * (BLOCKS * ((total + 1) // 2) + 4)
+    items = BLOCKS * ((total + GROUP - 1) // GROUP) + 8
     got = pl.pallas_call(
         functools.partial(attend_kernel, steps, partner, starts, final),
         out_shape=out_shape,
@@ -255,21 +256,19 @@
         scratch_shapes=work
         + [
             pltpu.VMEM((total + 1, 2 * BLOCK, HEAD_DIM), BF16),
-            pltpu.VMEM((2 * BLOCK, ROWS), F32),
-            pltpu.VMEM((2 * BLOCK, ROWS), F32),
+            pltpu.VMEM((GROUP * BLOCK, ROWS), F32),
+            pltpu.VMEM((GROUP * BLOCK, ROWS), F32),
             pltpu.VMEM((1, ROWS), F32),
             pltpu.VMEM((1, ROWS), F32),
-            pltpu.SMEM((slots // 2,), jnp.int32),
-            pltpu.SMEM((slots,), jnp.int32),
-            pltpu.SMEM((slots,), jnp.int32),
-            pltpu.SMEM((slots,), F32),
+            pltpu.SMEM((items,), jnp.int32),
+            pltpu.SMEM((64,), jnp.int32),
+            pltpu.SMEM((64,), jnp.int32),
+            pltpu.SMEM((total + 1,), jnp.int32),
         ]
         + ([pltpu.VMEM((BLOCKS, HEAD_DIM, ROWS), BF16)] if partner else []),
         compiler_params=pltpu.CompilerParams(vmem_limit_bytes=VMEM_BYTES),
         cost_estimate=pl.CostEstimate(
-            flops=pairs * 4 * BLOCK * ROWS * 8,
-            bytes_accessed=1 << 18,
-            transcendentals=pairs * BLOCK * ROWS // 32,
+            flops=pairs * 4 * BLOCK * ROWS * 8, bytes_accessed=1 << 18, transcendentals=pairs * 4096
         ),
         name="attend",
     )(*args)
@@ -277,16 +276,17 @@
 
 
 def combine_kernel(m_ref, acc_ref, other_ref, out_ref):
+    tail = other_ref[PARTIAL:].astype(F32)
+    logs = tail[:BLOCKS] + tail[BLOCKS : 2 * BLOCKS] + tail[2 * BLOCKS : 3 * BLOCKS]
     for i in range(BLOCKS):
         sums = acc_ref[i, HEAD_DIM : HEAD_DIM + 1]
         mine = m_ref[i] + jnp.log2(sums)
-        tail = other_ref[i, HEAD_DIM:].astype(F32)
-        theirs = tail[0:1] + tail[1:2] + tail[2:3]
+        theirs = logs[i : i + 1]
         top = jnp.maximum(mine, theirs)
         weight_mine, weight_theirs = jnp.exp2(mine - top), jnp.exp2(theirs - top)
         whole = weight_mine + weight_theirs
         result = acc_ref[i, :HEAD_DIM] * (weight_mine / (sums * whole)) + other_ref[
-            i, :HEAD_DIM
+            i * HEAD_DIM : (i + 1) * HEAD_DIM
         ].astype(F32) * (weight_theirs / whole)
         result = result.astype(BF16)
         for h in range(2):
@@ -306,7 +306,13 @@
     )(*state, other)
 
 
-def pack_kernel(queries_ref, keys_ref, values_ref, out_ref):
+def pack_kernel(queries_in, keys_in, values_in, out_ref, queries_ref, keys_ref, values_ref, sems):
+    pairs = ((queries_in, queries_ref), (keys_in, keys_ref), (values_in, values_ref))
+    copies = [pltpu.make_async_copy(a, b, sems.at[n]) for n, (a, b) in enumerate(pairs)]
+    for copy in copies:
+        copy.start()
+    for copy in copies:
+        copy.wait()
     for g in range(8):
         keys = keys_ref[:, g * HEAD_DIM : (g + 1) * HEAD_DIM]
         values = values_ref[:, g * HEAD_DIM : (g + 1) * HEAD_DIM]
@@ -322,9 +328,11 @@
     return pl.pallas_call(
         pack_kernel,
         out_shape=jax.ShapeDtypeStruct((16, rows, 4 * HEAD_DIM), BF16),
-        in_specs=[VMEM] * 3,
+        in_specs=[pl.BlockSpec(memory_space=pl.ANY)] * 3,
         out_specs=VMEM,
-        compiler_params=SMALL,
+        scratch_shapes=[pltpu.VMEM(a.shape, BF16) for a in (queries, keys, values)]
+        + [pltpu.SemaphoreType.DMA((3,))],
+        compiler_params=pltpu.CompilerParams(vmem_limit_bytes=56 * 2**20),
         name="pack",
     )(queries, keys, values)
 
@@ -372,25 +380,22 @@
 
     r2, s1 = onward(r1), swapped(r1)
     other_q = (other_a, lax.ppermute(q[2:], "yh", swap))
-    near = [(r1, 1, 0), (s1, -1, 0)]
-    mine = attend(meta, block_order, (q,), near, mine, False, False)
-    r2, mine, other_q = lax.optimization_barrier((r2, mine, other_q))
+    near = [(r1, 1), (s1, -1)]
+    r2, other_q = lax.optimization_barrier((r2, other_q))
 
     r3, s2 = onward(r2), swapped(r2)
-    theirs = attend(meta, block_order, other_q, [(kv, 0, 0)] + near, None, True, False)
+    theirs = attend(meta, block_order, other_q, [(kv, 0)] + near, None, True)
     r3, theirs = lax.optimization_barrier((r3, theirs))
 
-    r4 = onward(lax.dynamic_slice_in_dim(r3, 2 * lax.axis_index("c"), 2, 0))
-    s3 = swapped(r3)
-    middle = [(r2, 2, 0), (s2, -2, 0)]
-    theirs = attend(meta, block_order, other_q, middle, theirs, True, False)
+    r4, s3 = onward(r3), swapped(r3)
+    later = [(r2, 2), (s2, -2), (r3, 3), (s3, -3)]
+    theirs = attend(meta, block_order, other_q, later, theirs, True)
     r4, theirs = lax.optimization_barrier((r4, theirs))
 
-    s4 = swapped(r4)
-    far = [(r3, 3, 0), (s3, -3, 0), (r4, 4, 0), (s4, -4, 1)]
-    sent = attend(meta, block_order, other_q, far, theirs, True, True)
+    last = [(r4, 4)]
+    sent = attend(meta, block_order, other_q, last, theirs, True, True)
     other = lax.ppermute(sent, "yh", swap)
-    mine = attend(meta, block_order, (q,), middle + far, mine, False, False)
+    mine = attend(meta, block_order, (q,), near + later + last, mine, False)
     result = combine(mine, other).reshape(16, rows, 256)
     return unpack(lax.all_to_all(result, group, 0, 0, tiled=True))
 

time: 108 us -> 104 us (0.963)
  local copies, waits for them, and re-layouts: 6.02 us -> 0.04 us
  waiting for transfers between devices: 4.05 us -> 7.12 us
  Pallas kernels: 37.8 us -> 35.2 us
  starting transfers between devices: 24.1 us -> 25.5 us
    unnamed x20 -> x2, local copies, waits for them, and re-layouts: 5.96 us -> 0.01 us
    pallas_call x5 -> x4, Pallas kernels: 32 us -> 27.3 us  [attend(): pl.pallas_call(functools.partial(attend_kernel, steps, partner, starts, f...]
    ppermute x1, waiting for transfers between devices: 0.01 us -> 4.43 us  [body(): other_q = (other_a, lax.ppermute(q[2:], 'yh', swap))]
    ppermute x1, waiting for transfers between devices: 2.86 us -> 0.01 us  [body(): other = lax.ppermute(sent, 'yh', swap)]
    ppermute x4, waiting for transfers between devices: 0.01 us -> 2.44 us  [onward(): return lax.ppermute(a, ('z', 'c'), ring)]
    pallas_call x1, Pallas kernels: 0.1 us -> 2.21 us  [pack(): pl.pallas_call(pack_kernel, out_shape=jax.ShapeDtypeStruct((16, rows, 4 *...]
    ppermute x1, starting transfers between devices: 3.44 us -> 4.75 us  [body(): other = lax.ppermute(sent, 'yh', swap)]
    ppermute x4 -> x3, starting transfers between devices: 1.75 us -> 2.57 us  [swapped(): return lax.ppermute(a, 'c', swap)]
  transfers between devices with their start and end apart: 11 -> 10, of which waited for: 2 -> 4; matrix products, arithmetic and copies ran while one was open for 0% -> 0% of each run, Pallas kernels for 27% -> 28%
where the time goes in v4:
time: 104 us; the launch traced here: 105 us
  blocking collectives  36.8 us (35%)
  Pallas kernels  35.2 us (34%)
  starting transfers between devices  25.5 us (25%)
  waiting for transfers between devices  7.12 us (7%)
    pallas_call x4, Pallas kernels, attend(): pl.pallas_call(functools.partial(attend_kernel, steps, partner, starts, f...  27.3 us
    all_to_all x1, blocking collectives, body(): got = lax.all_to_all(pack(queries, keys, values), group, 0, 0, tiled=True)  23.1 us
    all_to_all x1, blocking collectives, body(): return unpack(lax.all_to_all(result, group, 0, 0, tiled=True))  13.8 us
    ppermute x4, starting transfers between devices, onward(): return lax.ppermute(a, ('z', 'c'), ring)  12.8 us
    ppermute x1, starting transfers between devices, body(): other = lax.ppermute(sent, 'yh', swap)  4.75 us
    ppermute x1, waiting for transfers between devices, body(): other_q = (other_a, lax.ppermute(q[2:], 'yh', swap))  4.43 us
    pallas_call x1, Pallas kernels, own_start(): pl.pallas_call(own_kernel, out_shape=(jax.ShapeDtypeStruct((BLOCKS, 1, RO...  4.33 us
    ppermute x1, starting transfers between devices, body(): other_a = lax.ppermute(q[:2], 'yh', swap)  2.71 us
  transfers between devices with their start and end apart: 10, of which 4 were waited for; matrix products, arithmetic and copies ran while one was open for 0% of the time, Pallas kernels for 28%

profile of v4, /device:TPU:1, one launch (start us, length us, event | category | flops | bytes accessed | tf_op | source)
XLA Modules:
  0.0 104.9 jit_solution(12264835394995465534)
XLA Ops:
  0.0 2.2 %pack.1 = bf16[16,64,512]{2,1,0:T(8,128)(2,1)} custom-call(bf16[64,4096]{1,0:T(8,128)(2,1)} %queries_in.1, bf16[64,1024]{1,0:T(8,128)(2,1)} %keys_in.1, bf16[64,1024]{1,0:T(8,128)(2,1)} %values_in.1), custom_call_target="tpu_custom_call" | custom-call | tf_op jit(solution)/shard_map/pack/pallas_call | solution.py:328
  2.2 23.1 %all_to_all.10 = bf16[16,64,512]{2,1,0:T(8,128)(2,1)S(1)} all-to-all(bf16[16,64,512]{2,1,0:T(8,128)(2,1)} %pack.1), channel_id=1, replica_groups=mesh['yh'=2,'z'=8,'c'=2,'yl'=2,'x'=4] {'c','yl','x'}, dimensions={0} | all-to-all | bytes 2097152 | tf_op jit(solution)/shard_map/all_to_all | solution.py:364
  25.3 0.0 copy-start
  25.3 0.3 prepare.1
  25.6 5.7 %collective-permute-start = (bf16[4,512,128]{2,1,0:T(8,128)(2,1)S(1)}, bf16[4,512,128]{2,1,0:T(8,128)(2,1)S(1)}, u32[]{:S(2)}, u32[]{:S(2)}) collective-permute-start(bf16[4,512,128]{2,1,0:T(8,128)(2,1)S(1)} %get-tuple-element.29.kv_ref.refs_4_), channel_id=1, source_target_pairs={{0,16},{8,120},{16,32},{24,8},{32,48},{40,24},{48,64},{56,40},{64,... | collective-permute-start | bytes 1572872 | tf_op jit(solution)/shard_map/ppermute | solution.py:371
  31.3 2.7 %collective-permute-start.1 = (bf16[2,128,512]{2,1,0:T(8,128)(2,1)S(1)}, bf16[2,128,512]{2,1,0:T(8,128)(2,1)S(1)}, u32[]{:S(2)}, u32[]{:S(2)}) collective-permute-start(bf16[2,128,512]{2,1,0:T(8,128)(2,1)S(1)} %slice.6), channel_id=1, source_target_pairs={{0,128},{128,0},{1,129},{129,1},{2,130},{130,2},{3,131},{131,3},{4... | collective-permute-start | bytes 786440 | tf_op jit(solution)/shard_map/ppermute | solution.py:377
  34.0 0.1 pad_add_fusion.meta_ref.refs_0_
  34.0 0.0 copy-done
  34.0 4.3 %own_start.1 = (f32[4,1,512]{2,1,0:T(1,128)S(1)}, f32[4,136,512]{2,1,0:T(8,128)S(1)}) custom-call(s32[3]{0:T(128)S(1)} %pad_add_fusion.meta_ref.refs_0_, s32[64]{0:T(128)S(1)} %copy-done, bf16[4,128,512]{2,1,0:T(8,128)(2,1)S(1)} %get-tuple-element.33.q_ref.refs_2_, bf16[4,512,128]{2,1,0:T(8,128)(2,1)S(1)} %get-tuple-element.29.kv_ref.refs_4_), custom_call_target="tpu_custom_call" | custom-call | flops 67108864 | bytes 262144 | tf_op jit(solution)/shard_map/own_start/pallas_call | solution.py:89
  38.4 0.0 collective-permute-done.1.refs_2_
  38.4 0.0 collective-permute-done.refs_5_.refs_3_
  38.4 3.4 %collective-permute-start.3 = (bf16[4,512,128]{2,1,0:T(8,128)(2,1)S(1)}, bf16[4,512,128]{2,1,0:T(8,128)(2,1)S(1)}, u32[]{:S(2)}, u32[]{:S(2)}) collective-permute-start(bf16[4,512,128]{2,1,0:T(8,128)(2,1)S(1)} %collective-permute-done.refs_5_.refs_3_), channel_id=1, source_target_pairs={{0,16},{8,120},{16,32},{24,8},{32,48},{40,24},{48,64},{56,40},{64,... | collective-permute-start | bytes 1572872 | tf_op jit(solution)/shard_map/ppermute | solution.py:371
  41.8 2.7 %collective-permute-start.4 = (bf16[2,128,512]{2,1,0:T(8,128)(2,1)S(1)}, bf16[2,128,512]{2,1,0:T(8,128)(2,1)S(1)}, u32[]{:S(2)}, u32[]{:S(2)}) collective-permute-start(bf16[2,128,512]{2,1,0:T(8,128)(2,1)S(1)} %slice.7), channel_id=1, source_target_pairs={{0,128},{128,0},{1,129},{129,1},{2,130},{130,2},{3,131},{131,3},{4... | collective-permute-start | bytes 786440 | tf_op jit(solution)/shard_map/ppermute | solution.py:382
  44.6 0.0 collective-permute-start.2
  44.6 4.4 %collective-permute-done.4.refs_3_ = bf16[2,128,512]{2,1,0:T(8,128)(2,1)S(1)} collective-permute-done((bf16[2,128,512]{2,1,0:T(8,128)(2,1)S(1)}, bf16[2,128,512]{2,1,0:T(8,128)(2,1)S(1)}, u32[]{:S(2)}, u32[]{:S(2)}) %collective-permute-start.4) | collective-permute-done | bytes 262176 | tf_op jit(solution)/shard_map/ppermute | solution.py:382
  49.0 0.0 collective-permute-done.3.refs_4_.refs_5_
  49.0 2.4 %collective-permute-start.6 = (bf16[4,512,128]{2,1,0:T(8,128)(2,1)S(1)}, bf16[4,512,128]{2,1,0:T(8,128)(2,1)S(1)}, u32[]{:S(2)}, u32[]{:S(2)}) collective-permute-start(bf16[4,512,128]{2,1,0:T(8,128)(2,1)S(1)} %collective-permute-done.3.refs_4_.refs_5_), channel_id=1, source_target_pairs={{0,16},{8,120},{16,32},{24,8},{32,48},{40,24},{48,64},{56,40},{64,... | collective-permute-start | bytes 1572872 | tf_op jit(solution)/shard_map/ppermute | solution.py:371
  51.4 0.0 collective-permute-start.5
  51.4 0.0 collective-permute-done.2.refs_6_.refs_4_
  51.4 4.3 %attend.4 = (f32[4,1,512]{2,1,0:T(1,128)S(1)}, f32[4,136,512]{2,1,0:T(8,128)S(1)}) custom-call(s32[3]{0:T(128)S(1)} %pad_add_fusion.meta_ref.refs_0_, s32[64]{0:T(128)S(1)} %copy-done, bf16[2,128,512]{2,1,0:T(8,128)(2,1)S(1)} %collective-permute-done.1.refs_2_, bf16[2,128,512]{2,1,0:T(8,128)(2,1)S(1)} %collective-permute-done.4.refs_3_, ...), custom_call_target="tpu_custom_call" | custom-call | flops 100663296 | bytes 262144 | tf_op jit(solution)/shard_map/attend/pallas_call | solution.py:251
  55.7 1.8 %collective-permute-done.6.refs_6_.refs_7_ = bf16[4,512,128]{2,1,0:T(8,128)(2,1)S(1)} collective-permute-done((bf16[4,512,128]{2,1,0:T(8,128)(2,1)S(1)}, bf16[4,512,128]{2,1,0:T(8,128)(2,1)S(1)}, u32[]{:S(2)}, u32[]{:S(2)}) %collective-permute-start.6) | collective-permute-done | bytes 524320 | tf_op jit(solution)/shard_map/ppermute | solution.py:371
  57.5 2.6 %collective-permute-start.7 = (bf16[4,512,128]{2,1,0:T(8,128)(2,1)S(1)}, bf16[4,512,128]{2,1,0:T(8,128)(2,1)S(1)}, u32[]{:S(2)}, u32[]{:S(2)}) collective-permute-start(bf16[4,512,128]{2,1,0:T(8,128)(2,1)S(1)} %collective-permute-done.6.refs_6_.refs_7_), channel_id=1, source_target_pairs={{0,8},{8,0},{1,9},{9,1},{2,10},{10,2},{3,11},{11,3},{4,12},{12,4},... | collective-permute-start | bytes 1572872 | tf_op jit(solution)/shard_map/ppermute | solution.py:374
  60.1 1.3 %collective-permute-start.8 = (bf16[4,512,128]{2,1,0:T(8,128)(2,1)S(1)}, bf16[4,512,128]{2,1,0:T(8,128)(2,1)S(1)}, u32[]{:S(2)}, u32[]{:S(2)}) collective-permute-start(bf16[4,512,128]{2,1,0:T(8,128)(2,1)S(1)} %collective-permute-done.6.refs_6_.refs_7_), channel_id=1, source_target_pairs={{0,16},{8,120},{16,32},{24,8},{32,48},{40,24},{48,64},{56,40},{64,... | collective-permute-start | bytes 1572872 | tf_op jit(solution)/shard_map/ppermute | solution.py:371
  61.3 0.0 collective-permute-done.5.refs_5_.refs_6_
  61.4 0.2 collective-permute-done.7.refs_7_.refs_8_
  61.6 6.1 %attend.5 = (f32[4,1,512]{2,1,0:T(1,128)S(1)}, f32[4,136,512]{2,1,0:T(8,128)S(1)}) custom-call(s32[3]{0:T(128)S(1)} %pad_add_fusion.meta_ref.refs_0_, s32[64]{0:T(128)S(1)} %copy-done, bf16[2,128,512]{2,1,0:T(8,128)(2,1)S(1)} %collective-permute-done.1.refs_2_, bf16[2,128,512]{2,1,0:T(8,128)(2,1)S(1)} %collective-permute-done.4.refs_3_, ...), custom_call_target="tpu_custom_call" | custom-call | flops 134217728 | bytes 262144 | tf_op jit(solution)/shard_map/attend/pallas_call | solution.py:251
  67.7 0.6 collective-permute-done.8.refs_9_.refs_4_
  68.4 2.4 %attend.7 = bf16[528,512]{1,0:T(8,128)(2,1)S(1)} custom-call(s32[3]{0:T(128)S(1)} %pad_add_fusion.meta_ref.refs_0_, s32[64]{0:T(128)S(1)} %copy-done, bf16[2,128,512]{2,1,0:T(8,128)(2,1)S(1)} %collective-permute-done.1.refs_2_, bf16[2,128,512]{2,1,0:T(8,128)(2,1)S(1)} %collective-permute-done.4.refs_3_, ...), custom_call_target="tpu_custom_call" | custom-call | flops 33554432 | bytes 262144 | tf_op jit(solution)/shard_map/attend/pallas_call | solution.py:251
  70.8 4.7 %collective-permute-start.9 = (bf16[528,512]{1,0:T(8,128)(2,1)S(1)}, bf16[528,512]{1,0:T(8,128)(2,1)S(1)}, u32[]{:S(2)}, u32[]{:S(2)}) collective-permute-start(bf16[528,512]{1,0:T(8,128)(2,1)S(1)} %attend.7), channel_id=1, source_target_pairs={{0,128},{128,0},{1,129},{129,1},{2,130},{130,2},{3,131},{131,3},{4... | collective-permute-start | bytes 1622024 | tf_op jit(solution)/shard_map/ppermute | solution.py:397
  75.6 14.4 %attend.6 = (f32[4,1,512]{2,1,0:T(1,128)S(1)}, f32[4,136,512]{2,1,0:T(8,128)S(1)}) custom-call(s32[3]{0:T(128)S(1)} %pad_add_fusion.meta_ref.refs_0_, s32[64]{0:T(128)S(1)} %copy-done, bf16[4,128,512]{2,1,0:T(8,128)(2,1)S(1)} %get-tuple-element.33.q_ref.refs_2_, bf16[4,512,128]{2,1,0:T(8,128)(2,1)S(1)} %collective-permute-done.refs_5_.refs_3_, ...), custom_call_target="tpu_custom_call" | custom-call | flops 234881024 | bytes 262144 | tf_op jit(solution)/shard_map/attend/pallas_call | solution.py:251
  90.0 0.0 collective-permute-done.9.other_ref
  90.0 0.3 combine.1
  90.3 13.8 %all_to_all.11.back_ref = bf16[16,64,256]{2,1,0:T(8,128)(2,1)S(1)} all-to-all(bf16[16,64,256]{2,1,0:T(8,128)(2,1)S(1)} %bitcast.6), channel_id=1, replica_groups=mesh['yh'=2,'z'=8,'c'=2,'yl'=2,'x'=4] {'c','yl','x'}, dimensions={0} | all-to-all | bytes 1048576 | tf_op jit(solution)/shard_map/all_to_all | solution.py:400
  104.1 0.8 unpack.1
  (2 shorter events, 0.0 us)
Async XLA Ops:
  25.3 8.7 %copy-start = (s32[64]{0:T(128)S(1)}, s32[64]{0:T(128)}, u32[]{:S(2)}) copy-start(s32[64]{0:T(128)} %refs_1_.7) | copy-start | bytes 772
  25.6 12.8 %collective-permute-start = (bf16[4,512,128]{2,1,0:T(8,128)(2,1)S(1)}, bf16[4,512,128]{2,1,0:T(8,128)(2,1)S(1)}, u32[]{:S(2)}, u32[]{:S(2)}) collective-permute-start(bf16[4,512,128]{2,1,0:T(8,128)(2,1)S(1)} %get-tuple-element.29.kv_ref.refs_4_), channel_id=1, source_target_pairs={{0,16},{8,120},{16,32},{24,8},{32,48},{40,24},{48,64},{56,40},{64,... | collective-permute-start | bytes 1572872 | tf_op jit(solution)/shard_map/ppermute | solution.py:371
  31.3 7.1 %collective-permute-start.1 = (bf16[2,128,512]{2,1,0:T(8,128)(2,1)S(1)}, bf16[2,128,512]{2,1,0:T(8,128)(2,1)S(1)}, u32[]{:S(2)}, u32[]{:S(2)}) collective-permute-start(bf16[2,128,512]{2,1,0:T(8,128)(2,1)S(1)} %slice.6), channel_id=1, source_target_pairs={{0,128},{128,0},{1,129},{129,1},{2,130},{130,2},{3,131},{131,3},{4... | collective-permute-start | bytes 786440 | tf_op jit(solution)/shard_map/ppermute | solution.py:377
  38.4 10.6 %collective-permute-start.3 = (bf16[4,512,128]{2,1,0:T(8,128)(2,1)S(1)}, bf16[4,512,128]{2,1,0:T(8,128)(2,1)S(1)}, u32[]{:S(2)}, u32[]{:S(2)}) collective-permute-start(bf16[4,512,128]{2,1,0:T(8,128)(2,1)S(1)} %collective-permute-done.refs_5_.refs_3_), channel_id=1, source_target_pairs={{0,16},{8,120},{16,32},{24,8},{32,48},{40,24},{48,64},{56,40},{64,... | collective-permute-start | bytes 1572872 | tf_op jit(solution)/shard_map/ppermute | solution.py:371
  41.8 7.1 %collective-permute-start.4 = (bf16[2,128,512]{2,1,0:T(8,128)(2,1)S(1)}, bf16[2,128,512]{2,1,0:T(8,128)(2,1)S(1)}, u32[]{:S(2)}, u32[]{:S(2)}) collective-permute-start(bf16[2,128,512]{2,1,0:T(8,128)(2,1)S(1)} %slice.7), channel_id=1, source_target_pairs={{0,128},{128,0},{1,129},{129,1},{2,130},{130,2},{3,131},{131,3},{4... | collective-permute-start | bytes 786440 | tf_op jit(solution)/shard_map/ppermute | solution.py:382
  44.6 6.8 %collective-permute-start.2 = (bf16[4,512,128]{2,1,0:T(8,128)(2,1)S(1)}, bf16[4,512,128]{2,1,0:T(8,128)(2,1)S(1)}, u32[]{:S(2)}, u32[]{:S(2)}) collective-permute-start(bf16[4,512,128]{2,1,0:T(8,128)(2,1)S(1)} %collective-permute-done.refs_5_.refs_3_), channel_id=1, source_target_pairs={{0,8},{8,0},{1,9},{9,1},{2,10},{10,2},{3,11},{11,3},{4,12},{12,4},... | collective-permute-start | bytes 1572872 | tf_op jit(solution)/shard_map/ppermute | solution.py:374
  49.0 8.5 %collective-permute-start.6 = (bf16[4,512,128]{2,1,0:T(8,128)(2,1)S(1)}, bf16[4,512,128]{2,1,0:T(8,128)(2,1)S(1)}, u32[]{:S(2)}, u32[]{:S(2)}) collective-permute-start(bf16[4,512,128]{2,1,0:T(8,128)(2,1)S(1)} %collective-permute-done.3.refs_4_.refs_5_), channel_id=1, source_target_pairs={{0,16},{8,120},{16,32},{24,8},{32,48},{40,24},{48,64},{56,40},{64,... | collective-permute-start | bytes 1572872 | tf_op jit(solution)/shard_map/ppermute | solution.py:371
  51.4 10.0 %collective-permute-start.5 = (bf16[4,512,128]{2,1,0:T(8,128)(2,1)S(1)}, bf16[4,512,128]{2,1,0:T(8,128)(2,1)S(1)}, u32[]{:S(2)}, u32[]{:S(2)}) collective-permute-start(bf16[4,512,128]{2,1,0:T(8,128)(2,1)S(1)} %collective-permute-done.3.refs_4_.refs_5_), channel_id=1, source_target_pairs={{0,8},{8,0},{1,9},{9,1},{2,10},{10,2},{3,11},{11,3},{4,12},{12,4},... | collective-permute-start | bytes 1572872 | tf_op jit(solution)/shard_map/ppermute | solution.py:374
  57.5 4.1 %collective-permute-start.7 = (bf16[4,512,128]{2,1,0:T(8,128)(2,1)S(1)}, bf16[4,512,128]{2,1,0:T(8,128)(2,1)S(1)}, u32[]{:S(2)}, u32[]{:S(2)}) collective-permute-start(bf16[4,512,128]{2,1,0:T(8,128)(2,1)S(1)} %collective-permute-done.6.refs_6_.refs_7_), channel_id=1, source_target_pairs={{0,8},{8,0},{1,9},{9,1},{2,10},{10,2},{3,11},{11,3},{4,12},{12,4},... | collective-permute-start | bytes 1572872 | tf_op jit(solution)/shard_map/ppermute | solution.py:374
  60.1 8.3 %collective-permute-start.8 = (bf16[4,512,128]{2,1,0:T(8,128)(2,1)S(1)}, bf16[4,512,128]{2,1,0:T(8,128)(2,1)S(1)}, u32[]{:S(2)}, u32[]{:S(2)}) collective-permute-start(bf16[4,512,128]{2,1,0:T(8,128)(2,1)S(1)} %collective-permute-done.6.refs_6_.refs_7_), channel_id=1, source_target_pairs={{0,16},{8,120},{16,32},{24,8},{32,48},{40,24},{48,64},{56,40},{64,... | collective-permute-start | bytes 1572872 | tf_op jit(solution)/shard_map/ppermute | solution.py:371
  70.8 19.2 %collective-permute-start.9 = (bf16[528,512]{1,0:T(8,128)(2,1)S(1)}, bf16[528,512]{1,0:T(8,128)(2,1)S(1)}, u32[]{:S(2)}, u32[]{:S(2)}) collective-permute-start(bf16[528,512]{1,0:T(8,128)(2,1)S(1)} %attend.7), channel_id=1, source_target_pairs={{0,128},{128,0},{1,129},{129,1},{2,130},{130,2},{3,131},{131,3},{4... | collective-permute-start | bytes 1622024 | tf_op jit(solution)/shard_map/ppermute | solution.py:397

commit v5 on v4

--- a/solution.py
+++ b/solution.py
@@ -381,7 +381,8 @@
     r2, s1 = onward(r1), swapped(r1)
     other_q = (other_a, lax.ppermute(q[2:], "yh", swap))
     near = [(r1, 1), (s1, -1)]
-    r2, other_q = lax.optimization_barrier((r2, other_q))
+    mine = attend(meta, block_order, (q,), near, mine, False)
+    r2, other_q, mine = lax.optimization_barrier((r2, other_q, mine))
 
     r3, s2 = onward(r2), swapped(r2)
     theirs = attend(meta, block_order, other_q, [(kv, 0)] + near, None, True)
@@ -395,7 +396,7 @@
     last = [(r4, 4)]
     sent = attend(meta, block_order, other_q, last, theirs, True, True)
     other = lax.ppermute(sent, "yh", swap)
-    mine = attend(meta, block_order, (q,), near + later + last, mine, False)
+    mine = attend(meta, block_order, (q,), later + last, mine, False)
     result = combine(mine, other).reshape(16, rows, 256)
     return unpack(lax.all_to_all(result, group, 0, 0, tiled=True))
 

time: 104 us -> 104 us (level); the launches traced: 105 us -> 103 us
  waiting for transfers between devices: 7.12 us -> 3.34 us
  Pallas kernels: 35.2 us -> 36.8 us
  blocking collectives: 36.8 us -> 38.1 us
    ppermute x1, waiting for transfers between devices: 4.43 us -> 0.01 us  [body(): other_q = (other_a, lax.ppermute(q[2:], 'yh', swap))]
    ppermute x1, waiting for transfers between devices: 0.01 us -> 2.78 us  [body(): other = lax.ppermute(sent, 'yh', swap)]
    ppermute x4, waiting for transfers between devices: 2.44 us -> 0.55 us  [onward(): return lax.ppermute(a, ('z', 'c'), ring)]
    pallas_call x4 -> x5, Pallas kernels: 27.3 us -> 28.9 us  [attend(): pl.pallas_call(functools.partial(attend_kernel, steps, partner, starts, f...]
    all_to_all x1, blocking collectives: 13.8 us -> 15 us  [body(): return unpack(lax.all_to_all(result, group, 0, 0, tiled=True))]
  transfers between devices with their start and end apart: 10 -> 10, of which waited for: 4 -> 2; matrix products, arithmetic and copies ran while one was open for 0% -> 0% of each run, Pallas kernels for 28% -> 29%
where the time goes in v5:
time: 104 us; the launch traced here: 103 us
  blocking collectives  38.1 us (37%)
  Pallas kernels  36.8 us (35%)
  starting transfers between devices  24.9 us (24%)
  waiting for transfers between devices  3.34 us (3%)
    pallas_call x5, Pallas kernels, attend(): pl.pallas_call(functools.partial(attend_kernel, steps, partner, starts, f...  28.9 us
    all_to_all x1, blocking collectives, body(): got = lax.all_to_all(pack(queries, keys, values), group, 0, 0, tiled=True)  23.1 us
    all_to_all x1, blocking collectives, body(): return unpack(lax.all_to_all(result, group, 0, 0, tiled=True))  15 us
    ppermute x4, starting transfers between devices, onward(): return lax.ppermute(a, ('z', 'c'), ring)  13.4 us
    pallas_call x1, Pallas kernels, own_start(): pl.pallas_call(own_kernel, out_shape=(jax.ShapeDtypeStruct((BLOCKS, 1, RO...  4.3 us
    ppermute x1, starting transfers between devices, body(): other = lax.ppermute(sent, 'yh', swap)  4.1 us
    ppermute x1, waiting for transfers between devices, body(): other = lax.ppermute(sent, 'yh', swap)  2.78 us
    ppermute x1, starting transfers between devices, body(): other_q = (other_a, lax.ppermute(q[2:], 'yh', swap))  2.71 us
  transfers between devices with their start and end apart: 10, of which 2 were waited for; matrix products, arithmetic and copies ran while one was open for 0% of the time, Pallas kernels for 29%

profile of v5, /device:TPU:1, one launch (start us, length us, event | category | flops | bytes accessed | tf_op | source)
XLA Modules:
  0.0 103.4 jit_solution(7608899190786720253)
XLA Ops:
  0.0 2.2 %pack.1 = bf16[16,64,512]{2,1,0:T(8,128)(2,1)} custom-call(bf16[64,4096]{1,0:T(8,128)(2,1)} %queries_in.1, bf16[64,1024]{1,0:T(8,128)(2,1)} %keys_in.1, bf16[64,1024]{1,0:T(8,128)(2,1)} %values_in.1), custom_call_target="tpu_custom_call" | custom-call | tf_op jit(solution)/shard_map/pack/pallas_call | solution.py:328
  2.2 23.1 %all_to_all.10 = bf16[16,64,512]{2,1,0:T(8,128)(2,1)S(1)} all-to-all(bf16[16,64,512]{2,1,0:T(8,128)(2,1)} %pack.1), channel_id=1, replica_groups=mesh['yh'=2,'z'=8,'c'=2,'yl'=2,'x'=4] {'c','yl','x'}, dimensions={0} | all-to-all | bytes 2097152 | tf_op jit(solution)/shard_map/all_to_all | solution.py:364
  25.3 0.0 copy-start
  25.3 0.3 prepare.1
  25.6 5.7 %collective-permute-start = (bf16[4,512,128]{2,1,0:T(8,128)(2,1)S(1)}, bf16[4,512,128]{2,1,0:T(8,128)(2,1)S(1)}, u32[]{:S(2)}, u32[]{:S(2)}) collective-permute-start(bf16[4,512,128]{2,1,0:T(8,128)(2,1)S(1)} %get-tuple-element.33.kv_ref.refs_4_), channel_id=1, source_target_pairs={{0,16},{8,120},{16,32},{24,8},{32,48},{40,24},{48,64},{56,40},{64,... | collective-permute-start | bytes 1572872 | tf_op jit(solution)/shard_map/ppermute | solution.py:371
  31.2 2.7 %collective-permute-start.1 = (bf16[2,128,512]{2,1,0:T(8,128)(2,1)S(1)}, bf16[2,128,512]{2,1,0:T(8,128)(2,1)S(1)}, u32[]{:S(2)}, u32[]{:S(2)}) collective-permute-start(bf16[2,128,512]{2,1,0:T(8,128)(2,1)S(1)} %slice.6), channel_id=1, source_target_pairs={{0,128},{128,0},{1,129},{129,1},{2,130},{130,2},{3,131},{131,3},{4... | collective-permute-start | bytes 786440 | tf_op jit(solution)/shard_map/ppermute | solution.py:377
  34.0 0.1 pad_add_fusion.meta_ref.refs_0_
  34.0 0.0 copy-done
  34.0 4.3 %own_start.1 = (f32[4,1,512]{2,1,0:T(1,128)S(1)}, f32[4,136,512]{2,1,0:T(8,128)S(1)}) custom-call(s32[3]{0:T(128)S(1)} %pad_add_fusion.meta_ref.refs_0_, s32[64]{0:T(128)S(1)} %copy-done, bf16[4,128,512]{2,1,0:T(8,128)(2,1)S(1)} %get-tuple-element.37.q_ref.refs_2_, bf16[4,512,128]{2,1,0:T(8,128)(2,1)S(1)} %get-tuple-element.33.kv_ref.refs_4_), custom_call_target="tpu_custom_call" | custom-call | flops 67108864 | bytes 262144 | tf_op jit(solution)/shard_map/own_start/pallas_call | solution.py:89
  38.3 0.0 collective-permute-done.1.refs_2_
  38.3 0.0 collective-permute-done.refs_3_.refs_5_
  38.4 0.5 collective-permute-start.4
  38.9 3.3 %collective-permute-start.2 = (bf16[4,512,128]{2,1,0:T(8,128)(2,1)S(1)}, bf16[4,512,128]{2,1,0:T(8,128)(2,1)S(1)}, u32[]{:S(2)}, u32[]{:S(2)}) collective-permute-start(bf16[4,512,128]{2,1,0:T(8,128)(2,1)S(1)} %collective-permute-done.refs_3_.refs_5_), channel_id=1, source_target_pairs={{0,16},{8,120},{16,32},{24,8},{32,48},{40,24},{48,64},{56,40},{64,... | collective-permute-start | bytes 1572872 | tf_op jit(solution)/shard_map/ppermute | solution.py:371
  42.2 2.7 %collective-permute-start.3 = (bf16[2,128,512]{2,1,0:T(8,128)(2,1)S(1)}, bf16[2,128,512]{2,1,0:T(8,128)(2,1)S(1)}, u32[]{:S(2)}, u32[]{:S(2)}) collective-permute-start(bf16[2,128,512]{2,1,0:T(8,128)(2,1)S(1)} %slice.7), channel_id=1, source_target_pairs={{0,128},{128,0},{1,129},{129,1},{2,130},{130,2},{3,131},{131,3},{4... | collective-permute-start | bytes 786440 | tf_op jit(solution)/shard_map/ppermute | solution.py:382
  44.9 0.0 collective-permute-done.4.refs_4_.refs_6_
  44.9 4.9 %attend.5 = (f32[4,1,512]{2,1,0:T(1,128)S(1)}, f32[4,136,512]{2,1,0:T(8,128)S(1)}) custom-call(s32[3]{0:T(128)S(1)} %pad_add_fusion.meta_ref.refs_0_, s32[64]{0:T(128)S(1)} %copy-done, bf16[4,128,512]{2,1,0:T(8,128)(2,1)S(1)} %get-tuple-element.37.q_ref.refs_2_, bf16[4,512,128]{2,1,0:T(8,128)(2,1)S(1)} %collective-permute-done.refs_3_.refs_5_, ...), custom_call_target="tpu_custom_call" | custom-call | flops 67108864 | bytes 262144 | tf_op jit(solution)/shard_map/attend/pallas_call | solution.py:251
  49.8 0.0 collective-permute-done.3.refs_3_
  49.9 0.0 collective-permute-done.2.refs_4_.refs_3_
  49.9 2.6 %collective-permute-start.6 = (bf16[4,512,128]{2,1,0:T(8,128)(2,1)S(1)}, bf16[4,512,128]{2,1,0:T(8,128)(2,1)S(1)}, u32[]{:S(2)}, u32[]{:S(2)}) collective-permute-start(bf16[4,512,128]{2,1,0:T(8,128)(2,1)S(1)} %collective-permute-done.2.refs_4_.refs_3_), channel_id=1, source_target_pairs={{0,16},{8,120},{16,32},{24,8},{32,48},{40,24},{48,64},{56,40},{64,... | collective-permute-start | bytes 1572872 | tf_op jit(solution)/shard_map/ppermute | solution.py:371
  52.5 0.0 collective-permute-start.5
  52.5 6.3 %attend.6 = (f32[4,1,512]{2,1,0:T(1,128)S(1)}, f32[4,136,512]{2,1,0:T(8,128)S(1)}) custom-call(s32[3]{0:T(128)S(1)} %pad_add_fusion.meta_ref.refs_0_, s32[64]{0:T(128)S(1)} %copy-done, bf16[2,128,512]{2,1,0:T(8,128)(2,1)S(1)} %collective-permute-done.1.refs_2_, bf16[2,128,512]{2,1,0:T(8,128)(2,1)S(1)} %collective-permute-done.3.refs_3_, ...), custom_call_target="tpu_custom_call" | custom-call | flops 100663296 | bytes 262144 | tf_op jit(solution)/shard_map/attend/pallas_call | solution.py:251
  58.9 0.0 collective-permute-done.6.refs_6_.refs_5_
  58.9 1.5 %collective-permute-start.7 = (bf16[4,512,128]{2,1,0:T(8,128)(2,1)S(1)}, bf16[4,512,128]{2,1,0:T(8,128)(2,1)S(1)}, u32[]{:S(2)}, u32[]{:S(2)}) collective-permute-start(bf16[4,512,128]{2,1,0:T(8,128)(2,1)S(1)} %collective-permute-done.6.refs_6_.refs_5_), channel_id=1, source_target_pairs={{0,8},{8,0},{1,9},{9,1},{2,10},{10,2},{3,11},{11,3},{4,12},{12,4},... | collective-permute-start | bytes 1572872 | tf_op jit(solution)/shard_map/ppermute | solution.py:374
  60.3 1.7 %collective-permute-start.8 = (bf16[4,512,128]{2,1,0:T(8,128)(2,1)S(1)}, bf16[4,512,128]{2,1,0:T(8,128)(2,1)S(1)}, u32[]{:S(2)}, u32[]{:S(2)}) collective-permute-start(bf16[4,512,128]{2,1,0:T(8,128)(2,1)S(1)} %collective-permute-done.6.refs_6_.refs_5_), channel_id=1, source_target_pairs={{0,16},{8,120},{16,32},{24,8},{32,48},{40,24},{48,64},{56,40},{64,... | collective-permute-start | bytes 1572872 | tf_op jit(solution)/shard_map/ppermute | solution.py:371
  62.1 0.0 collective-permute-done.5.refs_5_.refs_4_
  62.1 0.0 collective-permute-done.7.refs_7_.refs_6_
  62.1 6.0 %attend.7 = (f32[4,1,512]{2,1,0:T(1,128)S(1)}, f32[4,136,512]{2,1,0:T(8,128)S(1)}) custom-call(s32[3]{0:T(128)S(1)} %pad_add_fusion.meta_ref.refs_0_, s32[64]{0:T(128)S(1)} %copy-done, bf16[2,128,512]{2,1,0:T(8,128)(2,1)S(1)} %collective-permute-done.1.refs_2_, bf16[2,128,512]{2,1,0:T(8,128)(2,1)S(1)} %collective-permute-done.3.refs_3_, ...), custom_call_target="tpu_custom_call" | custom-call | flops 134217728 | bytes 262144 | tf_op jit(solution)/shard_map/attend/pallas_call | solution.py:251
  68.1 0.5 collective-permute-done.8.refs_7_.refs_4_
  68.7 3.1 %attend.9 = bf16[528,512]{1,0:T(8,128)(2,1)S(1)} custom-call(s32[3]{0:T(128)S(1)} %pad_add_fusion.meta_ref.refs_0_, s32[64]{0:T(128)S(1)} %copy-done, bf16[2,128,512]{2,1,0:T(8,128)(2,1)S(1)} %collective-permute-done.1.refs_2_, bf16[2,128,512]{2,1,0:T(8,128)(2,1)S(1)} %collective-permute-done.3.refs_3_, ...), custom_call_target="tpu_custom_call" | custom-call | flops 33554432 | bytes 262144 | tf_op jit(solution)/shard_map/attend/pallas_call | solution.py:251
  71.8 4.1 %collective-permute-start.9 = (bf16[528,512]{1,0:T(8,128)(2,1)S(1)}, bf16[528,512]{1,0:T(8,128)(2,1)S(1)}, u32[]{:S(2)}, u32[]{:S(2)}) collective-permute-start(bf16[528,512]{1,0:T(8,128)(2,1)S(1)} %attend.9), channel_id=1, source_target_pairs={{0,128},{128,0},{1,129},{129,1},{2,130},{130,2},{3,131},{131,3},{4... | collective-permute-start | bytes 1622024 | tf_op jit(solution)/shard_map/ppermute | solution.py:398
  75.9 8.5 %attend.8 = (f32[4,1,512]{2,1,0:T(1,128)S(1)}, f32[4,136,512]{2,1,0:T(8,128)S(1)}) custom-call(s32[3]{0:T(128)S(1)} %pad_add_fusion.meta_ref.refs_0_, s32[64]{0:T(128)S(1)} %copy-done, bf16[4,128,512]{2,1,0:T(8,128)(2,1)S(1)} %get-tuple-element.37.q_ref.refs_2_, bf16[4,512,128]{2,1,0:T(8,128)(2,1)S(1)} %collective-permute-done.2.refs_4_.refs_3_, ...), custom_call_target="tpu_custom_call" | custom-call | flops 167772160 | bytes 262144 | tf_op jit(solution)/shard_map/attend/pallas_call | solution.py:251
  84.4 2.8 %collective-permute-done.9.other_ref = bf16[528,512]{1,0:T(8,128)(2,1)S(1)} collective-permute-done((bf16[528,512]{1,0:T(8,128)(2,1)S(1)}, bf16[528,512]{1,0:T(8,128)(2,1)S(1)}, u32[]{:S(2)}, u32[]{:S(2)}) %collective-permute-start.9) | collective-permute-done | bytes 540704 | tf_op jit(solution)/shard_map/ppermute | solution.py:398
  87.2 0.3 combine.1
  87.5 15.0 %all_to_all.11.back_ref = bf16[16,64,256]{2,1,0:T(8,128)(2,1)S(1)} all-to-all(bf16[16,64,256]{2,1,0:T(8,128)(2,1)S(1)} %bitcast.6), channel_id=1, replica_groups=mesh['yh'=2,'z'=8,'c'=2,'yl'=2,'x'=4] {'c','yl','x'}, dimensions={0} | all-to-all | bytes 1048576 | tf_op jit(solution)/shard_map/all_to_all | solution.py:401
  102.6 0.8 unpack.1
  (2 shorter events, 0.0 us)
Async XLA Ops:
  25.3 8.7 %copy-start = (s32[64]{0:T(128)S(1)}, s32[64]{0:T(128)}, u32[]{:S(2)}) copy-start(s32[64]{0:T(128)} %refs_1_.9) | copy-start | bytes 772
  25.6 12.8 %collective-permute-start = (bf16[4,512,128]{2,1,0:T(8,128)(2,1)S(1)}, bf16[4,512,128]{2,1,0:T(8,128)(2,1)S(1)}, u32[]{:S(2)}, u32[]{:S(2)}) collective-permute-start(bf16[4,512,128]{2,1,0:T(8,128)(2,1)S(1)} %get-tuple-element.33.kv_ref.refs_4_), channel_id=1, source_target_pairs={{0,16},{8,120},{16,32},{24,8},{32,48},{40,24},{48,64},{56,40},{64,... | collective-permute-start | bytes 1572872 | tf_op jit(solution)/shard_map/ppermute | solution.py:371
  31.2 7.1 %collective-permute-start.1 = (bf16[2,128,512]{2,1,0:T(8,128)(2,1)S(1)}, bf16[2,128,512]{2,1,0:T(8,128)(2,1)S(1)}, u32[]{:S(2)}, u32[]{:S(2)}) collective-permute-start(bf16[2,128,512]{2,1,0:T(8,128)(2,1)S(1)} %slice.6), channel_id=1, source_target_pairs={{0,128},{128,0},{1,129},{129,1},{2,130},{130,2},{3,131},{131,3},{4... | collective-permute-start | bytes 786440 | tf_op jit(solution)/shard_map/ppermute | solution.py:377
  38.4 6.6 %collective-permute-start.4 = (bf16[4,512,128]{2,1,0:T(8,128)(2,1)S(1)}, bf16[4,512,128]{2,1,0:T(8,128)(2,1)S(1)}, u32[]{:S(2)}, u32[]{:S(2)}) collective-permute-start(bf16[4,512,128]{2,1,0:T(8,128)(2,1)S(1)} %collective-permute-done.refs_3_.refs_5_), channel_id=1, source_target_pairs={{0,8},{8,0},{1,9},{9,1},{2,10},{10,2},{3,11},{11,3},{4,12},{12,4},... | collective-permute-start | bytes 1572872 | tf_op jit(solution)/shard_map/ppermute | solution.py:374
  38.9 11.0 %collective-permute-start.2 = (bf16[4,512,128]{2,1,0:T(8,128)(2,1)S(1)}, bf16[4,512,128]{2,1,0:T(8,128)(2,1)S(1)}, u32[]{:S(2)}, u32[]{:S(2)}) collective-permute-start(bf16[4,512,128]{2,1,0:T(8,128)(2,1)S(1)} %collective-permute-done.refs_3_.refs_5_), channel_id=1, source_target_pairs={{0,16},{8,120},{16,32},{24,8},{32,48},{40,24},{48,64},{56,40},{64,... | collective-permute-start | bytes 1572872 | tf_op jit(solution)/shard_map/ppermute | solution.py:371
  42.2 7.6 %collective-permute-start.3 = (bf16[2,128,512]{2,1,0:T(8,128)(2,1)S(1)}, bf16[2,128,512]{2,1,0:T(8,128)(2,1)S(1)}, u32[]{:S(2)}, u32[]{:S(2)}) collective-permute-start(bf16[2,128,512]{2,1,0:T(8,128)(2,1)S(1)} %slice.7), channel_id=1, source_target_pairs={{0,128},{128,0},{1,129},{129,1},{2,130},{130,2},{3,131},{131,3},{4... | collective-permute-start | bytes 786440 | tf_op jit(solution)/shard_map/ppermute | solution.py:382
  49.9 9.0 %collective-permute-start.6 = (bf16[4,512,128]{2,1,0:T(8,128)(2,1)S(1)}, bf16[4,512,128]{2,1,0:T(8,128)(2,1)S(1)}, u32[]{:S(2)}, u32[]{:S(2)}) collective-permute-start(bf16[4,512,128]{2,1,0:T(8,128)(2,1)S(1)} %collective-permute-done.2.refs_4_.refs_3_), channel_id=1, source_target_pairs={{0,16},{8,120},{16,32},{24,8},{32,48},{40,24},{48,64},{56,40},{64,... | collective-permute-start | bytes 1572872 | tf_op jit(solution)/shard_map/ppermute | solution.py:371
  52.5 9.6 %collective-permute-start.5 = (bf16[4,512,128]{2,1,0:T(8,128)(2,1)S(1)}, bf16[4,512,128]{2,1,0:T(8,128)(2,1)S(1)}, u32[]{:S(2)}, u32[]{:S(2)}) collective-permute-start(bf16[4,512,128]{2,1,0:T(8,128)(2,1)S(1)} %collective-permute-done.2.refs_4_.refs_3_), channel_id=1, source_target_pairs={{0,8},{8,0},{1,9},{9,1},{2,10},{10,2},{3,11},{11,3},{4,12},{12,4},... | collective-permute-start | bytes 1572872 | tf_op jit(solution)/shard_map/ppermute | solution.py:374
  58.9 3.2 %collective-permute-start.7 = (bf16[4,512,128]{2,1,0:T(8,128)(2,1)S(1)}, bf16[4,512,128]{2,1,0:T(8,128)(2,1)S(1)}, u32[]{:S(2)}, u32[]{:S(2)}) collective-permute-start(bf16[4,512,128]{2,1,0:T(8,128)(2,1)S(1)} %collective-permute-done.6.refs_6_.refs_5_), channel_id=1, source_target_pairs={{0,8},{8,0},{1,9},{9,1},{2,10},{10,2},{3,11},{11,3},{4,12},{12,4},... | collective-permute-start | bytes 1572872 | tf_op jit(solution)/shard_map/ppermute | solution.py:374
  60.3 8.3 %collective-permute-start.8 = (bf16[4,512,128]{2,1,0:T(8,128)(2,1)S(1)}, bf16[4,512,128]{2,1,0:T(8,128)(2,1)S(1)}, u32[]{:S(2)}, u32[]{:S(2)}) collective-permute-start(bf16[4,512,128]{2,1,0:T(8,128)(2,1)S(1)} %collective-permute-done.6.refs_6_.refs_5_), channel_id=1, source_target_pairs={{0,16},{8,120},{16,32},{24,8},{32,48},{40,24},{48,64},{56,40},{64,... | collective-permute-start | bytes 1572872 | tf_op jit(solution)/shard_map/ppermute | solution.py:371
  71.8 15.4 %collective-permute-start.9 = (bf16[528,512]{1,0:T(8,128)(2,1)S(1)}, bf16[528,512]{1,0:T(8,128)(2,1)S(1)}, u32[]{:S(2)}, u32[]{:S(2)}) collective-permute-start(bf16[528,512]{1,0:T(8,128)(2,1)S(1)} %attend.9), channel_id=1, source_target_pairs={{0,128},{128,0},{1,129},{129,1},{2,130},{130,2},{3,131},{131,3},{4... | collective-permute-start | bytes 1622024 | tf_op jit(solution)/shard_map/ppermute | solution.py:398
